TPU v7x, 512 devices: a whole 4x8x8 slice. The times are simulated.
512 devices in a mesh: seq: 64 (over y, x, core), mp: 8 (over z).
Axes of the slice: x: 4, y: 8, z: 8, core: 2. Of those that a mesh axis runs over, the one named last changes fastest.
Arguments:
- tokens: bfloat16 [32768, 4096], P('seq', 'mp'), may hold values from -6 to 6
- x_gain: bfloat16 [4096], P('mp'), may hold values from 0.099609375 to 1.8984375
- w_router: bfloat16 [4096], P('mp'), may hold values from -0.09375 to 0.09375
- w_query: bfloat16 [4096, 4096], P('seq', 'mp'), may hold values from -0.09375 to 0.09375
- key_weight: bfloat16 [4096, 1024], P('seq', 'mp'), may hold values from -0.09375 to 0.09375
- value_weight: bfloat16 [4096, 1024], P('seq', 'mp'), may hold values from -0.09375 to 0.09375
- q_gain: float32 [128], replicated, may hold values from 1 to 3
- key_norm_gain: float32 [128], replicated, may hold values from 0.1 to 1.9
- route_pos: int32 [12288], P('seq'), may hold values from 0 to 511, as said below
- route_count: int32 [64], P('seq'), may hold values from 1 to 192, 4096 in all
Outputs:
- attended: bfloat16 [32768, 4096], P('seq', 'mp')
Inputs may be any that keep to these rules, and one draw needn't show every extreme that they name: The counts of all devices sum to exactly 4096; device s routes the positions in the first route_count[s] of its 192 slots of route_pos. `route_pos`: within one device's 192 slots the positions are distinct; they index positions of that device's block of 512.
All inputs are finite; a program needn't handle non-finite values.
Results may differ from a plain program's by a relative error of at most 0.011.
Values may be sent and summed in bfloat16 or wider, within the bound.
No kernel may reach another device: no remote copies, remote signals or barrier semaphores. Data moves between devices by JAX's collectives and lax.ppermute only.
A program may use at most 128 MiB of HBM per device.

v0:
```python
import math

import jax
import jax.numpy as jnp
from jax import lax
from jax.sharding import PartitionSpec as P


def per_head_norm(projected, gain):
    mean_sq = jnp.mean(projected * projected, axis=-1, keepdims=True)
    return (projected * lax.rsqrt(mean_sq + 1e-06) * gain).astype(jnp.bfloat16)


def project_rows(
    local_rows, x_gain, w_router, w_query, key_weight, value_weight, q_gain, key_norm_gain
):
    full_rows, gain_full, router_full = (
        lax.all_gather(local_rows, "mp", axis=1, tiled=True),
        lax.all_gather(x_gain, "mp", axis=0, tiled=True),
        lax.all_gather(w_router, "mp", axis=0, tiled=True),
    )
    count_of_rows = full_rows.shape[0]
    head_size = q_gain.shape[0]
    widened = full_rows.astype(jnp.float32)
    mean_sq = jnp.mean(widened * widened, axis=-1, keepdims=True)
    normalized_rows = (widened * lax.rsqrt(mean_sq + 1e-05) * gain_full.astype(jnp.float32)).astype(
        jnp.bfloat16
    )
    router_gate = jax.nn.sigmoid(
        jnp.dot(normalized_rows, router_full, preferred_element_type=jnp.float32)
    )
    pieces = (
        lax.all_gather(w_query, "seq", axis=0, tiled=True),
        lax.all_gather(key_weight, "seq", axis=0, tiled=True),
        lax.all_gather(value_weight, "seq", axis=0, tiled=True),
    )
    query_sum, key_sum, value_sum = tuple(
        (jnp.dot(normalized_rows, piece, preferred_element_type=jnp.float32) for piece in pieces)
    )
    query_matrix = per_head_norm(query_sum.reshape(count_of_rows, -1, head_size), q_gain)
    key_matrix = per_head_norm(key_sum.reshape(count_of_rows, -1, head_size), key_norm_gain)
    value_matrix = value_sum.astype(jnp.bfloat16).reshape(count_of_rows, -1, head_size)
    return (router_gate, query_matrix, key_matrix, value_matrix)


def attend(query_matrix, key_matrix, value_matrix, positions):
    count_of_rows, kv_heads, head_size = key_matrix.shape
    group_size = query_matrix.shape[1] // kv_heads
    grouped_heads = query_matrix.reshape(count_of_rows, kv_heads, group_size, head_size)
    logit_scale = 1.0 / math.sqrt(head_size)
    key_portion = lax.all_gather(key_matrix, "seq", axis=0, tiled=True)
    value_part = lax.all_gather(value_matrix, "seq", axis=0, tiled=True)
    key_pos = lax.all_gather(positions, "seq", axis=0, tiled=True)
    attention_logits = (
        jnp.einsum("iqef,oqf->iqeo", grouped_heads, key_portion, preferred_element_type=jnp.float32)
        * logit_scale
    )
    allowed = (key_pos[None, :] >= 0) & (key_pos[None, :] <= positions[:, None])
    weights = jnp.where(allowed[:, None, None, :], jnp.exp(attention_logits), 0.0)
    softmax_divisor = jnp.sum(weights, axis=-1)
    softmax_dividend = jnp.einsum(
        "vtme,eti->vtmi",
        weights.astype(jnp.bfloat16),
        value_part,
        preferred_element_type=jnp.float32,
    )
    return (softmax_dividend, softmax_divisor)


def finish(router_gate, softmax_dividend, softmax_divisor, is_live):
    safe_total = jnp.where(is_live[:, None, None], softmax_divisor, 1.0)
    result = router_gate[:, None, None, None] * softmax_dividend / safe_total[..., None]
    return result.reshape(softmax_dividend.shape[0], -1).astype(jnp.bfloat16)


def local(
    tokens,
    x_gain,
    w_router,
    w_query,
    key_weight,
    value_weight,
    q_gain,
    key_norm_gain,
    route_pos,
    route_count,
):
    block_rows = tokens.shape[0]
    slot_total = route_pos.shape[0]
    my_shard = lax.axis_index("seq")
    slot_index = jnp.arange(slot_total, dtype=jnp.int32)
    is_live = slot_index < route_count[0]
    positions = jnp.where(is_live, my_shard * block_rows + route_pos, -1)
    local_rows = jnp.take(tokens, route_pos, axis=0)
    router_gate, query_matrix, key_matrix, value_matrix = project_rows(
        local_rows, x_gain, w_router, w_query, key_weight, value_weight, q_gain, key_norm_gain
    )
    softmax_dividend, softmax_divisor = attend(query_matrix, key_matrix, value_matrix, positions)
    result = finish(router_gate, softmax_dividend, softmax_divisor, is_live)
    target = jnp.where(is_live, route_pos, block_rows)
    return (
        jnp.zeros((block_rows, result.shape[1]), jnp.bfloat16).at[target].set(result, mode="drop")
    )


def solution(mesh):
    return jax.shard_map(
        local,
        mesh=mesh,
        in_specs=(
            P("seq", "mp"),
            P("mp"),
            P("mp"),
            P("seq", "mp"),
            P("seq", "mp"),
            P("seq", "mp"),
            P(),
            P(),
            P("seq"),
            P("seq"),
        ),
        out_specs=P("seq", "mp"),
        check_vma=False,
    )
```

profile of v0, /device:TPU:57, one launch (start us, length us, event | category | flops | bytes accessed | tf_op | source)
XLA Modules:
  0.0 520.4 jit_solution(8698326952407650645)
XLA Ops:
  7.2 0.7 compare_and_fusion.1
  7.9 1.3 dynamic-slice
  9.9 0.8 fusion.55
  10.7 1.0 gather_fusion
  11.7 0.8 broadcast_select_fusion
  12.6 0.7 all-gather.15.cloned.1.call-update
  14.6 0.7 reshape.172
  15.3 22.3 %all-gather.2 = bf16[8,1,512]{2,1,0:T(2,128)(2,1)S(1)} all-gather(bf16[1,1,512]{2,1,0:T(2,128)(2,1)S(1)} %reshape.172), channel_id=1, replica_groups=mesh['seq'=64,'mp'=8] {'mp'}, dimensions={0}, use_global_device_ids=true | all-gather | bytes 9216 | tf_op jit(solution)/shard_map/all_gather | solution.py:19
  37.6 18.7 %all-gather.11.cloned.1.call-done = bf16[192,4096]{1,0:T(8,128)(2,1)} async-done(((bf16[192,512]{1,0:T(8,128)(2,1)}), bf16[192,4096]{1,0:T(8,128)(2,1)}) %all-gather.11.cloned.1.call-update) | async-done | bytes 1572880 | tf_op jit(solution)/shard_map/all_gather | solution.py:18
  56.3 1.9 fusion.6
  58.2 84.3 %all-gather.15.cloned.1.call-done = bf16[4096,128]{1,0:T(8,128)(2,1)} async-done(((bf16[64,128]{1,0:T(8,128)(2,1)}), bf16[4096,128]{1,0:T(8,128)(2,1)}) %all-gather.15.cloned.1.call-update) | async-done | bytes 1048592 | tf_op jit(solution)/shard_map/all_gather | solution.py:34
  142.6 2.5 multiply_reduce_fusion
  145.1 0.7 multiply_convert_fusion
  145.9 18.5 %all-gather.3 = bf16[8,1,512]{2,1,0:T(2,128)(2,1)S(1)} all-gather(bf16[1,1,512]{2,1,0:T(2,128)(2,1)S(1)} %reshape.174), channel_id=1, replica_groups=mesh['seq'=64,'mp'=8] {'mp'}, dimensions={0}, use_global_device_ids=true | all-gather | bytes 9216 | tf_op jit(solution)/shard_map/all_gather | solution.py:20
  164.4 236.2 %all-reduce = s32[12288]{0:T(1024)S(1)} all-reduce(s32[12288]{0:T(1024)S(1)} %get-tuple-element.5), channel_id=1, replica_groups=mesh['seq'=64,'mp'=8] {'seq'}, use_global_device_ids=true, to_apply=%add | all-reduce | flops 12288 | bytes 98304
  400.7 2.5 convolution_convert_fusion
  403.2 1.6 compare_and_fusion
  404.8 2.0 fusion.53
  406.9 4.6 fusion.56
  411.4 1.1 mul.108
  413.2 18.4 %fusion = (f32[192,4]{0,1:T(4,128)S(1)}, f32[12288,192,4]{0,1,2:T(8,128)}) fusion(pred[192,12288]{1,0:T(8,128)(4,1)S(1)} %compare_and_fusion, bf16[12288,128]{1,0:T(8,128)(2,1)} %all-gather.21.cloned.1.call-done, f32[192,512]{1,0:T(8,128)} %get-tuple-element.12, f32[24,8,4,128]{3,2,1,0:T(4,128)S(1)} %bitcast.104, f32[512]{0:T(512)S(1)} %broadcast_bitcast_fusion), kind=kOutput, calls=%fused_computation.3 | convolution fusion | flops 2444524800 | bytes 44045312 | tf_op jit(solution)/shard_map/iqef,oqf->iqeo/dot_general | solution.py:55
  431.6 64.8 %all-gather.19.cloned.1.call-done = bf16[12288,128]{1,0:T(8,128)(2,1)} async-done(((bf16[192,128]{1,0:T(8,128)(2,1)}), bf16[12288,128]{1,0:T(8,128)(2,1)}) %all-gather.19.cloned.1.call-update) | async-done | bytes 3145744 | tf_op jit(solution)/shard_map/all_gather | solution.py:52
  496.4 14.9 %fusion.32 = bf16[192,1,4,128]{3,0,2,1:T(8,128)(2,1)S(1)} fusion(f32[12288,192,4]{0,1,2:T(8,128)} %get-tuple-element.14, pred[192,12288]{1,0:T(8,128)(4,1)S(1)} %compare_and_fusion, bf16[12288,128]{1,0:T(8,128)(2,1)} %all-gather.19.cloned.1.call-done, f32[192,4]{0,1:T(4,128)S(1)} %broadcast_select_fusion.1, f32[192]{0:T(256)S(1)} %add_divide_fusion), kind=kOutput, calls=%fused_computation.22 | convolution fusion | flops 2444525568 | bytes 43454208 | tf_op jit(solution)/shard_map/vtme,eti->vtmi/dot_general | solution.py:61
  511.5 2.1 scatter_custom_fusion
  (39 shorter events, 2.3 us)
Async XLA Ops:
  6.5 4.1 copy-start
  6.5 49.8 %all-gather.11.cloned.1.call-start = ((), (), s32[]{:S(2)}) async-start(), calls=%async_computation | async-start | bytes 1769472 | tf_op jit(solution)/shard_map/all_gather | solution.py:18
  11.7 133.4 %copy-start.3 = (f32[128]{0:T(128)S(1)}, f32[128]{0:T(128)}, u32[]{:S(2)}) copy-start(f32[128]{0:T(128)} %param.17) | copy-start | bytes 1540
  11.7 134.2 %copy-start.2 = (bf16[512]{0:T(512)(128)(2,1)S(1)}, bf16[512]{0:T(512)(128)(2,1)}, u32[]{:S(2)}) copy-start(bf16[512]{0:T(512)(128)(2,1)} %param.12) | copy-start | bytes 3076
  12.5 388.1 %copy-start.4 = (f32[128]{0:T(128)S(1)}, f32[128]{0:T(128)}, u32[]{:S(2)}) copy-start(f32[128]{0:T(128)} %param.16) | copy-start | bytes 1540
  12.5 130.1 %all-gather.15.cloned.1.call-start = ((), (), s32[]{:S(2)}) async-start(), calls=%async_computation.2 | async-start | bytes 1064960 | tf_op jit(solution)/shard_map/all_gather | solution.py:34
  13.3 387.4 %all-gather.13.cloned.1.call-start = ((), (), s32[]{:S(2)}) async-start(), calls=%async_computation.1 | async-start | bytes 1064960 | tf_op jit(solution)/shard_map/all_gather | solution.py:35
  14.0 392.8 %all-gather.17.cloned.1.call-start = ((), (), s32[]{:S(2)}) async-start(), calls=%async_computation.3 | async-start | bytes 4259840 | tf_op jit(solution)/shard_map/all_gather | solution.py:33
  14.6 398.3 %all-gather.21.cloned.1.call-start = ((), (), s32[]{:S(2)}) async-start(), calls=%async_computation.5 | async-start | bytes 3194880 | tf_op jit(solution)/shard_map/all_gather | solution.py:51
  56.3 344.4 %copy-start.1 = (bf16[192,4096]{1,0:T(8,128)(2,1)S(1)}, bf16[192,4096]{1,0:T(8,128)(2,1)}, u32[]{:S(2)}) copy-start(bf16[192,4096]{1,0:T(8,128)(2,1)} %all-gather.11.cloned.1.call-done) | copy-start | bytes 4718596
  145.8 350.6 %all-gather.19.cloned.1.call-start = ((), (), s32[]{:S(2)}) async-start(), calls=%async_computation.4 | async-start | bytes 3194880 | tf_op jit(solution)/shard_map/all_gather | solution.py:52
Sparse Core Ops, SparseCore 0:
  12.6 43.6 all-gather.10
  59.7 82.8 all-gather.14
  145.9 79.5 all-gather.12
  228.8 82.1 all-gather.16
  314.2 81.1 all-gather.20
  403.3 93.0 all-gather.18
where the time goes:
time: 523 us; the launch traced here: 520 us
  blocking collectives  277 us (53%)
  waiting for transfers between devices  170 us (33%)
  matrix products  44.9 us (9%)
  between operations  15 us (3%)
  other arithmetic  6.88 us (1%)
  local copies, waits for them, and re-layouts  6.63 us (1%)
    unnamed x1, blocking collectives  236 us
    all_gather x1, waiting for transfers between devices, project_rows(): lax.all_gather(key_weight, 'seq', axis=0, tiled=True)  84.3 us
    all_gather x1, waiting for transfers between devices, attend(): value_part = lax.all_gather(value_matrix, 'seq', axis=0, tiled=True)  64.8 us
    all_gather x1, blocking collectives, project_rows(): lax.all_gather(x_gain, 'mp', axis=0, tiled=True)  22.3 us
    all_gather x1, waiting for transfers between devices, project_rows(): lax.all_gather(local_rows, 'mp', axis=1, tiled=True)  18.7 us
    all_gather x1, blocking collectives, project_rows(): lax.all_gather(w_router, 'mp', axis=0, tiled=True)  18.5 us
    dot_general x1, matrix products, attend(): jnp.einsum('iqef,oqf->iqeo', grouped_heads, key_portion, preferred_elemen...  18.4 us
    dot_general x1, matrix products, attend(): jnp.einsum('vtme,eti->vtmi', weights.astype(jnp.bfloat16), value_part, pr...  14.9 us
  transfers between devices with their start and end apart: 6, of which 3 were waited for; matrix products, arithmetic and copies ran while one was open for 7% of the time, Pallas kernels for 0%

commit v1 on v0

v1 whole, which is shorter than its diff:
```python
import math

import jax
import jax.numpy as jnp
from jax import lax
from jax.experimental import pallas as pl
from jax.experimental.pallas import tpu as pltpu
from jax.sharding import Mesh
from jax.sharding import PartitionSpec as P

PLANE = ("y", "x")
SEQ = ("y", "x", "core")
TILE = 512
VMEM_BYTES = 56 * 1024 * 1024


def whole(memory_space=pltpu.VMEM):
    return pl.BlockSpec(memory_space=memory_space)


def params():
    return pltpu.CompilerParams(vmem_limit_bytes=VMEM_BYTES)


def dot(a, b, contract_a=1, contract_b=0):
    return lax.dot_general(
        a, b, (((contract_a,), (contract_b,)), ((), ())), preferred_element_type=jnp.float32
    )


def pick_rows_kernel(tokens_ref, pos_ref, gain_ref, router_ref, out_ref):
    slots = pos_ref.shape[1]
    rows, width = tokens_ref.shape
    hit = lax.broadcasted_iota(jnp.int32, (rows, slots), 0) == pos_ref[...]
    one_hot = jnp.where(hit, 1.0, 0.0).astype(jnp.bfloat16)
    out_ref[:slots, :] = dot(one_hot, tokens_ref[...], 0, 0).astype(jnp.bfloat16)
    at = lax.broadcasted_iota(jnp.int32, (out_ref.shape[0] - slots, width), 0)
    extra = jnp.where(at == 0, gain_ref[...].astype(jnp.float32), 0.0)
    extra = jnp.where(at == 1, router_ref[...].astype(jnp.float32), extra)
    out_ref[slots:, :] = extra.astype(jnp.bfloat16)


def pick_rows(tokens, route_pos, x_gain, w_router):
    slots = route_pos.shape[0]
    width = tokens.shape[1]
    return pl.pallas_call(
        pick_rows_kernel,
        out_shape=jax.ShapeDtypeStruct((slots + 16, width), jnp.bfloat16),
        in_specs=[whole()] * 4,
        out_specs=whole(),
        compiler_params=params(),
        name="pick_rows",
    )(tokens, route_pos.reshape(1, slots), x_gain.reshape(1, width), w_router.reshape(1, width))


def head_norm(projected, gain):
    mean_sq = jnp.mean(projected * projected, axis=-1, keepdims=True)
    return (projected * lax.rsqrt(mean_sq + 1e-06) * gain).astype(jnp.bfloat16)


def in_feature_order(core, mine, other):
    even = jnp.where(core == 0, mine, other)
    odd = jnp.where(core == 0, other, mine)
    return jnp.stack([even, odd], axis=1).reshape(-1, mine.shape[-1])


def keys_kernel(place_ref, count_ref, rows_ref, mine_ref, other_ref, gain_ref, xn_ref, kv_ref, gate_ref):
    parts, padded, width = rows_ref.shape
    slots, head = kv_ref.shape[0], gain_ref.shape[1]
    core, count = place_ref[0], count_ref[0]
    square = jnp.zeros((slots, width), jnp.float32)
    for part in range(parts):
        wide = rows_ref[part, :slots, :].astype(jnp.float32)
        square += wide * wide
    mean_sq = jnp.sum(square, axis=-1, keepdims=True) / (parts * width)
    scale = lax.rsqrt(mean_sq + 1e-05)
    total = jnp.zeros((slots, 2 * head), jnp.float32)
    routed = jnp.zeros((slots, width), jnp.float32)
    step = mine_ref.shape[0] // parts
    for part in range(parts):
        extra = rows_ref[part, slots:, :].astype(jnp.float32)
        wide = rows_ref[part, :slots, :].astype(jnp.float32)
        normed = (wide * scale * extra[0:1]).astype(jnp.bfloat16)
        xn_ref[:, part * width : (part + 1) * width] = normed
        routed += normed.astype(jnp.float32) * extra[1:2]
        own = slice(part * step, (part + 1) * step)
        weights = in_feature_order(core, mine_ref[own, :64, :], other_ref[own, :64, :])
        total += dot(normed, weights)
    gate = jax.nn.sigmoid(jnp.sum(routed, axis=-1, keepdims=True))
    gate_ref[...] = jnp.broadcast_to(gate, gate_ref.shape)
    kv_ref[:, :head] = head_norm(total[:, :head], gain_ref[...])
    live = lax.broadcasted_iota(jnp.int32, (slots, head), 0) < count
    kv_ref[:, head:] = jnp.where(live, total[:, head:], 0.0).astype(jnp.bfloat16)


def make_keys(core, count, rows, mine, other, gain, slots):
    parts, _, width = rows.shape
    head = gain.shape[0]
    return pl.pallas_call(
        keys_kernel,
        out_shape=(
            jax.ShapeDtypeStruct((slots, parts * width), jnp.bfloat16),
            jax.ShapeDtypeStruct((slots, 2 * head), jnp.bfloat16),
            jax.ShapeDtypeStruct((slots, head), jnp.float32),
        ),
        in_specs=[whole(pltpu.SMEM)] * 2 + [whole()] * 4,
        out_specs=(whole(),) * 3,
        compiler_params=params(),
        name="make_keys",
    )(core, count, rows, mine, other, gain.reshape(1, head))


def queries_kernel(xn_ref, weights_ref, gain_ref, out_ref):
    blocks, _, width = weights_ref.shape
    slots, head = out_ref.shape[0], gain_ref.shape[1]
    total = jnp.zeros((slots, width), jnp.float32)
    step = 8
    for at in range(0, blocks, step):
        weights = weights_ref[at : at + step, :64, :].reshape(step * 64, width)
        total += dot(xn_ref[:, at * 64 : (at + step) * 64], weights)
    for at in range(0, width, head):
        out_ref[:, at : at + head] = head_norm(total[:, at : at + head], gain_ref[...])


def make_queries(xn, weights, gain):
    return pl.pallas_call(
        queries_kernel,
        out_shape=jax.ShapeDtypeStruct((xn.shape[0], weights.shape[2]), jnp.bfloat16),
        in_specs=[whole()] * 3,
        out_specs=whole(),
        compiler_params=params(),
        name="make_queries",
    )(xn, weights, gain.reshape(1, -1))


def attend_kernel(
    lengths_ref, count_ref, q_ref, own_ref, mine_ref, other_ref, pos_row_ref, pos_col_ref, gate_ref,
    out_ref, packed, total,
):
    slots, head = gate_ref.shape
    group = q_ref.shape[1] // head
    count = count_ref[0]
    factor = math.log2(math.e) / math.sqrt(head)
    fill = lax.broadcasted_iota(jnp.int32, (slots, head), 0)

    def pack(at, offset):
        for which, ref in enumerate((mine_ref, other_ref)):
            length = lengths_ref[which, at]

            @pl.when(length > 0)
            def _():
                where = pl.ds(pl.multiple_of(offset, 16), slots)
                packed[where, : 2 * head] = ref[at, :slots, :]
                packed[where, 2 * head :] = jnp.where(fill < length, 1.0, 0.0).astype(jnp.bfloat16)

            offset = offset + (length + 15) // 16 * 16
        return offset

    end = lax.fori_loop(0, mine_ref.shape[0], pack, jnp.int32(0))
    packed[pl.ds(pl.multiple_of(end, 16), TILE), :] = jnp.zeros((TILE, packed.shape[1]), jnp.bfloat16)

    allowed = (pos_row_ref[...] <= pos_col_ref[...]) & (
        lax.broadcasted_iota(jnp.int32, (slots, slots), 1) < count
    )
    summed = jnp.concatenate([own_ref[:, head:], jnp.ones((slots, head), jnp.bfloat16)], axis=1)
    for h in range(group):
        query = q_ref[:, h * head : (h + 1) * head]
        weights = jnp.exp2(dot(query, own_ref[:, :head], 1, 1) * factor)
        weights = jnp.where(allowed, weights, 0.0).astype(jnp.bfloat16)
        total[h] = dot(weights, summed)

    def tile(at, carry):
        rows = pl.ds(pl.multiple_of(at * TILE, TILE), TILE)
        keys, values = packed[rows, :head], packed[rows, head:]
        for h in range(group):
            query = q_ref[:, h * head : (h + 1) * head]
            weights = jnp.exp2(dot(query, keys, 1, 1) * factor).astype(jnp.bfloat16)
            total[h] += dot(weights, values)
        return carry

    lax.fori_loop(0, (end + TILE - 1) // TILE, tile, 0)

    block = out_ref.shape[0]
    live = fill < count
    pieces = []
    for h in range(group):
        sums = total[h]
        piece = gate_ref[...] * sums[:, :head] / jnp.where(live, sums[:, head:], 1.0)
        pieces.append(jnp.where(live, piece, 0.0).astype(jnp.bfloat16))
    hit = (lax.broadcasted_iota(jnp.int32, (block, slots), 0) == pos_row_ref[...]) & (
        lax.broadcasted_iota(jnp.int32, (block, slots), 1) < count
    )
    one_hot = jnp.where(hit, 1.0, 0.0).astype(jnp.bfloat16)
    out_ref[...] = dot(one_hot, jnp.concatenate(pieces, axis=1)).astype(jnp.bfloat16)


def attend(lengths, count, queries, own, mine, other, route_pos, gate, block):
    slots, width = queries.shape
    head = gate.shape[1]
    sources = 2 * mine.shape[0]
    most = sources * block // 8 + 16 * sources + slots + TILE
    return pl.pallas_call(
        attend_kernel,
        out_shape=jax.ShapeDtypeStruct((block, width), jnp.bfloat16),
        in_specs=[whole(pltpu.SMEM)] * 2 + [whole()] * 7,
        out_specs=whole(),
        scratch_shapes=[
            pltpu.VMEM(((most + TILE - 1) // TILE * TILE, 3 * head), jnp.bfloat16),
            pltpu.VMEM((width // head, slots, 2 * head), jnp.float32),
        ],
        compiler_params=params(),
        name="attend",
    )(lengths, count, queries, own, mine, other, route_pos.reshape(1, slots), route_pos.reshape(slots, 1), gate)


def to_all(block, axes, peers):
    return lax.all_to_all(
        jnp.broadcast_to(block[None], (peers,) + block.shape), axes, 0, 0, tiled=True
    )


def swap_cores(block):
    return lax.ppermute(block, "core", [(0, 1), (1, 0)])


def local(
    tokens, x_gain, w_router, w_query, key_weight, value_weight, q_gain, key_norm_gain, route_pos, route_count
):
    ny, nx, nz = lax.axis_size("y"), lax.axis_size("x"), lax.axis_size("z")
    block = tokens.shape[0]
    slots = route_pos.shape[0]
    core = lax.axis_index("core").astype(jnp.int32)
    shard = lax.axis_index(SEQ).astype(jnp.int32)

    picked = pick_rows(tokens, route_pos, x_gain, w_router)
    rows = lax.all_gather(picked, "z", axis=0, tiled=False)

    key_value = jnp.concatenate([key_weight, value_weight], axis=1)
    kv_mine = to_all(key_value, PLANE, ny * nx)
    kv_other = swap_cores(kv_mine)

    counted = jnp.broadcast_to(route_count.astype(jnp.bfloat16)[:, None], (16, w_query.shape[1]))
    wq = lax.all_gather(jnp.concatenate([w_query, counted], axis=0), SEQ, axis=0, tiled=False)

    normed, kv, gate = make_keys(core[None], route_count, rows, kv_mine, kv_other, key_norm_gain, slots)

    kv_y = lax.all_gather(kv, "y", axis=0, tiled=False)
    kv_yx = to_all(kv_y, "x", nx).reshape(nx * ny, slots, kv.shape[1])
    kv_xy_other = swap_cores(kv_yx)

    queries = make_queries(normed, wq, q_gain)
    counts = wq[:, w_query.shape[0], 0].astype(jnp.int32)
    counts = jnp.where(jnp.arange(counts.shape[0], dtype=jnp.int32) < shard, counts, 0)
    per_core = counts.reshape(ny, nx, 2).transpose(2, 1, 0).reshape(2, nx * ny)
    lengths = jnp.where(core == 0, per_core, per_core[::-1])
    return attend(lengths, route_count, queries, kv, kv_yx, kv_xy_other, route_pos, gate, block)


def solution(mesh):
    grid = Mesh(mesh.devices.reshape(8, 4, 2, 8), ("y", "x", "core", "z"))
    return jax.shard_map(
        local,
        mesh=grid,
        in_specs=(
            P(SEQ, "z"), P("z"), P("z"), P(SEQ, "z"), P(SEQ, "z"), P(SEQ, "z"), P(), P(), P(SEQ), P(SEQ),
        ),
        out_specs=P(SEQ, "z"),
        check_vma=False,
    )
```

time: 523 us -> 175 us (0.33)
  blocking collectives: 277 us -> 83.4 us
  waiting for transfers between devices: 170 us -> 16.8 us
  matrix products: 44.9 us -> 0 us
  starting transfers between devices: 0.2 us -> 26 us
  Pallas kernels: 0 us -> 24.1 us
    unnamed x1 -> x0, blocking collectives: 236 us -> none
    all_gather x6 -> x2, waiting for transfers between devices: 168 us -> 16.8 us  [the longest x1 13.3 us: local(): lax.all_gather(jnp.concatenate([w_query, counted], axis=0), SEQ, axis=0,...]
    all_to_all x0 -> x2, blocking collectives: none -> 62.3 us  [to_all(): lax.all_to_all(jnp.broadcast_to(block[None], (peers,) + block.shape), axe...]
    dot_general x6 -> x0, matrix products: 44.9 us -> none  [the longest x1 18.4 us: attend(): jnp.einsum('iqef,oqf->iqeo', grouped_heads, key_portion, preferred_elemen...]
    ppermute x0 -> x2, starting transfers between devices: none -> 25.9 us  [swap_cores(): return lax.ppermute(block, 'core', [(0, 1), (1, 0)])]
    pallas_call x0 -> x4, Pallas kernels: none -> 24.1 us  [the longest x1 12.6 us: attend(): pl.pallas_call(attend_kernel, out_shape=jax.ShapeDtypeStruct((block, widt...]
    all_gather x2 -> x1, blocking collectives: 40.8 us -> 21.2 us  [local(): kv_y = lax.all_gather(kv, 'y', axis=0, tiled=False)]
  transfers between devices with their start and end apart: 6 -> 4, of which waited for: 3 -> 2; matrix products, arithmetic and copies ran while one was open for 7% -> 4% of each run, Pallas kernels for 0% -> 5%
where the time goes in v1:
time: 175 us
  blocking collectives  83.4 us (48%)
  starting transfers between devices  26 us (15%)
  Pallas kernels  24.1 us (14%)
  waiting for transfers between devices  16.8 us (10%)
  between operations  14.1 us (8%)
  local copies, waits for them, and re-layouts  6.64 us (4%)
  other arithmetic  3.46 us (2%)
    all_to_all x2, blocking collectives, to_all(): lax.all_to_all(jnp.broadcast_to(block[None], (peers,) + block.shape), axe...  62.3 us
    ppermute x2, starting transfers between devices, swap_cores(): return lax.ppermute(block, 'core', [(0, 1), (1, 0)])  25.9 us
    all_gather x1, blocking collectives, local(): kv_y = lax.all_gather(kv, 'y', axis=0, tiled=False)  21.2 us
    all_gather x1, waiting for transfers between devices, local(): lax.all_gather(jnp.concatenate([w_query, counted], axis=0), SEQ, axis=0,...  13.3 us
    pallas_call x1, Pallas kernels, attend(): pl.pallas_call(attend_kernel, out_shape=jax.ShapeDtypeStruct((block, widt...  12.6 us
    pallas_call x1, Pallas kernels, make_queries(): pl.pallas_call(queries_kernel, out_shape=jax.ShapeDtypeStruct((xn.shape[0...  4.82 us
    pallas_call x1, Pallas kernels, make_keys(): pl.pallas_call(keys_kernel, out_shape=(jax.ShapeDtypeStruct((slots, parts...  4.64 us
  transfers between devices with their start and end apart: 4, of which 2 were waited for; matrix products, arithmetic and copies ran while one was open for 4% of the time, Pallas kernels for 5%

profile of v1, /device:TPU:57, one launch (start us, length us, event | category | flops | bytes accessed | tf_op | source)
XLA Modules:
  0.0 174.5 jit_solution(15348943654179619725)
XLA Ops:
  6.5 1.3 reshape.35.gain_ref
  7.8 1.3 reshape.36.router_ref
  9.0 2.0 %pick_rows.1 = bf16[208,512]{1,0:T(8,128)(2,1)} custom-call(bf16[512,512]{1,0:T(8,128)(2,1)} %tokens_ref.1, s32[1,192]{1,0:T(1,128)} %bitcast.18, bf16[1,512]{1,0:T(2,128)(2,1)} %reshape.35.gain_ref, bf16[1,512]{1,0:T(2,128)(2,1)} %reshape.36.router_ref), custom_call_target="tpu_custom_call" | custom-call | tf_op jit(solution)/shard_map/pick_rows/pallas_call | solution.py:46
  11.8 1.5 concatenate.6
  13.3 0.7 pad_maximum_fusion
  14.1 0.1 broadcast_in_dim.28
  14.2 32.4 %all_to_all.10.mine_ref = bf16[32,64,256]{2,1,0:T(8,128)(2,1)S(1)} all-to-all(bf16[32,64,256]{2,1,0:T(8,128)(2,1)S(1)} %broadcast_in_dim.28), channel_id=1, replica_groups=mesh['y'=8,'x'=4,'core'=2,'z'=8] {'y','x'}, dimensions={0} | all-to-all | bytes 2097152 | tf_op jit(solution)/shard_map/all_to_all | solution.py:217
  46.5 5.2 %collective-permute-start = (bf16[32,64,256]{2,1,0:T(8,128)(2,1)S(1)}, bf16[32,64,256]{2,1,0:T(8,128)(2,1)S(1)}, u32[]{:S(2)}, u32[]{:S(2)}) collective-permute-start(bf16[32,64,256]{2,1,0:T(8,128)(2,1)S(1)} %all_to_all.10.mine_ref), channel_id=1, source_target_pairs={{0,8},{8,0},{1,9},{9,1},{2,10},{10,2},{3,11},{11,3},{4,12},{12,4},... | collective-permute-start | bytes 3145736 | tf_op jit(solution)/shard_map/ppermute | solution.py:223
  51.7 3.5 %all-gather.8.cloned.1.call-done = bf16[1664,512]{1,0:T(8,128)(2,1)} async-done(((bf16[208,512]{1,0:T(8,128)(2,1)}), bf16[1664,512]{1,0:T(8,128)(2,1)}) %all-gather.8.cloned.1.call-update) | async-done | bytes 1703952 | tf_op jit(solution)/shard_map/all_gather | solution.py:236
  55.2 1.0 copy-done.2
  56.2 4.6 %make_keys.1 = (bf16[192,4096]{1,0:T(8,128)(2,1)}, bf16[192,256]{1,0:T(8,128)(2,1)}, f32[192,128]{1,0:T(8,128)}) custom-call(s32[1]{0:T(128)} %bitcast.3.place_ref, s32[1]{0:T(128)S(6)} %copy.14.count_ref, bf16[8,208,512]{2,1,0:T(8,128)(2,1)} %bitcast.17, bf16[32,64,256]{2,1,0:T(8,128)(2,1)} %copy-done.1, bf16[32,64,256]{2,1,0:T(8,128)(2,1)} %copy-done.2, ...), custom_call_target="tpu_custom_call" | custom-call | tf_op jit(solution)/shard_map/make_keys/pallas_call | solution.py:99
  60.9 21.2 %all-gather.2 = bf16[1536,256]{1,0:T(8,128)(2,1)S(1)} all-gather(bf16[192,256]{1,0:T(8,128)(2,1)} %get-tuple-element.9.own_ref), channel_id=4, replica_groups=mesh['y'=8,'x'=4,'core'=2,'z'=8] {'y'}, dimensions={0}, use_global_device_ids=true | all-gather | bytes 884736 | tf_op jit(solution)/shard_map/all_gather | solution.py:247
  82.0 0.4 broadcast_in_dim.29
  82.4 29.9 %all_to_all.11 = bf16[4,8,192,256]{3,2,1,0:T(8,128)(2,1)S(1)} all-to-all(bf16[4,8,192,256]{3,2,1,0:T(8,128)(2,1)S(1)} %broadcast_in_dim.29), channel_id=1, replica_groups=mesh['y'=8,'x'=4,'core'=2,'z'=8] {'x'}, dimensions={0} | all-to-all | bytes 6291456 | tf_op jit(solution)/shard_map/all_to_all | solution.py:217
  112.3 20.8 %collective-permute-start.1 = (bf16[32,192,256]{2,1,0:T(8,128)(2,1)S(1)}, bf16[32,192,256]{2,1,0:T(8,128)(2,1)}, u32[]{:S(2)}, u32[]{:S(2)}) collective-permute-start(bf16[32,192,256]{2,1,0:T(8,128)(2,1)S(1)} %bitcast.12), channel_id=1, source_target_pairs={{0,8},{8,0},{1,9},{9,1},{2,10},{10,2},{3,11},{11,3},{4,12},{12,4},... | collective-permute-start | bytes 9437192 | tf_op jit(solution)/shard_map/ppermute | solution.py:223
  133.1 0.8 copy.13.pos_col_ref
  133.9 13.3 %all-gather.6.cloned.1.call-done = bf16[5120,512]{1,0:T(8,128)(2,1)} async-done(((bf16[80,512]{1,0:T(8,128)(2,1)}), bf16[5120,512]{1,0:T(8,128)(2,1)}) %all-gather.6.cloned.1.call-update) | async-done | bytes 5242896 | tf_op jit(solution)/shard_map/all_gather | solution.py:243
  147.2 2.1 %fusion = s32[64]{0:T(128)S(1)} fusion(bf16[64,80,512]{2,1,0:T(8,128)(2,1)} %bitcast.14), kind=kLoop, calls=%fused_computation.1 | loop fusion | flops 64 | bytes 384 | tf_op jit(solution)/shard_map/convert_element_type | solution.py:252
  149.3 0.1 reshape.41
  149.5 0.1 copy.12
  149.6 0.1 reshape.33
  149.7 4.8 %make_queries.1.q_ref = bf16[192,512]{1,0:T(8,128)(2,1)} custom-call(bf16[192,4096]{1,0:T(8,128)(2,1)} %get-tuple-element.8.xn_ref, bf16[64,80,512]{2,1,0:T(8,128)(2,1)} %bitcast.15, f32[1,128]{1,0:T(1,128)} %bitcast.22), custom_call_target="tpu_custom_call" | custom-call | tf_op jit(solution)/shard_map/make_queries/pallas_call | solution.py:126
  154.5 0.6 broadcast_select_fusion.lengths_ref
  155.1 12.6 %attend.1 = bf16[512,512]{1,0:T(8,128)(2,1)} custom-call(s32[2,32]{1,0:T(2,128)} %broadcast_select_fusion.lengths_ref, s32[1]{0:T(128)S(6)} %copy.14.count_ref, bf16[192,512]{1,0:T(8,128)(2,1)} %make_queries.1.q_ref, bf16[192,256]{1,0:T(8,128)(2,1)} %get-tuple-element.9.own_ref, bf16[32,192,256]{2,1,0:T(8,128)(2,1)} %bitcast.13, ...), custom_call_target="tpu_custom_call" | custom-call | tf_op jit(solution)/shard_map/attend/pallas_call | solution.py:202
  (15 shorter events, 0.1 us)
Async XLA Ops:
  6.5 48.6 %all-gather.8.cloned.1.call-start = ((), (), s32[]{:S(2)}) async-start(), calls=%async_computation.3 | async-start | bytes 1916928 | tf_op jit(solution)/shard_map/all_gather | solution.py:236
  11.1 136.1 %all-gather.6.cloned.1.call-start = ((), (), s32[]{:S(2)}) async-start(), calls=%async_computation.2 | async-start | bytes 5324800 | tf_op jit(solution)/shard_map/all_gather | solution.py:243
  46.5 8.6 %copy-start.1 = (bf16[32,64,256]{2,1,0:T(8,128)(2,1)}, bf16[32,64,256]{2,1,0:T(8,128)(2,1)S(1)}, u32[]{:S(2)}) copy-start(bf16[32,64,256]{2,1,0:T(8,128)(2,1)S(1)} %all_to_all.10.mine_ref) | copy-start | bytes 3145732
  46.5 8.6 %collective-permute-start = (bf16[32,64,256]{2,1,0:T(8,128)(2,1)S(1)}, bf16[32,64,256]{2,1,0:T(8,128)(2,1)S(1)}, u32[]{:S(2)}, u32[]{:S(2)}) collective-permute-start(bf16[32,64,256]{2,1,0:T(8,128)(2,1)S(1)} %all_to_all.10.mine_ref), channel_id=1, source_target_pairs={{0,8},{8,0},{1,9},{9,1},{2,10},{10,2},{3,11},{11,3},{4,12},{12,4},... | collective-permute-start | bytes 3145736 | tf_op jit(solution)/shard_map/ppermute | solution.py:223
  55.2 1.0 copy-start.2
  82.4 50.7 %copy-start.3 = (s32[192]{0:T(256)S(1)}, s32[192]{0:T(256)}, u32[]{:S(2)}) copy-start(s32[192]{0:T(256)} %param.18) | copy-start | bytes 2308
  112.3 42.2 %copy-start = (bf16[4,8,192,256]{3,2,1,0:T(8,128)(2,1)}, bf16[4,8,192,256]{3,2,1,0:T(8,128)(2,1)S(1)}, u32[]{:S(2)}) copy-start(bf16[4,8,192,256]{3,2,1,0:T(8,128)(2,1)S(1)} %all_to_all.11) | copy-start | bytes 9437188
  112.3 42.7 %collective-permute-start.1 = (bf16[32,192,256]{2,1,0:T(8,128)(2,1)S(1)}, bf16[32,192,256]{2,1,0:T(8,128)(2,1)}, u32[]{:S(2)}, u32[]{:S(2)}) collective-permute-start(bf16[32,192,256]{2,1,0:T(8,128)(2,1)S(1)} %bitcast.12), channel_id=1, source_target_pairs={{0,8},{8,0},{1,9},{9,1},{2,10},{10,2},{3,11},{11,3},{4,12},{12,4},... | collective-permute-start | bytes 9437192 | tf_op jit(solution)/shard_map/ppermute | solution.py:223
Sparse Core Ops, SparseCore 0:
  11.2 43.8 all-gather.7
  58.5 88.6 all-gather.5

commit v2 on v1

v2 whole, which is shorter than its diff:
```python
import math

import jax
import jax.numpy as jnp
from jax import lax
from jax.experimental import pallas as pl
from jax.experimental.pallas import tpu as pltpu
from jax.sharding import Mesh
from jax.sharding import PartitionSpec as P

PLANE = ("y", "x")
SEQ = ("y", "x", "core")
TILE = 512
VMEM_BYTES = 56 * 1024 * 1024


def whole(memory_space=pltpu.VMEM):
    return pl.BlockSpec(memory_space=memory_space)


def params():
    return pltpu.CompilerParams(vmem_limit_bytes=VMEM_BYTES)


def dot(a, b, contract_a=1, contract_b=0):
    return lax.dot_general(
        a, b, (((contract_a,), (contract_b,)), ((), ())), preferred_element_type=jnp.float32
    )


def pick_rows_kernel(tokens_ref, pos_ref, gain_ref, router_ref, out_ref):
    slots = pos_ref.shape[1]
    rows, width = tokens_ref.shape
    hit = lax.broadcasted_iota(jnp.int32, (rows, slots), 0) == pos_ref[...]
    one_hot = jnp.where(hit, 1.0, 0.0).astype(jnp.bfloat16)
    out_ref[:slots, :] = dot(one_hot, tokens_ref[...], 0, 0).astype(jnp.bfloat16)
    at = lax.broadcasted_iota(jnp.int32, (out_ref.shape[0] - slots, width), 0)
    extra = jnp.where(at == 0, gain_ref[...].astype(jnp.float32).reshape(1, width), 0.0)
    extra = jnp.where(at == 1, router_ref[...].astype(jnp.float32).reshape(1, width), extra)
    out_ref[slots:, :] = extra.astype(jnp.bfloat16)


def pick_rows(tokens, route_pos, x_gain, w_router):
    slots = route_pos.shape[0]
    width = tokens.shape[1]
    return pl.pallas_call(
        pick_rows_kernel,
        out_shape=jax.ShapeDtypeStruct((slots + 16, width), jnp.bfloat16),
        in_specs=[whole()] * 4,
        out_specs=whole(),
        compiler_params=params(),
        name="pick_rows",
    )(tokens, route_pos.reshape(1, slots), x_gain, w_router)


def head_norm(projected, gain):
    mean_sq = jnp.mean(projected * projected, axis=-1, keepdims=True)
    return (projected * lax.rsqrt(mean_sq + 1e-06) * gain).astype(jnp.bfloat16)


def in_feature_order(core, mine, other):
    even = jnp.where(core == 0, mine, other)
    odd = jnp.where(core == 0, other, mine)
    return jnp.stack([even, odd], axis=1).reshape(-1, mine.shape[-1])


def keys_kernel(
    place_ref, count_ref, rows_ref, mine_ref, other_ref, gain_ref, xn_ref, kv_ref, gate_ref, total, routed, scale
):
    parts, _, width = rows_ref.shape
    slots, head = gate_ref.shape
    core, count = place_ref[0], count_ref[0]
    at, steps, each = pl.program_id(0), pl.num_programs(0), mine_ref.shape[1]

    @pl.when(at == 0)
    def _():
        square = jnp.zeros((slots, width), jnp.float32)
        for part in range(parts):
            wide = rows_ref[part, :slots, :].astype(jnp.float32)
            square += wide * wide
        mean_sq = jnp.sum(square, axis=-1, keepdims=True) / (parts * width)
        scale[...] = jnp.broadcast_to(lax.rsqrt(mean_sq + 1e-05), scale.shape)
        total[...] = jnp.zeros_like(total)
        routed[...] = jnp.zeros_like(routed)

    for k in range(each):
        part = at * each + k
        extra = rows_ref[part, slots:, :].astype(jnp.float32)
        wide = rows_ref[part, :slots, :].astype(jnp.float32)
        normed = (wide * scale[:, :1] * extra[0:1]).astype(jnp.bfloat16)
        xn_ref[:, k * width : (k + 1) * width] = normed
        routed[...] += normed.astype(jnp.float32) * extra[1:2]
        weights = in_feature_order(core, mine_ref[:, k, :64, :], other_ref[:, k, :64, :])
        total[...] += dot(normed, weights)

    @pl.when(at == steps - 1)
    def _():
        gate = jax.nn.sigmoid(jnp.sum(routed[...], axis=-1, keepdims=True))
        gate_ref[...] = jnp.broadcast_to(gate, gate_ref.shape)
        kv_ref[0] = head_norm(total[:, :head], gain_ref[...])
        live = lax.broadcasted_iota(jnp.int32, (slots, head), 0) < count
        kv_ref[1] = jnp.where(live, total[:, head:], 0.0).astype(jnp.bfloat16)


def make_keys(core, count, rows, mine, other, gain, slots):
    parts, _, width = rows.shape
    nx, _, deep, both = mine.shape
    head = gain.shape[0]
    steps = 4
    each = parts // steps
    weights = pl.BlockSpec((nx, each, deep, both), lambda i: (0, i, 0, 0))
    return pl.pallas_call(
        keys_kernel,
        grid=(steps,),
        out_shape=(
            jax.ShapeDtypeStruct((slots, parts * width), jnp.bfloat16),
            jax.ShapeDtypeStruct((2, slots, head), jnp.bfloat16),
            jax.ShapeDtypeStruct((slots, head), jnp.float32),
        ),
        in_specs=[
            whole(pltpu.SMEM),
            whole(pltpu.SMEM),
            whole(),
            weights,
            weights,
            whole(),
        ],
        out_specs=(
            pl.BlockSpec((slots, each * width), lambda i: (0, i)),
            whole(),
            whole(),
        ),
        scratch_shapes=[
            pltpu.VMEM((slots, both), jnp.float32),
            pltpu.VMEM((slots, width), jnp.float32),
            pltpu.VMEM((slots, head), jnp.float32),
        ],
        compiler_params=params(),
        name="make_keys",
    )(core, count, rows, mine, other, gain.reshape(1, head))


def queries_kernel(xn_ref, weights_ref, gain_ref, out_ref, total):
    blocks, each, deep, width = weights_ref.shape
    head = gain_ref.shape[1]
    at = pl.program_id(0)

    @pl.when(at == 0)
    def _():
        total[...] = jnp.zeros_like(total)

    for k in range(each):
        weights = weights_ref[:, k].reshape(blocks * deep, width)
        total[...] += dot(xn_ref[:, k * blocks * deep : (k + 1) * blocks * deep], weights)

    @pl.when(at == pl.num_programs(0) - 1)
    def _():
        for h in range(0, width, head):
            out_ref[:, h : h + head] = head_norm(total[:, h : h + head], gain_ref[...])


def make_queries(xn, weights, gain):
    blocks, parts, deep, width = weights.shape
    slots = xn.shape[0]
    steps = 4
    each = parts // steps
    return pl.pallas_call(
        queries_kernel,
        grid=(steps,),
        out_shape=jax.ShapeDtypeStruct((slots, width), jnp.bfloat16),
        in_specs=[
            pl.BlockSpec((slots, each * blocks * deep), lambda i: (0, i)),
            pl.BlockSpec((blocks, each, deep, width), lambda i: (0, i, 0, 0)),
            whole(),
        ],
        out_specs=whole(),
        scratch_shapes=[pltpu.VMEM((slots, width), jnp.float32)],
        compiler_params=params(),
        name="make_queries",
    )(xn, weights, gain.reshape(1, -1))


def attend_kernel(
    place_ref, lengths_ref, count_ref, q_ref, own_ref, keys_ref, mine_ref, other_ref, pos_row_ref, pos_col_ref,
    gate_ref, out_ref, packed, total, end_ref,
):
    slots, head = gate_ref.shape
    group = q_ref.shape[1] // head
    core, count = place_ref[0], count_ref[0]
    step, steps = pl.program_id(0), pl.num_programs(0)
    factor = math.log2(math.e) / math.sqrt(head)
    fill = lax.broadcasted_iota(jnp.int32, (slots, head), 0)

    @pl.when(step == 0)
    def _():
        end_ref[0] = 0
        allowed = (pos_row_ref[...] <= pos_col_ref[...]) & (
            lax.broadcasted_iota(jnp.int32, (slots, slots), 1) < count
        )
        summed = jnp.concatenate([own_ref[1], jnp.ones((slots, head), jnp.bfloat16)], axis=1)
        for h in range(group):
            query = q_ref[:, h * head : (h + 1) * head]
            weights = jnp.exp2(dot(query, own_ref[0], 1, 1) * factor)
            weights = jnp.where(allowed, weights, 0.0).astype(jnp.bfloat16)
            total[h] = dot(weights, summed)

    def pack(at, offset):
        for which, ref in enumerate((mine_ref, other_ref)):
            length = lengths_ref[which, step * mine_ref.shape[1] + at]
            side = jnp.where(core == 0, which, 1 - which)

            @pl.when(length > 0)
            def _():
                where = pl.ds(pl.multiple_of(offset, 16), slots)
                packed[where, :head] = keys_ref[0, side, at]
                packed[where, head : 2 * head] = ref[0, at]
                packed[where, 2 * head :] = jnp.where(fill < length, 1.0, 0.0).astype(jnp.bfloat16)

            offset = offset + (length + 15) // 16 * 16
        return offset

    start = end_ref[0]
    end = lax.fori_loop(0, mine_ref.shape[1], pack, start)
    end_ref[0] = end

    @pl.when(step == steps - 1)
    def _():
        rest = pl.ds(pl.multiple_of(end, 16), TILE)
        packed[rest, :] = jnp.zeros((TILE, packed.shape[1]), jnp.bfloat16)

    def tile(at, carry):
        rows = pl.ds(pl.multiple_of(at * TILE, TILE), TILE)
        keys, values = packed[rows, :head], packed[rows, head:]
        for h in range(group):
            query = q_ref[:, h * head : (h + 1) * head]
            weights = jnp.exp2(dot(query, keys, 1, 1) * factor).astype(jnp.bfloat16)
            total[h] += dot(weights, values)
        return carry

    closing = jnp.where(step == steps - 1, TILE - 1, 0)
    lax.fori_loop(start // TILE, (end + closing) // TILE, tile, 0)

    @pl.when(step == steps - 1)
    def _():
        block = out_ref.shape[0]
        live = fill < count
        pieces = []
        for h in range(group):
            sums = total[h]
            piece = gate_ref[...] * sums[:, :head] / jnp.where(live, sums[:, head:], 1.0)
            pieces.append(jnp.where(live, piece, 0.0).astype(jnp.bfloat16))
        hit = (lax.broadcasted_iota(jnp.int32, (block, slots), 0) == pos_row_ref[...]) & (
            lax.broadcasted_iota(jnp.int32, (block, slots), 1) < count
        )
        one_hot = jnp.where(hit, 1.0, 0.0).astype(jnp.bfloat16)
        out_ref[...] = dot(one_hot, jnp.concatenate(pieces, axis=1)).astype(jnp.bfloat16)


def attend(core, lengths, count, queries, own, keys, mine, other, route_pos, gate, block):
    slots, width = queries.shape
    head = gate.shape[1]
    nx, ny = mine.shape[:2]
    sources = 2 * nx * ny
    most = sources * block // 8 + 16 * sources + slots + TILE
    values = pl.BlockSpec((1, ny, slots, head), lambda i: (i, 0, 0, 0))
    return pl.pallas_call(
        attend_kernel,
        grid=(nx,),
        out_shape=jax.ShapeDtypeStruct((block, width), jnp.bfloat16),
        in_specs=[
            whole(pltpu.SMEM),
            whole(pltpu.SMEM),
            whole(pltpu.SMEM),
            whole(),
            whole(),
            pl.BlockSpec((1, 2, ny, slots, head), lambda i: (i, 0, 0, 0, 0)),
            values,
            values,
            whole(),
            whole(),
            whole(),
        ],
        out_specs=whole(),
        scratch_shapes=[
            pltpu.VMEM(((most + TILE - 1) // TILE * TILE, 3 * head), jnp.bfloat16),
            pltpu.VMEM((width // head, slots, 2 * head), jnp.float32),
            pltpu.SMEM((1,), jnp.int32),
        ],
        compiler_params=params(),
        name="attend",
    )(
        core, lengths, count, queries, own, keys, mine, other,
        route_pos.reshape(1, slots), route_pos.reshape(slots, 1), gate,
    )


def to_all(block, axes, peers):
    return lax.all_to_all(
        jnp.broadcast_to(block[None], (peers,) + block.shape), axes, 0, 0, tiled=True
    )


def swap_cores(block):
    return lax.ppermute(block, "core", [(0, 1), (1, 0)])


def local(
    tokens, x_gain, w_router, w_query, key_weight, value_weight, q_gain, key_norm_gain, route_pos, route_count
):
    ny, nx, nz = lax.axis_size("y"), lax.axis_size("x"), lax.axis_size("z")
    block = tokens.shape[0]
    slots = route_pos.shape[0]
    core = lax.axis_index("core").astype(jnp.int32)
    shard = lax.axis_index(SEQ).astype(jnp.int32)
    deep, width = w_query.shape
    head = q_gain.shape[0]

    picked = pick_rows(tokens, route_pos, x_gain, w_router)
    rows = lax.all_gather(picked, "z", axis=0, tiled=False)

    weights = jnp.concatenate([w_query, key_weight, value_weight], axis=1)
    counted = jnp.full((8, weights.shape[1]), route_count[0].astype(jnp.bfloat16))
    weights_y = lax.all_gather(jnp.concatenate([weights, counted], axis=0), "y", axis=0, tiled=False)
    kv_mine = to_all(weights_y[:, :, width:], "x", nx)
    kv_other = swap_cores(kv_mine)
    wq = lax.all_gather(weights_y[:, :deep, :width], ("x", "core"), axis=0, tiled=False)

    normed, own, gate = make_keys(core[None], route_count, rows, kv_mine, kv_other, key_norm_gain, slots)

    own_y = lax.all_gather(own.reshape(2 * slots, head), "y", axis=0, tiled=False).reshape(ny, 2, slots, head)
    keys = lax.all_gather(own_y[:, 0], ("x", "core"), axis=0, tiled=False)
    keys = keys.reshape(nx, 2, ny, slots, head)
    mine = to_all(own_y[:, 1], "x", nx)
    other = swap_cores(mine)

    queries = make_queries(normed, wq, q_gain)
    counts = jnp.stack([kv_mine[:, :, deep, 0], kv_other[:, :, deep, 0]]).astype(jnp.int32)
    across, along = jnp.arange(nx, dtype=jnp.int32)[:, None], jnp.arange(ny, dtype=jnp.int32)[None, :]
    sides = jnp.stack([core, 1 - core])[:, None, None]
    earlier = (along * nx + across)[None] * 2 + sides < shard
    lengths = jnp.where(earlier, counts, 0).reshape(2, nx * ny)
    return attend(core[None], lengths, route_count, queries, own, keys, mine, other, route_pos, gate, block)


def solution(mesh):
    grid = Mesh(mesh.devices.reshape(8, 4, 2, 8), ("y", "x", "core", "z"))
    return jax.shard_map(
        local,
        mesh=grid,
        in_specs=(
            P(SEQ, "z"), P("z"), P("z"), P(SEQ, "z"), P(SEQ, "z"), P(SEQ, "z"), P(), P(), P(SEQ), P(SEQ),
        ),
        out_specs=P(SEQ, "z"),
        check_vma=False,
    )
```

time: 175 us -> 150 us (0.86)
  starting transfers between devices: 26 us -> 16.8 us
  waiting for transfers between devices: 16.8 us -> 9.07 us
  blocking collectives: 83.4 us -> 76.9 us
  other arithmetic: 3.46 us -> 1.63 us
    all_to_all x2, blocking collectives: 62.3 us -> 33.2 us  [to_all(): lax.all_to_all(jnp.broadcast_to(block[None], (peers,) + block.shape), axe...]
    all_gather x1 -> x2, blocking collectives: 21.2 us -> 43.7 us  [the longest x1 22.8 us: local(): lax.all_gather(own.reshape(2 * slots, head), 'y', axis=0, tiled=False)]
    ppermute x2, starting transfers between devices: 25.9 us -> 16.7 us  [swap_cores(): return lax.ppermute(block, 'core', [(0, 1), (1, 0)])]
    all_gather x1 -> x2, waiting for transfers between devices: 13.3 us -> 6.57 us  [the longest x1 6.56 us: local(): keys = lax.all_gather(own_y[:, 0], ('x', 'core'), axis=0, tiled=False)]
    all_gather x1, waiting for transfers between devices: 3.47 us -> 0.01 us  [local(): rows = lax.all_gather(picked, 'z', axis=0, tiled=False)]
    slice x0 -> x4, local copies, waits for them, and re-layouts: none -> 2.84 us  [the longest x1 0.99 us: local(): kv_other[:, :, deep, 0]]
    reshape x3 -> x0, local copies, waits for them, and re-layouts: 2.6 us -> none  [the longest x1 1.26 us: pick_rows(): x_gain.reshape(1, width)]
    ppermute x2, waiting for transfers between devices: 0.01 us -> 2.45 us  [swap_cores(): return lax.ppermute(block, 'core', [(0, 1), (1, 0)])]
  transfers between devices with their start and end apart: 4 -> 5, of which waited for: 2 -> 2; matrix products, arithmetic and copies ran while one was open for 4% -> 5% of each run, Pallas kernels for 5% -> 7%
where the time goes in v2:
time: 150 us; the launch traced here: 149 us
  blocking collectives  76.9 us (51%)
  Pallas kernels  24.5 us (16%)
  starting transfers between devices  16.8 us (11%)
  between operations  13.9 us (9%)
  waiting for transfers between devices  9.07 us (6%)
  local copies, waits for them, and re-layouts  6.19 us (4%)
  other arithmetic  1.63 us (1%)
    all_to_all x2, blocking collectives, to_all(): lax.all_to_all(jnp.broadcast_to(block[None], (peers,) + block.shape), axe...  33.2 us
    all_gather x1, blocking collectives, local(): lax.all_gather(own.reshape(2 * slots, head), 'y', axis=0, tiled=False)  22.8 us
    all_gather x1, blocking collectives, local(): lax.all_gather(jnp.concatenate([weights, counted], axis=0), 'y', axis=0,...  21 us
    ppermute x2, starting transfers between devices, swap_cores(): return lax.ppermute(block, 'core', [(0, 1), (1, 0)])  16.7 us
    pallas_call x1, Pallas kernels, attend(): pl.pallas_call(attend_kernel, grid=(nx,), out_shape=jax.ShapeDtypeStruct(...  11.8 us
    all_gather x1, waiting for transfers between devices, local(): keys = lax.all_gather(own_y[:, 0], ('x', 'core'), axis=0, tiled=False)  6.56 us
    pallas_call x1, Pallas kernels, make_keys(): pl.pallas_call(keys_kernel, grid=(steps,), out_shape=(jax.ShapeDtypeStruc...  5.64 us
    pallas_call x1, Pallas kernels, make_queries(): pl.pallas_call(queries_kernel, grid=(steps,), out_shape=jax.ShapeDtypeStr...  5.01 us
  transfers between devices with their start and end apart: 5, of which 2 were waited for; matrix products, arithmetic and copies ran while one was open for 5% of the time, Pallas kernels for 7%

profile of v2, /device:TPU:57, one launch (start us, length us, event | category | flops | bytes accessed | tf_op | source)
XLA Modules:
  0.0 149.0 jit_solution(7482042441741172251)
XLA Ops:
  6.5 2.0 %pick_rows.1 = bf16[208,512]{1,0:T(8,128)(2,1)} custom-call(bf16[512,512]{1,0:T(8,128)(2,1)} %tokens_ref.1, s32[1,192]{1,0:T(1,128)} %bitcast.22, bf16[512]{0:T(512)(128)(2,1)} %gain_ref.1, bf16[512]{0:T(512)(128)(2,1)} %router_ref.1), custom_call_target="tpu_custom_call" | custom-call | tf_op jit(solution)/shard_map/pick_rows/pallas_call | solution.py:46
  9.3 0.9 fusion.4
  10.2 21.0 %all-gather = bf16[576,768]{1,0:T(8,128)(2,1)S(1)} all-gather(bf16[72,768]{1,0:T(8,128)(2,1)S(1)} %fusion.4), channel_id=2, replica_groups=mesh['y'=8,'x'=4,'core'=2,'z'=8] {'y'}, dimensions={0}, use_global_device_ids=true | all-gather | bytes 995328 | tf_op jit(solution)/shard_map/all_gather | solution.py:323
  31.2 0.8 slice.27
  32.2 13.9 %all_to_all.10.mine_ref = bf16[4,8,72,256]{3,2,1,0:T(8,128)(2,1)S(1)} all-to-all(bf16[4,8,72,256]{3,2,1,0:T(8,128)(2,1)S(1)} %broadcast_in_dim.12), channel_id=1, replica_groups=mesh['y'=8,'x'=4,'core'=2,'z'=8] {'x'}, dimensions={0} | all-to-all | bytes 2359296 | tf_op jit(solution)/shard_map/all_to_all | solution.py:298
  46.1 10.0 %collective-permute-start = (bf16[4,8,72,256]{3,2,1,0:T(8,128)(2,1)S(1)}, bf16[4,8,72,256]{3,2,1,0:T(8,128)(2,1)S(1)}, u32[]{:S(2)}, u32[]{:S(2)}) collective-permute-start(bf16[4,8,72,256]{3,2,1,0:T(8,128)(2,1)S(1)} %all_to_all.10.mine_ref), channel_id=1, source_target_pairs={{0,8},{8,0},{1,9},{9,1},{2,10},{10,2},{3,11},{11,3},{4,12},{12,4},... | collective-permute-start | bytes 3538952 | tf_op jit(solution)/shard_map/ppermute | solution.py:304
  56.1 2.4 %collective-permute-done.other_ref = bf16[4,8,72,256]{3,2,1,0:T(8,128)(2,1)S(1)} collective-permute-done((bf16[4,8,72,256]{3,2,1,0:T(8,128)(2,1)S(1)}, bf16[4,8,72,256]{3,2,1,0:T(8,128)(2,1)S(1)}, u32[]{:S(2)}, u32[]{:S(2)}) %collective-permute-start) | collective-permute-done | bytes 1179680 | tf_op jit(solution)/shard_map/ppermute | solution.py:304
  58.6 1.1 copy-done.3
  59.6 5.6 %make_keys.1 = (bf16[192,4096]{1,0:T(8,128)(2,1)}, bf16[2,192,128]{2,1,0:T(8,128)(2,1)}, f32[192,128]{1,0:T(8,128)}) custom-call(s32[1]{0:T(128)} %bitcast.place_ref, s32[1]{0:T(128)S(6)} %copy.13.count_ref, bf16[8,208,512]{2,1,0:T(8,128)(2,1)} %bitcast.20, bf16[4,8,72,256]{3,2,1,0:T(8,128)(2,1)} %copy-done.1, bf16[4,8,72,256]{3,2,1,0:T(8,128)(2,1)} %copy-done.3, ...), custom_call_target="tpu_custom_call" | custom-call | tf_op jit(solution)/shard_map/make_keys/pallas_call | solution.py:112
  65.3 22.8 %all_gather.30 = bf16[8,384,128]{2,1,0:T(8,128)(2,1)S(1)} all-gather(bf16[1,384,128]{2,1,0:T(8,128)(2,1)} %bitcast.21), channel_id=1, replica_groups=mesh['y'=8,'x'=4,'core'=2,'z'=8] {'y'}, dimensions={0}, use_global_device_ids=true | all-gather | bytes 884736 | tf_op jit(solution)/shard_map/all_gather | solution.py:330
  88.0 0.8 slice_bitcast_fusion
  88.9 0.3 broadcast_in_dim.30
  89.3 19.3 %all_to_all.11.mine_ref = bf16[4,8,192,128]{3,2,1,0:T(8,128)(2,1)S(1)} all-to-all(bf16[4,8,192,128]{3,2,1,0:T(8,128)(2,1)S(1)} %broadcast_in_dim.30), channel_id=1, replica_groups=mesh['y'=8,'x'=4,'core'=2,'z'=8] {'x'}, dimensions={0} | all-to-all | bytes 3145728 | tf_op jit(solution)/shard_map/all_to_all | solution.py:298
  108.6 6.7 %collective-permute-start.1 = (bf16[4,8,192,128]{3,2,1,0:T(8,128)(2,1)S(1)}, bf16[4,8,192,128]{3,2,1,0:T(8,128)(2,1)S(1)}, u32[]{:S(2)}, u32[]{:S(2)}) collective-permute-start(bf16[4,8,192,128]{3,2,1,0:T(8,128)(2,1)S(1)} %all_to_all.11.mine_ref), channel_id=1, source_target_pairs={{0,8},{8,0},{1,9},{9,1},{2,10},{10,2},{3,11},{11,3},{4,12},{12,4},... | collective-permute-start | bytes 4718600 | tf_op jit(solution)/shard_map/ppermute | solution.py:304
  115.3 0.1 mul.31
  115.4 0.8 copy.12.pos_col_ref
  116.2 1.0 slice_reduce_fusion.1
  117.2 0.1 stack.16
  117.3 1.0 slice_reduce_fusion
  118.3 0.1 stack.17
  118.4 0.7 compare_select_fusion.lengths_ref
  119.0 5.0 %make_queries.1.q_ref = bf16[192,512]{1,0:T(8,128)(2,1)} custom-call(bf16[192,4096]{1,0:T(8,128)(2,1)} %get-tuple-element.8.xn_ref, bf16[8,8,64,512]{3,2,1,0:T(8,128)(2,1)} %bitcast.15, f32[1,128]{1,0:T(1,128)} %bitcast.26), custom_call_target="tpu_custom_call" | custom-call | tf_op jit(solution)/shard_map/make_queries/pallas_call | solution.py:167
  124.1 6.6 %all-gather.12.cloned.1.call-done = bf16[64,1,192,128]{3,2,1,0:T(8,128)(2,1)} async-done(((bf16[8,1,192,128]{3,2,1,0:T(8,128)(2,1)}), bf16[64,1,192,128]{3,2,1,0:T(8,128)(2,1)}) %all-gather.12.cloned.1.call-update) | async-done | bytes 3145744 | tf_op jit(solution)/shard_map/all_gather | solution.py:331
  130.6 11.8 %attend.1 = bf16[512,512]{1,0:T(8,128)(2,1)} custom-call(s32[1]{0:T(128)} %bitcast.place_ref, s32[2,32]{1,0:T(2,128)} %compare_select_fusion.lengths_ref, s32[1]{0:T(128)S(6)} %copy.13.count_ref, bf16[192,512]{1,0:T(8,128)(2,1)} %make_queries.1.q_ref, bf16[2,192,128]{2,1,0:T(8,128)(2,1)} %get-tuple-element.9.own_ref, bf16[4,2,8,192,128]{4,3,2,1,0:T(8,128)(2,1)} %bitcast.18, ...), custom_call_target="tpu_custom_call" | custom-call | tf_op jit(solution)/shard_map/attend/pallas_call | solution.py:266
  (23 shorter events, 0.3 us)
Async XLA Ops:
  6.5 52.0 %all-gather.8.cloned.1.call-start = ((), (), s32[]{:S(2)}) async-start(), calls=%async_computation.2 | async-start | bytes 1916928 | tf_op jit(solution)/shard_map/all_gather | solution.py:319
  8.6 110.4 %all-gather.10.cloned.1.call-start = ((), (), s32[]{:S(2)}) async-start(), calls=%async_computation.3 | async-start | bytes 4718592 | tf_op jit(solution)/shard_map/all_gather | solution.py:326
  32.0 98.6 %all-gather.12.cloned.1.call-start = ((), (), s32[]{:S(2)}) async-start(), calls=%async_computation.4 | async-start | bytes 3538944 | tf_op jit(solution)/shard_map/all_gather | solution.py:331
  46.1 12.5 %copy-start.1 = (bf16[4,8,72,256]{3,2,1,0:T(8,128)(2,1)}, bf16[4,8,72,256]{3,2,1,0:T(8,128)(2,1)S(1)}, u32[]{:S(2)}) copy-start(bf16[4,8,72,256]{3,2,1,0:T(8,128)(2,1)S(1)} %all_to_all.10.mine_ref) | copy-start | bytes 3538948
  46.1 12.5 %collective-permute-start = (bf16[4,8,72,256]{3,2,1,0:T(8,128)(2,1)S(1)}, bf16[4,8,72,256]{3,2,1,0:T(8,128)(2,1)S(1)}, u32[]{:S(2)}, u32[]{:S(2)}) collective-permute-start(bf16[4,8,72,256]{3,2,1,0:T(8,128)(2,1)S(1)} %all_to_all.10.mine_ref), channel_id=1, source_target_pairs={{0,8},{8,0},{1,9},{9,1},{2,10},{10,2},{3,11},{11,3},{4,12},{12,4},... | collective-permute-start | bytes 3538952 | tf_op jit(solution)/shard_map/ppermute | solution.py:304
  58.6 1.1 copy-start.3
  89.2 26.1 %copy-start.4 = (s32[192]{0:T(256)S(1)}, s32[192]{0:T(256)}, u32[]{:S(2)}) copy-start(s32[192]{0:T(256)} %param.18) | copy-start | bytes 2308
  108.6 15.5 %copy-start = (bf16[4,8,192,128]{3,2,1,0:T(8,128)(2,1)}, bf16[4,8,192,128]{3,2,1,0:T(8,128)(2,1)S(1)}, u32[]{:S(2)}) copy-start(bf16[4,8,192,128]{3,2,1,0:T(8,128)(2,1)S(1)} %all_to_all.11.mine_ref) | copy-start | bytes 4718596
  108.6 15.5 %collective-permute-start.1 = (bf16[4,8,192,128]{3,2,1,0:T(8,128)(2,1)S(1)}, bf16[4,8,192,128]{3,2,1,0:T(8,128)(2,1)S(1)}, u32[]{:S(2)}, u32[]{:S(2)}) collective-permute-start(bf16[4,8,192,128]{3,2,1,0:T(8,128)(2,1)S(1)} %all_to_all.11.mine_ref), channel_id=1, source_target_pairs={{0,8},{8,0},{1,9},{9,1},{2,10},{10,2},{3,11},{11,3},{4,12},{12,4},... | collective-permute-start | bytes 4718600 | tf_op jit(solution)/shard_map/ppermute | solution.py:304
  124.1 6.6 %copy-start.2 = (bf16[4,8,192,128]{3,2,1,0:T(8,128)(2,1)}, bf16[4,8,192,128]{3,2,1,0:T(8,128)(2,1)S(1)}, u32[]{:S(2)}) copy-start(bf16[4,8,192,128]{3,2,1,0:T(8,128)(2,1)S(1)} %collective-permute-done.1.other_ref) | copy-start | bytes 4718596
Sparse Core Ops, SparseCore 0:
  9.4 43.7 all-gather.7
  55.4 39.9 all-gather.9
  97.5 33.0 all-gather.11

commit v3 on v1

v3 whole, which is shorter than its diff:
```python
import math

import jax
import jax.numpy as jnp
from jax import lax
from jax.experimental import pallas as pl
from jax.experimental.pallas import tpu as pltpu
from jax.sharding import Mesh
from jax.sharding import PartitionSpec as P

SEQ = ("yh", "yl", "x", "core")
TILE = 1024
HALF = 512


def whole(memory_space=pltpu.VMEM):
    return pl.BlockSpec(memory_space=memory_space)


def params(mebibytes):
    return pltpu.CompilerParams(vmem_limit_bytes=mebibytes * 1024 * 1024)


def dot(a, b, contract_a=1, contract_b=0):
    return lax.dot_general(
        a, b, (((contract_a,), (contract_b,)), ((), ())), preferred_element_type=jnp.float32
    )


def pick_rows_kernel(tokens_ref, pos_ref, gain_ref, router_ref, out_ref):
    slots = pos_ref.shape[1]
    rows, width = tokens_ref.shape
    hit = lax.broadcasted_iota(jnp.int32, (rows, slots), 0) == pos_ref[...]
    one_hot = jnp.where(hit, 1.0, 0.0).astype(jnp.bfloat16)
    out_ref[:slots, :] = dot(one_hot, tokens_ref[...], 0, 0).astype(jnp.bfloat16)
    at = lax.broadcasted_iota(jnp.int32, (out_ref.shape[0] - slots, width), 0)
    extra = jnp.where(at == 0, gain_ref[...].astype(jnp.float32).reshape(1, width), 0.0)
    extra = jnp.where(at == 1, router_ref[...].astype(jnp.float32).reshape(1, width), extra)
    out_ref[slots:, :] = extra.astype(jnp.bfloat16)


def pick_rows(tokens, route_pos, x_gain, w_router):
    slots = route_pos.shape[0]
    width = tokens.shape[1]
    return pl.pallas_call(
        pick_rows_kernel,
        out_shape=jax.ShapeDtypeStruct((slots + 16, width), jnp.bfloat16),
        in_specs=[whole()] * 4,
        out_specs=whole(),
        compiler_params=params(8),
        name="pick_rows",
    )(tokens, route_pos.reshape(1, slots), x_gain, w_router)


def head_norm(projected, gain):
    mean_sq = jnp.mean(projected * projected, axis=-1, keepdims=True)
    return (projected * lax.rsqrt(mean_sq + 1e-06) * gain).astype(jnp.bfloat16)


def in_feature_order(core, mine, other):
    even = jnp.where(core == 0, mine, other)
    odd = jnp.where(core == 0, other, mine)
    return jnp.stack([even, odd], axis=1).reshape(-1, mine.shape[-1])


def keys_kernel(place_ref, count_ref, rows_ref, mine_ref, other_ref, gain_ref, xn_ref, kv_ref, gate_ref):
    parts, _, width = rows_ref.shape
    slots, head = gate_ref.shape
    core, count = place_ref[0], count_ref[0]
    square = jnp.zeros((slots, width), jnp.float32)
    for part in range(parts):
        wide = rows_ref[part, :slots, :].astype(jnp.float32)
        square += wide * wide
    mean_sq = jnp.sum(square, axis=-1, keepdims=True) / (parts * width)
    scale = lax.rsqrt(mean_sq + 1e-05)
    total = jnp.zeros((slots, 2 * head), jnp.float32)
    routed = jnp.zeros((slots, width), jnp.float32)
    for part in range(parts):
        extra = rows_ref[part, slots:, :].astype(jnp.float32)
        wide = rows_ref[part, :slots, :].astype(jnp.float32)
        normed = (wide * scale * extra[0:1]).astype(jnp.bfloat16)
        xn_ref[:, part * width : (part + 1) * width] = normed
        routed += normed.astype(jnp.float32) * extra[1:2]
        weights = in_feature_order(core, mine_ref[:, part], other_ref[:, part])
        total += dot(normed, weights)
    gate = jax.nn.sigmoid(jnp.sum(routed, axis=-1, keepdims=True))
    gate_ref[...] = jnp.broadcast_to(gate, gate_ref.shape)
    kv_ref[0] = head_norm(total[:, :head], gain_ref[...])
    live = lax.broadcasted_iota(jnp.int32, (slots, head), 0) < count
    kv_ref[1] = jnp.where(live, total[:, head:], 0.0).astype(jnp.bfloat16)


def make_keys(place, count, rows, mine, other, gain, slots):
    parts, _, width = rows.shape
    head = gain.shape[0]
    return pl.pallas_call(
        keys_kernel,
        out_shape=(
            jax.ShapeDtypeStruct((slots, parts * width), jnp.bfloat16),
            jax.ShapeDtypeStruct((2, slots, head), jnp.bfloat16),
            jax.ShapeDtypeStruct((slots, head), jnp.float32),
        ),
        in_specs=[whole(pltpu.SMEM)] * 2 + [whole()] * 4,
        out_specs=(whole(),) * 3,
        compiler_params=params(16),
        name="make_keys",
    )(place, count, rows, mine, other, gain.reshape(1, head))


def queries_kernel(xn_ref, weights_ref, gain_ref, out_ref, counts_ref, total):
    blocks, each, _, width = weights_ref.shape
    head = gain_ref.shape[1]
    deep = xn_ref.shape[1] // (blocks * each)
    at = pl.program_id(0)

    @pl.when(at == 0)
    def _():
        total[...] = jnp.zeros_like(total)

    for k in range(each):
        weights = weights_ref[:, k, :deep].reshape(blocks * deep, width)
        total[...] += dot(xn_ref[:, k * blocks * deep : (k + 1) * blocks * deep], weights)
        counts = jnp.max(weights_ref[:, k, deep:, :head].astype(jnp.float32), axis=1)
        counts_ref[at * each + k] = counts.astype(jnp.int32)

    @pl.when(at == pl.num_programs(0) - 1)
    def _():
        for h in range(0, width, head):
            out_ref[:, h : h + head] = head_norm(total[:, h : h + head], gain_ref[...])


def make_queries(xn, weights, gain):
    blocks, parts, padded, width = weights.shape
    slots = xn.shape[0]
    head = gain.shape[0]
    steps = 4
    each = parts // steps
    return pl.pallas_call(
        queries_kernel,
        grid=(steps,),
        out_shape=(
            jax.ShapeDtypeStruct((slots, width), jnp.bfloat16),
            jax.ShapeDtypeStruct((parts, blocks, head), jnp.int32),
        ),
        in_specs=[
            pl.BlockSpec((slots, xn.shape[1] // steps), lambda i: (0, i)),
            pl.BlockSpec((blocks, each, padded, width), lambda i: (0, i, 0, 0)),
            whole(),
        ],
        out_specs=(whole(), whole()),
        scratch_shapes=[pltpu.VMEM((slots, width), jnp.float32)],
        compiler_params=params(16),
        name="make_queries",
    )(xn, weights, gain.reshape(1, -1))


def pack(place_ref, counts_ref, nx, store):
    ny = counts_ref.shape[0]
    core, shard = place_ref[0], place_ref[1]

    def step(at, offset):
        x, y = at // ny, at % ny
        for which in range(2):
            side = jnp.where(core == 0, which, 1 - which)
            earlier = (y * nx + x) * 2 + side < shard
            length = jnp.where(earlier, counts_ref[y, x * 2 + side, 0], 0)

            @pl.when(length > 0)
            def _():
                store(pl.multiple_of(offset, 16), which, side, x, y, length)

            offset = offset + (length + 15) // 16 * 16
        return offset

    return lax.fori_loop(0, nx * ny, step, jnp.int32(0))


def scores_kernel(
    place_ref, counts_ref, count_ref, q_ref, own_ref, mine_ref, other_ref, pos_row_ref, pos_col_ref,
    out_ref, sums_ref, packed, end_ref,
):
    slots, head = own_ref.shape[1:]
    group = q_ref.shape[1] // head
    count = count_ref[0]
    at = pl.program_id(0)
    factor = math.log2(math.e) / math.sqrt(head)

    @pl.when(at == 0)
    def _():
        def store(offset, which, side, x, y, length):
            packed[pl.ds(offset, slots), :] = (mine_ref, other_ref)[which][x, y]

        end = pack(place_ref, counts_ref, mine_ref.shape[0], store)
        end_ref[0] = end
        packed[pl.ds(pl.multiple_of(end, 16), TILE), :] = jnp.zeros((TILE, head), jnp.bfloat16)
        allowed = (pos_row_ref[...] <= pos_col_ref[...]) & (
            lax.broadcasted_iota(jnp.int32, (slots, slots), 1) < count
        )
        summed = jnp.concatenate([own_ref[1], jnp.ones((slots, head), jnp.bfloat16)], axis=1)
        for h in range(group):
            query = q_ref[:, h * head : (h + 1) * head]
            weights = jnp.exp2(dot(query, own_ref[0], 1, 1) * factor)
            weights = jnp.where(allowed, weights, 0.0).astype(jnp.bfloat16)
            sums_ref[h] = dot(weights, summed)

    for half in range(0, TILE, HALF):

        @pl.when(at * TILE + half < end_ref[0])
        def _():
            keys = packed[pl.ds(pl.multiple_of(at * TILE + half, HALF), HALF), :]
            for h in range(group):
                query = q_ref[:, h * head : (h + 1) * head]
                weights = jnp.exp2(dot(query, keys, 1, 1) * factor)
                out_ref[h, :, half : half + HALF] = weights.astype(jnp.bfloat16)


def packed_rows(sources, block, slots):
    return -(-(sources * block // 8 + 16 * sources) // TILE) * TILE


def scores(place, counts, count, queries, own, mine, other, route_pos, block):
    slots, width = queries.shape
    head = own.shape[2]
    nx, ny = mine.shape[:2]
    rows = packed_rows(2 * nx * ny, block, slots)
    group = width // head
    return pl.pallas_call(
        scores_kernel,
        grid=(rows // TILE,),
        out_shape=(
            jax.ShapeDtypeStruct((group, slots, rows), jnp.bfloat16),
            jax.ShapeDtypeStruct((group, slots, 2 * head), jnp.float32),
        ),
        in_specs=[whole(pltpu.SMEM)] * 3 + [whole()] * 6,
        out_specs=(pl.BlockSpec((group, slots, TILE), lambda i: (0, 0, i)), whole()),
        scratch_shapes=[pltpu.VMEM((rows + TILE, head), jnp.bfloat16), pltpu.SMEM((1,), jnp.int32)],
        compiler_params=params(24),
        name="scores",
    )(place, counts, count, queries, own, mine, other, route_pos.reshape(1, slots), route_pos.reshape(slots, 1))


def attend_kernel(
    place_ref, counts_ref, count_ref, weights_ref, sums_ref, values_ref, pos_row_ref, gate_ref,
    out_ref, packed, total, end_ref,
):
    slots, head = gate_ref.shape
    group = weights_ref.shape[0]
    count = count_ref[0]
    at = pl.program_id(0)
    fill = lax.broadcasted_iota(jnp.int32, (slots, head), 0)

    @pl.when(at == 0)
    def _():
        def store(offset, which, side, x, y, length):
            packed[pl.ds(offset, slots), :head] = values_ref[x, side, y]
            packed[pl.ds(offset, slots), head:] = jnp.where(fill < length, 1.0, 0.0).astype(jnp.bfloat16)

        end = pack(place_ref, counts_ref, values_ref.shape[0], store)
        end_ref[0] = end
        packed[pl.ds(pl.multiple_of(end, 16), TILE), :] = jnp.zeros((TILE, 2 * head), jnp.bfloat16)
        total[...] = sums_ref[...]

    for half in range(0, TILE, HALF):

        @pl.when(at * TILE + half < end_ref[0])
        def _():
            values = packed[pl.ds(pl.multiple_of(at * TILE + half, HALF), HALF), :]
            for h in range(group):
                total[h] += dot(weights_ref[h, :, half : half + HALF], values)

    @pl.when(at == pl.num_programs(0) - 1)
    def _():
        block = out_ref.shape[0]
        live = fill < count
        pieces = []
        for h in range(group):
            sums = total[h]
            piece = gate_ref[...] * sums[:, :head] / jnp.where(live, sums[:, head:], 1.0)
            pieces.append(jnp.where(live, piece, 0.0).astype(jnp.bfloat16))
        hit = (lax.broadcasted_iota(jnp.int32, (block, slots), 0) == pos_row_ref[...]) & (
            lax.broadcasted_iota(jnp.int32, (block, slots), 1) < count
        )
        one_hot = jnp.where(hit, 1.0, 0.0).astype(jnp.bfloat16)
        out_ref[...] = dot(one_hot, jnp.concatenate(pieces, axis=1)).astype(jnp.bfloat16)


def attend(place, counts, count, weights, sums, values, route_pos, gate, block):
    group, slots, rows = weights.shape
    head = gate.shape[1]
    return pl.pallas_call(
        attend_kernel,
        grid=(rows // TILE,),
        out_shape=jax.ShapeDtypeStruct((block, group * head), jnp.bfloat16),
        in_specs=[whole(pltpu.SMEM)] * 3
        + [pl.BlockSpec((group, slots, TILE), lambda i: (0, 0, i))]
        + [whole()] * 4,
        out_specs=whole(),
        scratch_shapes=[
            pltpu.VMEM((rows + TILE, 2 * head), jnp.bfloat16),
            pltpu.VMEM((group, slots, 2 * head), jnp.float32),
            pltpu.SMEM((1,), jnp.int32),
        ],
        compiler_params=params(24),
        name="attend",
    )(place, counts, count, weights, sums, values, route_pos.reshape(1, slots), gate)


def to_all(block, axes, peers):
    return lax.all_to_all(
        jnp.broadcast_to(block[None], (peers,) + block.shape), axes, 0, 0, tiled=True
    )


def over_y(block):
    pair = lax.all_gather(block, "yl", axis=0, tiled=False)
    every = lax.all_gather(pair, "yh", axis=0, tiled=False)
    return every.reshape((-1,) + block.shape)


def swap_cores(block):
    return lax.ppermute(block, "core", [(0, 1), (1, 0)])


def local(
    tokens, x_gain, w_router, w_query, key_weight, value_weight, q_gain, key_norm_gain, route_pos, route_count
):
    ny, nx = lax.axis_size(("yh", "yl")), lax.axis_size("x")
    block = tokens.shape[0]
    slots = route_pos.shape[0]
    place = jnp.stack([lax.axis_index("core"), lax.axis_index(SEQ)]).astype(jnp.int32)
    deep, width = w_query.shape
    head = q_gain.shape[0]

    picked = pick_rows(tokens, route_pos, x_gain, w_router)
    rows = lax.all_gather(picked, "z", axis=0, tiled=False)

    weights = jnp.concatenate([w_query, key_weight, value_weight], axis=1)
    counted = jnp.full((16, weights.shape[1]), route_count[0].astype(jnp.bfloat16))
    weights_y = over_y(jnp.concatenate([weights, counted], axis=0))
    kv_mine = to_all(weights_y[:, :deep, width:], "x", nx)
    weights_y, kv_mine = lax.optimization_barrier((weights_y, kv_mine))
    kv_other = swap_cores(kv_mine)
    wq = lax.all_gather(weights_y[:, :, :width], ("x", "core"), axis=0, tiled=False)

    normed, own, gate = make_keys(place, route_count, rows, kv_mine, kv_other, key_norm_gain, slots)

    own_y = over_y(own.reshape(2 * slots, head)).reshape(ny, 2, slots, head)
    values = lax.all_gather(own_y[:, 1], ("x", "core"), axis=0, tiled=False).reshape(nx, 2, ny, slots, head)
    mine = to_all(own_y[:, 0], "x", nx)
    other = swap_cores(mine)

    queries, counts = make_queries(normed, wq, q_gain)
    parts, sums = scores(place, counts, route_count, queries, own, mine, other, route_pos, block)
    return attend(place, counts, route_count, parts, sums, values, route_pos, gate, block)


def solution(mesh):
    grid = Mesh(mesh.devices.reshape(4, 2, 4, 2, 8), SEQ + ("z",))
    return jax.shard_map(
        local,
        mesh=grid,
        in_specs=(
            P(SEQ, "z"), P("z"), P("z"), P(SEQ, "z"), P(SEQ, "z"), P(SEQ, "z"), P(), P(), P(SEQ), P(SEQ),
        ),
        out_specs=P(SEQ, "z"),
        check_vma=False,
    )
```

time: 175 us -> 163 us (0.931)
  local copies, waits for them, and re-layouts: 6.64 us -> 22.2 us
  starting transfers between devices: 26 us -> 11.9 us
  waiting for transfers between devices: 16.8 us -> 7.16 us
  Pallas kernels: 24.1 us -> 21.3 us
  other arithmetic: 3.46 us -> 0.96 us
  blocking collectives: 83.4 us -> 85.2 us
    all_gather x1 -> x4, blocking collectives: 21.2 us -> 43.1 us  [the longest x2 31.7 us: over_y(): every = lax.all_gather(pair, 'yh', axis=0, tiled=False)]
    all_to_all x2, blocking collectives: 62.3 us -> 42.2 us  [to_all(): lax.all_to_all(jnp.broadcast_to(block[None], (peers,) + block.shape), axe...]
    unnamed x8 -> x32, local copies, waits for them, and re-layouts: 1.04 us -> 19.9 us
    ppermute x2, starting transfers between devices: 25.9 us -> 11.8 us  [swap_cores(): return lax.ppermute(block, 'core', [(0, 1), (1, 0)])]
    all_gather x1 -> x2, waiting for transfers between devices: 13.3 us -> 4.93 us  [the longest x1 4.91 us: local(): lax.all_gather(own_y[:, 1], ('x', 'core'), axis=0, tiled=False)]
    all_gather x1, waiting for transfers between devices: 3.47 us -> 0.01 us  [local(): rows = lax.all_gather(picked, 'z', axis=0, tiled=False)]
    reshape x4 -> x1, local copies, waits for them, and re-layouts: 3.36 us -> 0.12 us  [scores(): route_pos.reshape(slots, 1)]
    pallas_call x1, Pallas kernels: 4.64 us -> 2.1 us  [make_keys(): pl.pallas_call(keys_kernel, out_shape=(jax.ShapeDtypeStruct((slots, parts...]
  transfers between devices with their start and end apart: 4 -> 5, of which waited for: 2 -> 2; matrix products, arithmetic and copies ran while one was open for 4% -> 2% of each run, Pallas kernels for 5% -> 7%
where the time goes in v3:
time: 163 us
  blocking collectives  85.2 us (52%)
  local copies, waits for them, and re-layouts  22.2 us (14%)
  Pallas kernels  21.3 us (13%)
  between operations  13.9 us (9%)
  starting transfers between devices  11.9 us (7%)
  waiting for transfers between devices  7.16 us (4%)
    all_to_all x2, blocking collectives, to_all(): lax.all_to_all(jnp.broadcast_to(block[None], (peers,) + block.shape), axe...  42.2 us
    all_gather x2, blocking collectives, over_y(): every = lax.all_gather(pair, 'yh', axis=0, tiled=False)  31.7 us
    unnamed x32, local copies, waits for them, and re-layouts  19.9 us
    ppermute x2, starting transfers between devices, swap_cores(): return lax.ppermute(block, 'core', [(0, 1), (1, 0)])  11.8 us
    all_gather x2, blocking collectives, over_y(): pair = lax.all_gather(block, 'yl', axis=0, tiled=False)  11.4 us
    pallas_call x1, Pallas kernels, attend(): pl.pallas_call(attend_kernel, grid=(rows // TILE,), out_shape=jax.ShapeDt...  8.66 us
    pallas_call x1, Pallas kernels, scores(): pl.pallas_call(scores_kernel, grid=(rows // TILE,), out_shape=(jax.ShapeD...  7.32 us
    all_gather x1, waiting for transfers between devices, local(): lax.all_gather(own_y[:, 1], ('x', 'core'), axis=0, tiled=False)  4.91 us
  transfers between devices with their start and end apart: 5, of which 2 were waited for; matrix products, arithmetic and copies ran while one was open for 2% of the time, Pallas kernels for 7%

profile of v3, /device:TPU:57, one launch (start us, length us, event | category | flops | bytes accessed | tf_op | source)
XLA Modules:
  0.0 162.7 jit_solution(13610315954339193672)
XLA Ops:
  6.5 1.0 copy-done.9
  9.6 1.0 pick_rows.1
  12.2 4.9 %all-gather.1 = bf16[160,768]{1,0:T(8,128)(2,1)S(1)} all-gather(bf16[80,768]{1,0:T(8,128)(2,1)S(1)} %fusion.4), channel_id=3, replica_groups=mesh['yh'=4,'yl'=2,'x'=4,'core'=2,'z'=8] {'yl'}, dimensions={0}, use_global_device_ids=true | all-gather | bytes 368640 | tf_op jit(solution)/shard_map/all_gather | solution.py:315
  17.1 17.0 %all-gather.2 = bf16[8,80,768]{2,1,0:T(8,128)(2,1)S(1)} all-gather(bf16[2,80,768]{2,1,0:T(8,128)(2,1)S(1)} %bitcast.26), channel_id=4, replica_groups=mesh['yh'=4,'yl'=2,'x'=4,'core'=2,'z'=8] {'yh'}, dimensions={0}, use_global_device_ids=true | all-gather | bytes 1228800 | tf_op jit(solution)/shard_map/all_gather | solution.py:316
  34.2 14.8 %all_to_all.10.mine_ref = bf16[4,8,64,256]{3,2,1,0:T(8,128)(2,1)S(1)} all-to-all(bf16[4,8,64,256]{3,2,1,0:T(8,128)(2,1)S(1)} %broadcast_in_dim.6), channel_id=1, replica_groups=mesh['yh'=4,'yl'=2,'x'=4,'core'=2,'z'=8] {'x'}, dimensions={0} | all-to-all | bytes 2097152 | tf_op jit(solution)/shard_map/all_to_all | solution.py:309
  50.0 7.4 %collective-permute-start = (bf16[4,8,64,256]{3,2,1,0:T(8,128)(2,1)S(1)}, bf16[4,8,64,256]{3,2,1,0:T(8,128)(2,1)S(1)}, u32[]{:S(2)}, u32[]{:S(2)}) collective-permute-start(bf16[4,8,64,256]{3,2,1,0:T(8,128)(2,1)S(1)} %all_to_all.10.mine_ref), channel_id=1, source_target_pairs={{0,8},{8,0},{1,9},{9,1},{2,10},{10,2},{3,11},{11,3},{4,12},{12,4},... | collective-permute-start | bytes 3145736 | tf_op jit(solution)/shard_map/ppermute | solution.py:321
  57.5 2.2 %collective-permute-done.other_ref = bf16[4,8,64,256]{3,2,1,0:T(8,128)(2,1)S(1)} collective-permute-done((bf16[4,8,64,256]{3,2,1,0:T(8,128)(2,1)S(1)}, bf16[4,8,64,256]{3,2,1,0:T(8,128)(2,1)S(1)}, u32[]{:S(2)}, u32[]{:S(2)}) %collective-permute-start) | collective-permute-done | bytes 1048608 | tf_op jit(solution)/shard_map/ppermute | solution.py:321
  59.7 1.5 copy-done.4
  61.2 2.1 %make_keys.1 = (bf16[192,4096]{1,0:T(8,128)(2,1)S(1)}, bf16[2,192,128]{2,1,0:T(8,128)(2,1)S(1)}, f32[192,128]{1,0:T(8,128)S(1)}) custom-call(s32[2]{0:T(128)S(1)} %pad_add_fusion.place_ref, s32[1]{0:T(128)S(6)} %copy.13.count_ref, bf16[8,208,512]{2,1,0:T(8,128)(2,1)S(1)} %bitcast.17, bf16[4,8,64,256]{3,2,1,0:T(8,128)(2,1)S(1)} %all_to_all.10.mine_ref, ...), custom_call_target="tpu_custom_call" | custom-call | tf_op jit(solution)/shard_map/make_keys/pallas_call | solution.py:96
  63.3 1.2 copy-done.5
  64.4 6.5 %all_gather.44 = bf16[2,384,128]{2,1,0:T(8,128)(2,1)S(1)} all-gather(bf16[1,384,128]{2,1,0:T(8,128)(2,1)S(1)} %bitcast.18), channel_id=1, replica_groups=mesh['yh'=4,'yl'=2,'x'=4,'core'=2,'z'=8] {'yl'}, dimensions={0}, use_global_device_ids=true | all-gather | bytes 294912 | tf_op jit(solution)/shard_map/all_gather | solution.py:315
  71.0 14.7 %all-gather.4 = bf16[8,384,128]{2,1,0:T(8,128)(2,1)S(1)} all-gather(bf16[2,384,128]{2,1,0:T(8,128)(2,1)S(1)} %all_gather.44), channel_id=6, replica_groups=mesh['yh'=4,'yl'=2,'x'=4,'core'=2,'z'=8] {'yh'}, dimensions={0}, use_global_device_ids=true | all-gather | bytes 983040 | tf_op jit(solution)/shard_map/all_gather | solution.py:316
  86.9 27.4 %all_to_all.11.mine_ref = bf16[4,8,192,128]{3,2,1,0:T(8,128)(2,1)S(1)} all-to-all(bf16[4,8,192,128]{3,2,1,0:T(8,128)(2,1)S(1)} %broadcast_in_dim.16), channel_id=1, replica_groups=mesh['yh'=4,'yl'=2,'x'=4,'core'=2,'z'=8] {'x'}, dimensions={0} | all-to-all | bytes 3145728 | tf_op jit(solution)/shard_map/all_to_all | solution.py:309
  114.3 4.4 %collective-permute-start.1 = (bf16[4,8,192,128]{3,2,1,0:T(8,128)(2,1)S(1)}, bf16[4,8,192,128]{3,2,1,0:T(8,128)(2,1)S(1)}, u32[]{:S(2)}, u32[]{:S(2)}) collective-permute-start(bf16[4,8,192,128]{3,2,1,0:T(8,128)(2,1)S(1)} %all_to_all.11.mine_ref), channel_id=1, source_target_pairs={{0,8},{8,0},{1,9},{9,1},{2,10},{10,2},{3,11},{11,3},{4,12},{12,4},... | collective-permute-start | bytes 4718600 | tf_op jit(solution)/shard_map/ppermute | solution.py:321
  118.8 2.5 %copy-done.2 = bf16[64,80,512]{2,1,0:T(8,128)(2,1)S(1)} copy-done((bf16[64,80,512]{2,1,0:T(8,128)(2,1)S(1)}, bf16[64,80,512]{2,1,0:T(8,128)(2,1)}, u32[]{:S(2)}) %copy-start.2) | copy-done | bytes 5242904
  121.3 1.5 copy-done.6
  122.8 2.3 %make_queries.1 = (bf16[192,512]{1,0:T(8,128)(2,1)S(1)}, s32[8,8,128]{2,1,0:T(8,128)S(1)}) custom-call(bf16[192,4096]{1,0:T(8,128)(2,1)S(1)} %copy-done.6, bf16[8,8,80,512]{3,2,1,0:T(8,128)(2,1)S(1)} %bitcast.15, f32[1,128]{1,0:T(1,128)S(1)} %bitcast.24), custom_call_target="tpu_custom_call" | custom-call | tf_op jit(solution)/shard_map/make_queries/pallas_call | solution.py:138
  125.1 7.3 %scores.1 = (bf16[4,192,5120]{2,1,0:T(8,128)(2,1)S(1)}, f32[4,192,256]{2,1,0:T(8,128)S(1)}) custom-call(s32[2]{0:T(128)S(1)} %pad_add_fusion.place_ref, s32[8,8,128]{2,1,0:T(8,128)S(1)} %get-tuple-element.17.counts_ref, s32[1]{0:T(128)S(6)} %copy.13.count_ref, bf16[192,512]{1,0:T(8,128)(2,1)S(1)} %get-tuple-element.18.q_ref, ...), custom_call_target="tpu_custom_call" | custom-call | tf_op jit(solution)/shard_map/scores/pallas_call | solution.py:227
  132.4 3.1 %copy-done = bf16[4,192,5120]{2,1,0:T(8,128)(2,1)} copy-done((bf16[4,192,5120]{2,1,0:T(8,128)(2,1)}, bf16[4,192,5120]{2,1,0:T(8,128)(2,1)S(1)}, u32[]{:S(2)}) %copy-start) | copy-done | bytes 7864344
  136.3 4.9 %all-gather.14.cloned.1.call-done = bf16[64,1,192,128]{3,2,1,0:T(8,128)(2,1)} async-done(((bf16[8,1,192,128]{3,2,1,0:T(8,128)(2,1)}), bf16[64,1,192,128]{3,2,1,0:T(8,128)(2,1)}) %all-gather.14.cloned.1.call-update) | async-done | bytes 3145744 | tf_op jit(solution)/shard_map/all_gather | solution.py:348
  141.3 3.2 %copy-done.1 = bf16[4,192,5120]{2,1,0:T(8,128)(2,1)S(1)} copy-done((bf16[4,192,5120]{2,1,0:T(8,128)(2,1)S(1)}, bf16[4,192,5120]{2,1,0:T(8,128)(2,1)}, u32[]{:S(2)}) %copy-start.1) | copy-done | bytes 7864344
  144.5 1.9 %copy-done.3 = bf16[64,1,192,128]{3,2,1,0:T(8,128)(2,1)S(1)} copy-done((bf16[64,1,192,128]{3,2,1,0:T(8,128)(2,1)S(1)}, bf16[64,1,192,128]{3,2,1,0:T(8,128)(2,1)}, u32[]{:S(2)}) %copy-start.3) | copy-done | bytes 3145752
  146.4 1.1 copy-done.8
  147.5 8.7 %attend.1 = bf16[512,512]{1,0:T(8,128)(2,1)} custom-call(s32[2]{0:T(128)S(1)} %pad_add_fusion.place_ref, s32[8,8,128]{2,1,0:T(8,128)S(1)} %get-tuple-element.17.counts_ref, s32[1]{0:T(128)S(6)} %copy.13.count_ref, bf16[4,192,5120]{2,1,0:T(8,128)(2,1)S(1)} %copy-done.1, f32[4,192,256]{2,1,0:T(8,128)S(1)} %copy-done.8, ...), custom_call_target="tpu_custom_call" | custom-call | tf_op jit(solution)/shard_map/attend/pallas_call | solution.py:290
  (40 shorter events, 6.4 us)
Async XLA Ops:
  6.5 53.2 %all-gather.10.cloned.1.call-start = ((), (), s32[]{:S(2)}) async-start(), calls=%async_computation.2 | async-start | bytes 1916928 | tf_op jit(solution)/shard_map/all_gather | solution.py:335
  6.5 1.0 copy-start.9
  7.6 0.7 copy-start.10
  8.3 0.7 copy-start.12
  8.9 0.7 copy-start.13
  10.6 108.2 %all-gather.12.cloned.1.call-start = ((), (), s32[]{:S(2)}) async-start(), calls=%async_computation.3 | async-start | bytes 5898240 | tf_op jit(solution)/shard_map/all_gather | solution.py:343
  34.2 25.5 %copy-start.14 = (f32[128]{0:T(128)S(1)}, f32[128]{0:T(128)}, u32[]{:S(2)}) copy-start(f32[128]{0:T(128)} %param.17) | copy-start | bytes 1540
  49.9 91.3 %all-gather.14.cloned.1.call-start = ((), (), s32[]{:S(2)}) async-start(), calls=%async_computation.4 | async-start | bytes 3538944 | tf_op jit(solution)/shard_map/all_gather | solution.py:348
  50.0 9.7 %collective-permute-start = (bf16[4,8,64,256]{3,2,1,0:T(8,128)(2,1)S(1)}, bf16[4,8,64,256]{3,2,1,0:T(8,128)(2,1)S(1)}, u32[]{:S(2)}, u32[]{:S(2)}) collective-permute-start(bf16[4,8,64,256]{3,2,1,0:T(8,128)(2,1)S(1)} %all_to_all.10.mine_ref), channel_id=1, source_target_pairs={{0,8},{8,0},{1,9},{9,1},{2,10},{10,2},{3,11},{11,3},{4,12},{12,4},... | collective-permute-start | bytes 3145736 | tf_op jit(solution)/shard_map/ppermute | solution.py:321
  59.7 1.5 copy-start.4
  63.3 1.2 copy-start.5
  86.8 31.8 %copy-start.11 = (s32[192]{0:T(256)S(1)}, s32[192]{0:T(256)}, u32[]{:S(2)}) copy-start(s32[192]{0:T(256)} %param.18) | copy-start | bytes 2308
  86.8 32.0 %copy-start.15 = (f32[128]{0:T(128)S(1)}, f32[128]{0:T(128)}, u32[]{:S(2)}) copy-start(f32[128]{0:T(128)} %param.16) | copy-start | bytes 1540
  114.3 10.8 %collective-permute-start.1 = (bf16[4,8,192,128]{3,2,1,0:T(8,128)(2,1)S(1)}, bf16[4,8,192,128]{3,2,1,0:T(8,128)(2,1)S(1)}, u32[]{:S(2)}, u32[]{:S(2)}) collective-permute-start(bf16[4,8,192,128]{3,2,1,0:T(8,128)(2,1)S(1)} %all_to_all.11.mine_ref), channel_id=1, source_target_pairs={{0,8},{8,0},{1,9},{9,1},{2,10},{10,2},{3,11},{11,3},{4,12},{12,4},... | collective-permute-start | bytes 4718600 | tf_op jit(solution)/shard_map/ppermute | solution.py:321
  118.8 2.5 %copy-start.2 = (bf16[64,80,512]{2,1,0:T(8,128)(2,1)S(1)}, bf16[64,80,512]{2,1,0:T(8,128)(2,1)}, u32[]{:S(2)}) copy-start(bf16[64,80,512]{2,1,0:T(8,128)(2,1)} %all-gather.12.cloned.1.call-done) | copy-start | bytes 15728644
  121.3 1.5 copy-start.6
  132.4 3.1 %copy-start = (bf16[4,192,5120]{2,1,0:T(8,128)(2,1)}, bf16[4,192,5120]{2,1,0:T(8,128)(2,1)S(1)}, u32[]{:S(2)}) copy-start(bf16[4,192,5120]{2,1,0:T(8,128)(2,1)S(1)} %get-tuple-element.20.weights_ref) | copy-start | bytes 23592964
  135.5 0.9 copy-start.7
  141.3 3.2 %copy-start.1 = (bf16[4,192,5120]{2,1,0:T(8,128)(2,1)S(1)}, bf16[4,192,5120]{2,1,0:T(8,128)(2,1)}, u32[]{:S(2)}) copy-start(bf16[4,192,5120]{2,1,0:T(8,128)(2,1)} %copy-done) | copy-start | bytes 23592964
  144.5 1.9 %copy-start.3 = (bf16[64,1,192,128]{3,2,1,0:T(8,128)(2,1)S(1)}, bf16[64,1,192,128]{3,2,1,0:T(8,128)(2,1)}, u32[]{:S(2)}) copy-start(bf16[64,1,192,128]{3,2,1,0:T(8,128)(2,1)} %all-gather.14.cloned.1.call-done) | copy-start | bytes 9437188
  146.4 1.1 copy-start.8
Sparse Core Ops, SparseCore 0:
  10.7 43.8 all-gather.9
  56.8 52.5 all-gather.11
  111.5 29.7 all-gather.13

commit v4 on v1

v4 whole, which is shorter than its diff:
```python
import math

import jax
import jax.numpy as jnp
from jax import lax
from jax.experimental import pallas as pl
from jax.experimental.pallas import tpu as pltpu
from jax.sharding import Mesh
from jax.sharding import PartitionSpec as P

SEQ = ("y", "x", "core")
TILE = 1024
HALF = 512


def whole(memory_space=pltpu.VMEM):
    return pl.BlockSpec(memory_space=memory_space)


def params(mebibytes=56):
    return pltpu.CompilerParams(vmem_limit_bytes=mebibytes * 1024 * 1024)


def dot(a, b, contract_a=1, contract_b=0):
    return lax.dot_general(
        a, b, (((contract_a,), (contract_b,)), ((), ())), preferred_element_type=jnp.float32
    )


def stage_kernel(
    count_ref, tokens_ref, pos_ref, gain_ref, router_ref, query_ref, key_ref, value_ref, rows_ref, weights_ref
):
    slots = pos_ref.shape[1]
    block, width = tokens_ref.shape
    hit = lax.broadcasted_iota(jnp.int32, (block, slots), 0) == pos_ref[...]
    one_hot = jnp.where(hit, 1.0, 0.0).astype(jnp.bfloat16)
    rows_ref[:slots, :] = dot(one_hot, tokens_ref[...], 0, 0).astype(jnp.bfloat16)
    at = lax.broadcasted_iota(jnp.int32, (rows_ref.shape[0] - slots, width), 0)
    extra = jnp.where(at == 0, gain_ref[...].astype(jnp.float32).reshape(1, width), 0.0)
    extra = jnp.where(at == 1, router_ref[...].astype(jnp.float32).reshape(1, width), extra)
    rows_ref[slots:, :] = extra.astype(jnp.bfloat16)
    deep, query = query_ref.shape
    key = key_ref.shape[1]
    weights_ref[:deep, :query] = query_ref[...]
    weights_ref[:deep, query : query + key] = key_ref[...]
    weights_ref[:deep, query + key :] = value_ref[...]
    count = jnp.full((weights_ref.shape[0] - deep, weights_ref.shape[1]), count_ref[0], jnp.int32)
    weights_ref[deep:, :] = count.astype(jnp.float32).astype(jnp.bfloat16)


def stage(count, tokens, route_pos, x_gain, w_router, w_query, key_weight, value_weight):
    slots = route_pos.shape[0]
    width = tokens.shape[1]
    deep = w_query.shape[0]
    across = w_query.shape[1] + key_weight.shape[1] + value_weight.shape[1]
    return pl.pallas_call(
        stage_kernel,
        out_shape=(
            jax.ShapeDtypeStruct((slots + 16, width), jnp.bfloat16),
            jax.ShapeDtypeStruct((deep + 8, across), jnp.bfloat16),
        ),
        in_specs=[whole(pltpu.SMEM)] + [whole()] * 7,
        out_specs=(whole(), whole()),
        compiler_params=params(),
        name="stage",
    )(count, tokens, route_pos.reshape(1, slots), x_gain, w_router, w_query, key_weight, value_weight)


def head_norm(projected, gain):
    mean_sq = jnp.mean(projected * projected, axis=-1, keepdims=True)
    return (projected * lax.rsqrt(mean_sq + 1e-06) * gain).astype(jnp.bfloat16)


def in_feature_order(core, mine, other):
    even = jnp.where(core == 0, mine, other)
    odd = jnp.where(core == 0, other, mine)
    return jnp.stack([even, odd], axis=1).reshape(-1, mine.shape[-1])


def norm_scale(rows_ref, slots):
    parts, _, width = rows_ref.shape
    square = jnp.zeros((slots, width), jnp.float32)
    for part in range(parts):
        wide = rows_ref[part, :slots, :].astype(jnp.float32)
        square += wide * wide
    mean_sq = jnp.sum(square, axis=-1, keepdims=True) / (parts * width)
    return lax.rsqrt(mean_sq + 1e-05)


def normed_part(rows_ref, part, slots, scale):
    extra = rows_ref[part, slots:, :].astype(jnp.float32)
    wide = rows_ref[part, :slots, :].astype(jnp.float32)
    return (wide * scale * extra[0:1]).astype(jnp.bfloat16), extra[1:2]


def keys_kernel(place_ref, count_ref, rows_ref, mine_ref, other_ref, gain_ref, kv_ref, counts_ref):
    slots, head = kv_ref.shape[1:]
    nx, parts, _, both = mine_ref.shape
    deep = rows_ref.shape[2] // (2 * nx)
    core, count = place_ref[0], count_ref[0]
    scale = norm_scale(rows_ref, slots)
    total = jnp.zeros((slots, both), jnp.float32)
    for part in range(parts):
        block, _ = normed_part(rows_ref, part, slots, scale)
        weights = in_feature_order(core, mine_ref[:, part, :deep], other_ref[:, part, :deep])
        total += dot(block, weights)
    kv_ref[0] = head_norm(total[:, :head], gain_ref[...])
    live = lax.broadcasted_iota(jnp.int32, (slots, head), 0) < count
    kv_ref[1] = jnp.where(live, total[:, head:], 0.0).astype(jnp.bfloat16)
    for which, ref in enumerate((mine_ref, other_ref)):
        for x in range(nx):
            counts = jnp.max(ref[x, :, deep:, :head].astype(jnp.float32), axis=1)
            counts_ref[which, x] = counts.astype(jnp.int32)


def make_keys(place, count, rows, mine, other, gain, slots):
    nx, ny = mine.shape[:2]
    head = gain.shape[0]
    return pl.pallas_call(
        keys_kernel,
        out_shape=(
            jax.ShapeDtypeStruct((2, slots, head), jnp.bfloat16),
            jax.ShapeDtypeStruct((2, nx, ny, head), jnp.int32),
        ),
        in_specs=[whole(pltpu.SMEM)] * 2 + [whole()] * 4,
        out_specs=(whole(), whole()),
        compiler_params=params(16),
        name="make_keys",
    )(place, count, rows, mine, other, gain.reshape(1, head))


def queries_kernel(
    place_ref, rows_hbm, mine_hbm, other_hbm, gain_ref, out_ref, gate_ref, rows, weights, rows_here, weights_here
):
    parts, nx, _, deep, width = weights.shape
    slots, head = gate_ref.shape
    core = place_ref[0]
    rows_copies, weights_copies = [], []
    for part in range(parts):
        rows_copies.append(pltpu.make_async_copy(rows_hbm.at[part], rows.at[part], rows_here.at[part]))
        rows_copies[part].start()
    for part in range(parts):
        weights_copies.append(
            [
                pltpu.make_async_copy(source.at[:, part], weights.at[part, :, side], weights_here.at[which, part])
                for which, (source, side) in enumerate(((mine_hbm, core), (other_hbm, 1 - core)))
            ]
        )
        for copy in weights_copies[part]:
            copy.start()
    for copy in rows_copies:
        copy.wait()
    scale = norm_scale(rows, slots)
    routed = jnp.zeros((slots, rows.shape[2]), jnp.float32)
    total = jnp.zeros((slots, width), jnp.float32)
    for part in range(parts):
        block, router = normed_part(rows, part, slots, scale)
        routed += block.astype(jnp.float32) * router
        for copy in weights_copies[part]:
            copy.wait()
        total += dot(block, weights[part].reshape(nx * 2 * deep, width))
    gate = jax.nn.sigmoid(jnp.sum(routed, axis=-1, keepdims=True))
    gate_ref[...] = jnp.broadcast_to(gate, gate_ref.shape)
    for h in range(0, width, head):
        out_ref[:, h : h + head] = head_norm(total[:, h : h + head], gain_ref[...])


def make_queries(place, rows, mine, other, gain, slots):
    nx, parts, deep, width = mine.shape
    head = gain.shape[0]
    return pl.pallas_call(
        queries_kernel,
        out_shape=(
            jax.ShapeDtypeStruct((slots, width), jnp.bfloat16),
            jax.ShapeDtypeStruct((slots, head), jnp.float32),
        ),
        in_specs=[whole(pltpu.SMEM)] + [whole(pl.ANY)] * 3 + [whole()],
        out_specs=(whole(), whole()),
        scratch_shapes=[
            pltpu.VMEM(rows.shape, jnp.bfloat16),
            pltpu.VMEM((parts, nx, 2, deep, width), jnp.bfloat16),
            pltpu.SemaphoreType.DMA((parts,)),
            pltpu.SemaphoreType.DMA((2, parts)),
        ],
        compiler_params=params(),
        name="make_queries",
    )(place, rows, mine, other, gain.reshape(1, -1))


def pack_kernel(
    place_ref, counts_ref, count_ref, mine_hbm, other_hbm, _, keys_ref, flags, table_ref, mine_ref, other_ref, here
):
    nx, ny, slots, head = mine_ref.shape
    copies = [
        [
            pltpu.make_async_copy(source.at[x], target.at[x], here.at[which, x])
            for which, (source, target) in enumerate(((mine_hbm, mine_ref), (other_hbm, other_ref)))
        ]
        for x in range(nx)
    ]
    for pair in copies:
        for copy in pair:
            copy.start()
    core, shard = place_ref[0], place_ref[1]
    fill = lax.broadcasted_iota(jnp.int32, (slots, head), 0)

    end = jnp.int32(0)
    for x in range(nx):
        for copy in copies[x]:
            copy.wait()
        for y in range(ny):
            for which, ref in enumerate((mine_ref, other_ref)):
                side = jnp.where(core == 0, which, 1 - which)
                earlier = (y * nx + x) * 2 + side < shard
                length = jnp.where(earlier, counts_ref[which, x, y, 0], 0)
                table_ref[which, x * ny + y] = jnp.where(length > 0, end, -1)

                @pl.when(length > 0)
                def _():
                    where = pl.ds(pl.multiple_of(end, 16), slots)
                    keys_ref[where, :] = ref[x, y]
                    flags[where, :] = jnp.where(fill < length, 1.0, 0.0).astype(jnp.bfloat16)

                end = end + (length + 15) // 16 * 16
        table_ref[2, 3 + x] = end
    table_ref[2, 0] = end
    table_ref[2, 1] = core
    table_ref[2, 2] = count_ref[0]
    rest = pl.ds(pl.multiple_of(end, 16), TILE)
    keys_ref[rest, :] = jnp.zeros((TILE, head), jnp.bfloat16)
    flags[rest, :] = jnp.zeros((TILE, head), jnp.bfloat16)


def packed_rows(sources, block):
    return -(-(sources * block // 8 + 16 * sources) // TILE) * TILE


def pack_keys(place, counts, count, mine, other, after, block):
    nx, ny, _, head = mine.shape
    rows = packed_rows(2 * nx * ny, block)
    return pl.pallas_call(
        pack_kernel,
        out_shape=(
            jax.ShapeDtypeStruct((rows + TILE, head), jnp.bfloat16),
            jax.ShapeDtypeStruct((rows + TILE, head), jnp.bfloat16),
            jax.ShapeDtypeStruct((3, nx * ny), jnp.int32),
        ),
        in_specs=[whole(pltpu.SMEM)] * 3 + [whole(pl.ANY)] * 3,
        out_specs=(whole(), whole(), whole(pltpu.SMEM)),
        scratch_shapes=[
            pltpu.VMEM(mine.shape, jnp.bfloat16),
            pltpu.VMEM(other.shape, jnp.bfloat16),
            pltpu.SemaphoreType.DMA((2, nx)),
        ],
        compiler_params=params(),
        name="pack_keys",
    )(place, counts, count, mine, other, after)


def attend_kernel(
    table_ref, q_ref, own_ref, pos_row_ref, gate_ref, keys_hbm, flags_hbm, values_hbm,
    out_ref, keys_ref, values, packed, total, arrived, chunks,
):
    nx, _, ny, slots, head = values.shape
    group = q_ref.shape[1] // head
    end, core, count = table_ref[2, 0], table_ref[2, 1], table_ref[2, 2]
    factor = math.log2(math.e) / math.sqrt(head)
    copies = [pltpu.make_async_copy(values_hbm.at[x], values.at[x], arrived.at[x]) for x in range(nx)]
    halves = (end + HALF - 1) // HALF

    def chunk(at):
        rows = pl.ds(pl.multiple_of(at * TILE, TILE), TILE)
        return (
            pltpu.make_async_copy(keys_hbm.at[rows, :], keys_ref.at[rows, :], chunks.at[0, at]),
            pltpu.make_async_copy(flags_hbm.at[rows, :], packed.at[rows, head:], chunks.at[1, at]),
        )

    def begin(at, carry):
        for copy in chunk(at):
            copy.start()
        return carry

    copies[0].start()
    lax.fori_loop(0, (halves + 1) // 2, begin, 0)
    for copy in copies[1:]:
        copy.start()

    across = lax.broadcasted_iota(jnp.int32, (slots, slots), 1)
    along = lax.broadcasted_iota(jnp.int32, (slots, slots), 0)
    positions = jnp.broadcast_to(pos_row_ref[...].astype(jnp.float32), (slots, slots))
    mine = jnp.sum(jnp.where(across == along, positions, 0.0), axis=1, keepdims=True)
    allowed = (positions <= mine) & (across < count)
    summed = jnp.concatenate([own_ref[1], jnp.ones((slots, head), jnp.bfloat16)], axis=1)
    for h in range(group):
        query = q_ref[:, h * head : (h + 1) * head]
        weights = jnp.exp2(dot(query, own_ref[0], 1, 1) * factor)
        total[h] = dot(jnp.where(allowed, weights, 0.0).astype(jnp.bfloat16), summed)

    def weigh(start, size):
        rows = pl.ds(pl.multiple_of(start, size), size)
        keys, vals = keys_ref[rows, :], packed[rows, :]
        for h in range(group):
            query = q_ref[:, h * head : (h + 1) * head]
            weights = jnp.exp2(dot(query, keys, 1, 1) * factor).astype(jnp.bfloat16)
            total[h] += dot(weights, vals)

    def tile(at, carry):
        for copy in chunk(at):
            copy.wait()
        weigh(at * TILE, TILE)
        return carry

    done = jnp.int32(0)
    for x in range(nx):
        copies[x].wait()
        for y in range(ny):
            for which in range(2):
                offset = table_ref[which, x * ny + y]

                @pl.when(offset >= 0)
                def _():
                    side = jnp.where(core == 0, which, 1 - which)
                    packed[pl.ds(pl.multiple_of(offset, 16), slots), :head] = values[x, side, y]

        if x == nx - 1:
            packed[pl.ds(pl.multiple_of(end, 16), TILE), :head] = jnp.zeros((TILE, head), jnp.bfloat16)
        ready = halves // 2 if x == nx - 1 else table_ref[2, 3 + x] // TILE
        lax.fori_loop(done, ready, tile, 0)
        done = ready

    @pl.when(halves % 2 == 1)
    def _():
        for copy in chunk(done):
            copy.wait()
        weigh(done * TILE, HALF)

    block = out_ref.shape[0]
    live = lax.broadcasted_iota(jnp.int32, (slots, 1), 0) < count
    pieces = []
    for h in range(group):
        sums = total[h]
        scale = jnp.where(live, gate_ref[...] / jnp.where(live, sums[:, head:], 1.0), 0.0)
        pieces.append((sums[:, :head] * scale).astype(jnp.bfloat16))
    hit = (lax.broadcasted_iota(jnp.int32, (block, slots), 0) == pos_row_ref[...]) & (
        lax.broadcasted_iota(jnp.int32, (block, slots), 1) < count
    )
    one_hot = jnp.where(hit, 1.0, 0.0).astype(jnp.bfloat16)
    out_ref[...] = dot(one_hot, jnp.concatenate(pieces, axis=1)).astype(jnp.bfloat16)


def attend(table, queries, own, keys, flags, route_pos, gate, values, block):
    slots, width = queries.shape
    head = gate.shape[1]
    group = width // head
    return pl.pallas_call(
        attend_kernel,
        out_shape=jax.ShapeDtypeStruct((block, width), jnp.bfloat16),
        in_specs=[whole(pltpu.SMEM)] + [whole()] * 4 + [whole(pltpu.HBM)] * 3,
        out_specs=whole(),
        scratch_shapes=[
            pltpu.VMEM(keys.shape, jnp.bfloat16),
            pltpu.VMEM(values.shape, jnp.bfloat16),
            pltpu.VMEM((keys.shape[0], 2 * head), jnp.bfloat16),
            pltpu.VMEM((group, slots, 2 * head), jnp.float32),
            pltpu.SemaphoreType.DMA((values.shape[0],)),
            pltpu.SemaphoreType.DMA((2, keys.shape[0] // TILE)),
        ],
        compiler_params=params(),
        name="attend",
    )(table, queries, own, route_pos.reshape(1, slots), gate, keys, flags, values)


def to_all(block, axes, peers):
    return lax.all_to_all(
        jnp.broadcast_to(block[None], (peers,) + block.shape), axes, 0, 0, tiled=True
    )


def swap_cores(block):
    return lax.ppermute(block, "core", [(0, 1), (1, 0)])


def local(
    tokens, x_gain, w_router, w_query, key_weight, value_weight, q_gain, key_norm_gain, route_pos, route_count
):
    ny, nx = lax.axis_size("y"), lax.axis_size("x")
    block = tokens.shape[0]
    slots = route_pos.shape[0]
    place = jnp.stack([lax.axis_index("core"), lax.axis_index(SEQ)]).astype(jnp.int32)
    deep, width = w_query.shape
    head = q_gain.shape[0]

    picked, weights = stage(
        route_count, tokens, route_pos, x_gain, w_router, w_query, key_weight, value_weight
    )
    rows = lax.all_gather(picked, "z", axis=0, tiled=False)

    weights_y = lax.all_gather(weights, "y", axis=0, tiled=False)
    kv_mine = to_all(weights_y[:, :, width:], "x", nx)
    kv_other = swap_cores(kv_mine)
    wq_mine = lax.all_gather(weights_y[:, :deep, :width], "x", axis=0, tiled=False)
    wq_other = swap_cores(wq_mine)

    own, counts = make_keys(place, route_count, rows, kv_mine, kv_other, key_norm_gain, slots)

    own_y = lax.all_gather(own.reshape(2 * slots, head), "y", axis=0, tiled=False)
    own_y = own_y.reshape(ny, 2, slots, head)
    values = lax.all_gather(own_y[:, 1], ("x", "core"), axis=0, tiled=False).reshape(nx, 2, ny, slots, head)
    mine = to_all(own_y[:, 0], "x", nx)
    other = swap_cores(mine)

    queries, gate = make_queries(place, rows, wq_mine, wq_other, q_gain, slots)
    keys, flags, table = pack_keys(place, counts, route_count, mine, other, queries, block)
    return attend(table, queries, own, keys, flags, route_pos, gate, values, block)


def solution(mesh):
    grid = Mesh(mesh.devices.reshape(8, 4, 2, 8), SEQ + ("z",))
    return jax.shard_map(
        local,
        mesh=grid,
        in_specs=(
            P(SEQ, "z"), P("z"), P("z"), P(SEQ, "z"), P(SEQ, "z"), P(SEQ, "z"), P(), P(), P(SEQ), P(SEQ),
        ),
        out_specs=P(SEQ, "z"),
        check_vma=False,
    )
```

time: 175 us -> 146 us (0.83)
  blocking collectives: 83.4 us -> 57.3 us
  other arithmetic: 3.46 us -> 0.08 us
  starting transfers between devices: 26 us -> 23.9 us
    all_to_all x2 -> x1, blocking collectives: 62.3 us -> 14.2 us  [to_all(): lax.all_to_all(jnp.broadcast_to(block[None], (peers,) + block.shape), axe...]
    all_gather x1 -> x2, blocking collectives: 21.2 us -> 43.2 us  [the longest x1 22.2 us: local(): lax.all_gather(own.reshape(2 * slots, head), 'y', axis=0, tiled=False)]
    all_to_all x0 -> x1, waiting for transfers between devices: none -> 9.71 us  [to_all(): lax.all_to_all(jnp.broadcast_to(block[None], (peers,) + block.shape), axe...]
    all_gather x1 -> x2, waiting for transfers between devices: 13.3 us -> 6.24 us  [the longest x1 3.68 us: local(): lax.all_gather(weights_y[:, :deep, :width], 'x', axis=0, tiled=False)]
    ppermute x2 -> x3, starting transfers between devices: 25.9 us -> 20.2 us  [swap_cores(): return lax.ppermute(block, 'core', [(0, 1), (1, 0)])]
    pallas_call x3 -> x4, Pallas kernels: 11.5 us -> 15.8 us  [the longest x1 6.52 us: make_queries(): pl.pallas_call(queries_kernel, out_shape=(jax.ShapeDtypeStruct((slots, wi...]
    all_to_all x0 -> x1, starting transfers between devices: none -> 3.57 us  [to_all(): lax.all_to_all(jnp.broadcast_to(block[None], (peers,) + block.shape), axe...]
    all_gather x1, waiting for transfers between devices: 3.47 us -> 0.01 us  [local(): rows = lax.all_gather(picked, 'z', axis=0, tiled=False)]
  transfers between devices with their start and end apart: 4 -> 7, of which waited for: 2 -> 4; matrix products, arithmetic and copies ran while one was open for 4% -> 2% of each run, Pallas kernels for 5% -> 9%
where the time goes in v4:
time: 146 us
  blocking collectives  57.3 us (39%)
  Pallas kernels  25.5 us (17%)
  starting transfers between devices  23.9 us (16%)
  waiting for transfers between devices  18.4 us (13%)
  between operations  13.9 us (10%)
  local copies, waits for them, and re-layouts  6.52 us (4%)
    all_gather x1, blocking collectives, local(): lax.all_gather(own.reshape(2 * slots, head), 'y', axis=0, tiled=False)  22.2 us
    all_gather x1, blocking collectives, local(): weights_y = lax.all_gather(weights, 'y', axis=0, tiled=False)  20.9 us
    ppermute x3, starting transfers between devices, swap_cores(): return lax.ppermute(block, 'core', [(0, 1), (1, 0)])  20.2 us
    all_to_all x1, blocking collectives, to_all(): lax.all_to_all(jnp.broadcast_to(block[None], (peers,) + block.shape), axe...  14.2 us
    all_to_all x1, waiting for transfers between devices, to_all(): lax.all_to_all(jnp.broadcast_to(block[None], (peers,) + block.shape), axe...  9.71 us
    pallas_call x1, Pallas kernels, attend(): pl.pallas_call(attend_kernel, out_shape=jax.ShapeDtypeStruct((block, widt...  9.64 us
    pallas_call x1, Pallas kernels, make_queries(): pl.pallas_call(queries_kernel, out_shape=(jax.ShapeDtypeStruct((slots, wi...  6.52 us
    pallas_call x1, Pallas kernels, pack_keys(): pl.pallas_call(pack_kernel, out_shape=(jax.ShapeDtypeStruct((rows + TILE,...  5.6 us
  transfers between devices with their start and end apart: 7, of which 4 were waited for; matrix products, arithmetic and copies ran while one was open for 2% of the time, Pallas kernels for 9%

profile of v4, /device:TPU:57, one launch (start us, length us, event | category | flops | bytes accessed | tf_op | source)
XLA Modules:
  0.0 145.6 jit_solution(2237438365549390077)
XLA Ops:
  7.2 2.1 %stage.1 = (bf16[208,512]{1,0:T(8,128)(2,1)}, bf16[72,768]{1,0:T(8,128)(2,1)}) custom-call(s32[1]{0:T(128)S(6)} %copy.11.count_ref, bf16[512,512]{1,0:T(8,128)(2,1)} %tokens_ref.1, s32[1,192]{1,0:T(1,128)} %bitcast.23, bf16[512]{0:T(512)(128)(2,1)} %gain_ref.1, bf16[512]{0:T(512)(128)(2,1)} %router_ref.1, bf16[64,512]{1,0:T(8,128)(2,1)} %query_ref.1, ...), custom_call_target="tpu_custom_call" | custom-call | tf_op jit(solution)/shard_map/stage/pallas_call | solution.py:56
  9.3 20.9 %all-gather.1 = bf16[576,768]{1,0:T(8,128)(2,1)S(1)} all-gather(bf16[72,768]{1,0:T(8,128)(2,1)} %get-tuple-element.15), channel_id=3, replica_groups=mesh['y'=8,'x'=4,'core'=2,'z'=8] {'y'}, dimensions={0}, use_global_device_ids=true | all-gather | bytes 995328 | tf_op jit(solution)/shard_map/all_gather | solution.py:398
  30.3 0.8 slice.18
  31.2 0.1 broadcast_in_dim.6
  31.3 14.2 %all_to_all.10.mine_ref = bf16[4,8,72,256]{3,2,1,0:T(8,128)(2,1)S(1)} all-to-all(bf16[4,8,72,256]{3,2,1,0:T(8,128)(2,1)S(1)} %broadcast_in_dim.6), channel_id=1, replica_groups=mesh['y'=8,'x'=4,'core'=2,'z'=8] {'x'}, dimensions={0} | all-to-all | bytes 2359296 | tf_op jit(solution)/shard_map/all_to_all | solution.py:374
  45.5 10.1 %collective-permute-start = (bf16[4,8,72,256]{3,2,1,0:T(8,128)(2,1)S(1)}, bf16[4,8,72,256]{3,2,1,0:T(8,128)(2,1)S(1)}, u32[]{:S(2)}, u32[]{:S(2)}) collective-permute-start(bf16[4,8,72,256]{3,2,1,0:T(8,128)(2,1)S(1)} %all_to_all.10.mine_ref), channel_id=1, source_target_pairs={{0,8},{8,0},{1,9},{9,1},{2,10},{10,2},{3,11},{11,3},{4,12},{12,4},... | collective-permute-start | bytes 3538952 | tf_op jit(solution)/shard_map/ppermute | solution.py:380
  55.6 0.1 pad_add_fusion.place_ref
  55.7 2.4 %collective-permute-done.other_ref = bf16[4,8,72,256]{3,2,1,0:T(8,128)(2,1)S(1)} collective-permute-done((bf16[4,8,72,256]{3,2,1,0:T(8,128)(2,1)S(1)}, bf16[4,8,72,256]{3,2,1,0:T(8,128)(2,1)S(1)}, u32[]{:S(2)}, u32[]{:S(2)}) %collective-permute-start) | collective-permute-done | bytes 1179680 | tf_op jit(solution)/shard_map/ppermute | solution.py:380
  58.1 1.5 copy-done
  59.5 1.6 %make_keys.1 = (bf16[2,192,128]{2,1,0:T(8,128)(2,1)S(1)}, s32[2,4,8,128]{3,2,1,0:T(8,128)S(1)}) custom-call(s32[2]{0:T(128)S(1)} %pad_add_fusion.place_ref, s32[1]{0:T(128)S(6)} %copy.11.count_ref, bf16[8,208,512]{2,1,0:T(8,128)(2,1)S(1)} %bitcast.14, bf16[4,8,72,256]{3,2,1,0:T(8,128)(2,1)S(1)} %all_to_all.10.mine_ref, ...), custom_call_target="tpu_custom_call" | custom-call | tf_op jit(solution)/shard_map/make_keys/pallas_call | solution.py:119
  61.2 0.6 copy-done.2
  61.8 22.2 %all_gather.28 = bf16[8,384,128]{2,1,0:T(8,128)(2,1)S(1)} all-gather(bf16[1,384,128]{2,1,0:T(8,128)(2,1)S(1)} %bitcast.15), channel_id=1, replica_groups=mesh['y'=8,'x'=4,'core'=2,'z'=8] {'y'}, dimensions={0}, use_global_device_ids=true | all-gather | bytes 884736 | tf_op jit(solution)/shard_map/all_gather | solution.py:406
  84.0 0.8 fusion
  84.8 1.6 %broadcast_in_dim.15 = bf16[4,8,192,128]{3,2,1,0:T(8,128)(2,1)} broadcast(bf16[8,192,128]{2,1,0:T(8,128)(2,1)S(1)} %get-tuple-element.24), dimensions={1,2,3} | broadcast | bytes 1966080 | tf_op jit(solution)/shard_map/broadcast_in_dim | solution.py:375
  86.4 3.6 %all-to-all-start.1 = ((bf16[4,8,192,128]{3,2,1,0:T(8,128)(2,1)}), bf16[4,8,192,128]{3,2,1,0:T(8,128)(2,1)S(1)}, u32[]{:S(2)}, u32[]{:S(2)}) async-start(bf16[4,8,192,128]{3,2,1,0:T(8,128)(2,1)} %broadcast_in_dim.15), calls=%async_computation.1 | async-start | bytes 3145728 | tf_op jit(solution)/shard_map/all_to_all | solution.py:374
  90.0 3.7 %all-gather.10.cloned.1.call-done = bf16[32,64,512]{2,1,0:T(8,128)(2,1)} async-done(((bf16[8,64,512]{2,1,0:T(8,128)(2,1)}), bf16[32,64,512]{2,1,0:T(8,128)(2,1)}) %all-gather.10.cloned.1.call-update) | async-done | bytes 2097168 | tf_op jit(solution)/shard_map/all_gather | solution.py:401
  93.6 2.6 %collective-permute-start.2 = (bf16[4,8,64,512]{3,2,1,0:T(8,128)(2,1)}, bf16[4,8,64,512]{3,2,1,0:T(8,128)(2,1)}, u32[]{:S(2)}, u32[]{:S(2)}) collective-permute-start(bf16[4,8,64,512]{3,2,1,0:T(8,128)(2,1)} %bitcast.21), channel_id=1, source_target_pairs={{0,8},{8,0},{1,9},{9,1},{2,10},{10,2},{3,11},{11,3},{4,12},{12,4},... | collective-permute-start | bytes 6291464 | tf_op jit(solution)/shard_map/ppermute | solution.py:380
  96.2 9.7 %all-to-all-done.1.mine_hbm = bf16[4,8,192,128]{3,2,1,0:T(8,128)(2,1)S(1)} async-done(((bf16[4,8,192,128]{3,2,1,0:T(8,128)(2,1)}), bf16[4,8,192,128]{3,2,1,0:T(8,128)(2,1)S(1)}, u32[]{:S(2)}, u32[]{:S(2)}) %all-to-all-start.1) | async-done | bytes 1572896 | tf_op jit(solution)/shard_map/all_to_all | solution.py:374
  106.0 7.5 %collective-permute-start.1 = (bf16[4,8,192,128]{3,2,1,0:T(8,128)(2,1)S(1)}, bf16[4,8,192,128]{3,2,1,0:T(8,128)(2,1)S(1)}, u32[]{:S(2)}, u32[]{:S(2)}) collective-permute-start(bf16[4,8,192,128]{3,2,1,0:T(8,128)(2,1)S(1)} %all-to-all-done.1.mine_hbm), channel_id=1, source_target_pairs={{0,8},{8,0},{1,9},{9,1},{2,10},{10,2},{3,11},{11,3},{4,12},{12,4},... | collective-permute-start | bytes 4718600 | tf_op jit(solution)/shard_map/ppermute | solution.py:380
  113.5 6.5 %make_queries.1 = (bf16[192,512]{1,0:T(8,128)(2,1)}, f32[192,128]{1,0:T(8,128)}) custom-call(s32[2]{0:T(128)} %copy-done.3, bf16[8,208,512]{2,1,0:T(8,128)(2,1)} %bitcast.13, bf16[4,8,64,512]{3,2,1,0:T(8,128)(2,1)} %bitcast.22, bf16[4,8,64,512]{3,2,1,0:T(8,128)(2,1)} %collective-permute-done.2.other_hbm, f32[1,128]{1,0:T(1,128)} %bitcast.25), custom_call_target="tpu_custom_call" | custom-call | tf_op jit(solution)/shard_map/make_queries/pallas_call | solution.py:171
  120.1 1.1 copy-done.6
  121.2 5.6 %pack_keys.1 = (bf16[6144,128]{1,0:T(8,128)(2,1)}, bf16[6144,128]{1,0:T(8,128)(2,1)}, s32[3,32]{1,0:T(4,128)}) custom-call(s32[2]{0:T(128)} %copy-done.3, s32[2,4,8,128]{3,2,1,0:T(8,128)} %copy-done.2, s32[1]{0:T(128)S(6)} %copy.11.count_ref, bf16[4,8,192,128]{3,2,1,0:T(8,128)(2,1)} %copy-done.5, bf16[4,8,192,128]{3,2,1,0:T(8,128)(2,1)} %copy-done.6, ...), custom_call_target="tpu_custom_call" | custom-call | tf_op jit(solution)/shard_map/pack_keys/pallas_call | solution.py:241
  126.8 2.6 %all-gather.12.cloned.1.call-done = bf16[64,1,192,128]{3,2,1,0:T(8,128)(2,1)} async-done(((bf16[8,1,192,128]{3,2,1,0:T(8,128)(2,1)}), bf16[64,1,192,128]{3,2,1,0:T(8,128)(2,1)}) %all-gather.12.cloned.1.call-update) | async-done | bytes 3145744 | tf_op jit(solution)/shard_map/all_gather | solution.py:408
  129.4 9.6 %attend.1 = bf16[512,512]{1,0:T(8,128)(2,1)} custom-call(s32[3,32]{1,0:T(4,128)} %get-tuple-element.19.table_ref, bf16[192,512]{1,0:T(8,128)(2,1)} %get-tuple-element.18._.q_ref, bf16[2,192,128]{2,1,0:T(8,128)(2,1)} %copy-done.1, s32[1,192]{1,0:T(1,128)} %bitcast.24, f32[192,128]{1,0:T(8,128)} %get-tuple-element.20.gate_ref, ...), custom_call_target="tpu_custom_call" | custom-call | tf_op jit(solution)/shard_map/attend/pallas_call | solution.py:355
  (21 shorter events, 0.2 us)
Async XLA Ops:
  6.5 51.5 %all-gather.8.cloned.1.call-start = ((), (), s32[]{:S(2)}) async-start(), calls=%async_computation.2 | async-start | bytes 1916928 | tf_op jit(solution)/shard_map/all_gather | solution.py:396
  9.3 84.3 %all-gather.10.cloned.1.call-start = ((), (), s32[]{:S(2)}) async-start(), calls=%async_computation.3 | async-start | bytes 2621440 | tf_op jit(solution)/shard_map/all_gather | solution.py:401
  31.2 98.2 %all-gather.12.cloned.1.call-start = ((), (), s32[]{:S(2)}) async-start(), calls=%async_computation.4 | async-start | bytes 3538944 | tf_op jit(solution)/shard_map/all_gather | solution.py:408
  31.2 26.8 %copy-start.4 = (f32[128]{0:T(128)S(1)}, f32[128]{0:T(128)}, u32[]{:S(2)}) copy-start(f32[128]{0:T(128)} %param.17) | copy-start | bytes 1540
  45.5 12.6 %collective-permute-start = (bf16[4,8,72,256]{3,2,1,0:T(8,128)(2,1)S(1)}, bf16[4,8,72,256]{3,2,1,0:T(8,128)(2,1)S(1)}, u32[]{:S(2)}, u32[]{:S(2)}) collective-permute-start(bf16[4,8,72,256]{3,2,1,0:T(8,128)(2,1)S(1)} %all_to_all.10.mine_ref), channel_id=1, source_target_pairs={{0,8},{8,0},{1,9},{9,1},{2,10},{10,2},{3,11},{11,3},{4,12},{12,4},... | collective-permute-start | bytes 3538952 | tf_op jit(solution)/shard_map/ppermute | solution.py:380
  55.7 5.5 %copy-start.3 = (s32[2]{0:T(128)}, s32[2]{0:T(128)S(1)}, u32[]{:S(2)}) copy-start(s32[2]{0:T(128)S(1)} %pad_add_fusion.place_ref) | copy-start | bytes 28
  58.1 1.5 copy-start
  61.2 0.6 copy-start.2
  61.8 24.6 %copy-start.1 = (bf16[2,192,128]{2,1,0:T(8,128)(2,1)}, bf16[2,192,128]{2,1,0:T(8,128)(2,1)S(1)}, u32[]{:S(2)}) copy-start(bf16[2,192,128]{2,1,0:T(8,128)(2,1)S(1)} %get-tuple-element.17.own_ref) | copy-start | bytes 294916
  86.4 19.6 %all-to-all-start.1 = ((bf16[4,8,192,128]{3,2,1,0:T(8,128)(2,1)}), bf16[4,8,192,128]{3,2,1,0:T(8,128)(2,1)S(1)}, u32[]{:S(2)}, u32[]{:S(2)}) async-start(bf16[4,8,192,128]{3,2,1,0:T(8,128)(2,1)} %broadcast_in_dim.15), calls=%async_computation.1 | async-start | bytes 3145728 | tf_op jit(solution)/shard_map/all_to_all | solution.py:374
  93.6 19.9 %collective-permute-start.2 = (bf16[4,8,64,512]{3,2,1,0:T(8,128)(2,1)}, bf16[4,8,64,512]{3,2,1,0:T(8,128)(2,1)}, u32[]{:S(2)}, u32[]{:S(2)}) collective-permute-start(bf16[4,8,64,512]{3,2,1,0:T(8,128)(2,1)} %bitcast.21), channel_id=1, source_target_pairs={{0,8},{8,0},{1,9},{9,1},{2,10},{10,2},{3,11},{11,3},{4,12},{12,4},... | collective-permute-start | bytes 6291464 | tf_op jit(solution)/shard_map/ppermute | solution.py:380
  106.0 14.1 %copy-start.5 = (bf16[4,8,192,128]{3,2,1,0:T(8,128)(2,1)}, bf16[4,8,192,128]{3,2,1,0:T(8,128)(2,1)S(1)}, u32[]{:S(2)}) copy-start(bf16[4,8,192,128]{3,2,1,0:T(8,128)(2,1)S(1)} %all-to-all-done.1.mine_hbm) | copy-start | bytes 4718596
  106.0 14.1 %collective-permute-start.1 = (bf16[4,8,192,128]{3,2,1,0:T(8,128)(2,1)S(1)}, bf16[4,8,192,128]{3,2,1,0:T(8,128)(2,1)S(1)}, u32[]{:S(2)}, u32[]{:S(2)}) collective-permute-start(bf16[4,8,192,128]{3,2,1,0:T(8,128)(2,1)S(1)} %all-to-all-done.1.mine_hbm), channel_id=1, source_target_pairs={{0,8},{8,0},{1,9},{9,1},{2,10},{10,2},{3,11},{11,3},{4,12},{12,4},... | collective-permute-start | bytes 4718600 | tf_op jit(solution)/shard_map/ppermute | solution.py:380
  120.1 1.2 copy-start.6
Sparse Core Ops, SparseCore 0:
  9.4 43.7 all-gather.7
  55.4 38.2 all-gather.9
  95.8 33.5 all-gather.11

commit v5 on v4

--- a/solution.py
+++ b/solution.py
@@ -10,7 +10,7 @@
 
 SEQ = ("y", "x", "core")
 TILE = 1024
-HALF = 512
+PIECE = 256
 
 
 def whole(memory_space=pltpu.VMEM):
@@ -56,7 +56,7 @@
     return pl.pallas_call(
         stage_kernel,
         out_shape=(
-            jax.ShapeDtypeStruct((slots + 16, width), jnp.bfloat16),
+            jax.ShapeDtypeStruct((slots + 8, width), jnp.bfloat16),
             jax.ShapeDtypeStruct((deep + 8, across), jnp.bfloat16),
         ),
         in_specs=[whole(pltpu.SMEM)] + [whole()] * 7,
@@ -266,7 +266,8 @@
     end, core, count = table_ref[2, 0], table_ref[2, 1], table_ref[2, 2]
     factor = math.log2(math.e) / math.sqrt(head)
     copies = [pltpu.make_async_copy(values_hbm.at[x], values.at[x], arrived.at[x]) for x in range(nx)]
-    halves = (end + HALF - 1) // HALF
+    pieces_used = (end + PIECE - 1) // PIECE
+    full, tail = pieces_used // (TILE // PIECE), pieces_used % (TILE // PIECE)
 
     def chunk(at):
         rows = pl.ds(pl.multiple_of(at * TILE, TILE), TILE)
@@ -281,7 +282,7 @@
         return carry
 
     copies[0].start()
-    lax.fori_loop(0, (halves + 1) // 2, begin, 0)
+    lax.fori_loop(0, (end + TILE - 1) // TILE, begin, 0)
     for copy in copies[1:]:
         copy.start()
 
@@ -324,15 +325,20 @@
 
         if x == nx - 1:
             packed[pl.ds(pl.multiple_of(end, 16), TILE), :head] = jnp.zeros((TILE, head), jnp.bfloat16)
-        ready = halves // 2 if x == nx - 1 else table_ref[2, 3 + x] // TILE
+        ready = full if x == nx - 1 else table_ref[2, 3 + x] // TILE
         lax.fori_loop(done, ready, tile, 0)
         done = ready
 
-    @pl.when(halves % 2 == 1)
+    @pl.when(tail > 0)
     def _():
         for copy in chunk(done):
             copy.wait()
-        weigh(done * TILE, HALF)
+
+    for size in (2 * PIECE, PIECE):
+
+        @pl.when((tail * PIECE) & size > 0)
+        def _():
+            weigh(done * TILE + ((tail * PIECE) // (2 * size) * (2 * size)), size)
 
     block = out_ref.shape[0]
     live = lax.broadcasted_iota(jnp.int32, (slots, 1), 0) < count

time: 146 us -> 146 us (level)
  no operation moved by 1% of the time
where the time goes in v5:
time: 146 us; the launch traced here: 145 us
  blocking collectives  57.3 us (39%)
  Pallas kernels  24.8 us (17%)
  starting transfers between devices  24 us (16%)
  waiting for transfers between devices  18.2 us (12%)
  between operations  13.9 us (10%)
  local copies, waits for them, and re-layouts  6.48 us (4%)
    all_gather x1, blocking collectives, local(): lax.all_gather(own.reshape(2 * slots, head), 'y', axis=0, tiled=False)  22.2 us
    all_gather x1, blocking collectives, local(): weights_y = lax.all_gather(weights, 'y', axis=0, tiled=False)  20.9 us
    ppermute x3, starting transfers between devices, swap_cores(): return lax.ppermute(block, 'core', [(0, 1), (1, 0)])  20.3 us
    all_to_all x1, blocking collectives, to_all(): lax.all_to_all(jnp.broadcast_to(block[None], (peers,) + block.shape), axe...  14.2 us
    all_to_all x1, waiting for transfers between devices, to_all(): lax.all_to_all(jnp.broadcast_to(block[None], (peers,) + block.shape), axe...  9.69 us
    pallas_call x1, Pallas kernels, attend(): pl.pallas_call(attend_kernel, out_shape=jax.ShapeDtypeStruct((block, widt...  8.96 us
    pallas_call x1, Pallas kernels, make_queries(): pl.pallas_call(queries_kernel, out_shape=(jax.ShapeDtypeStruct((slots, wi...  6.5 us
    pallas_call x1, Pallas kernels, pack_keys(): pl.pallas_call(pack_kernel, out_shape=(jax.ShapeDtypeStruct((rows + TILE,...  5.6 us
  transfers between devices with their start and end apart: 7, of which 4 were waited for; matrix products, arithmetic and copies ran while one was open for 2% of the time, Pallas kernels for 9%

profile of v5, /device:TPU:57, one launch (start us, length us, event | category | flops | bytes accessed | tf_op | source)
XLA Modules:
  0.0 144.8 jit_solution(2049559923735068889)
XLA Ops:
  7.2 2.1 %stage.1 = (bf16[200,512]{1,0:T(8,128)(2,1)}, bf16[72,768]{1,0:T(8,128)(2,1)}) custom-call(s32[1]{0:T(128)S(6)} %copy.11.count_ref, bf16[512,512]{1,0:T(8,128)(2,1)} %tokens_ref.1, s32[1,192]{1,0:T(1,128)} %bitcast.23, bf16[512]{0:T(512)(128)(2,1)} %gain_ref.1, bf16[512]{0:T(512)(128)(2,1)} %router_ref.1, bf16[64,512]{1,0:T(8,128)(2,1)} %query_ref.1, ...), custom_call_target="tpu_custom_call" | custom-call | tf_op jit(solution)/shard_map/stage/pallas_call | solution.py:56
  9.3 20.9 %all-gather.1 = bf16[576,768]{1,0:T(8,128)(2,1)S(1)} all-gather(bf16[72,768]{1,0:T(8,128)(2,1)} %get-tuple-element.15), channel_id=3, replica_groups=mesh['y'=8,'x'=4,'core'=2,'z'=8] {'y'}, dimensions={0}, use_global_device_ids=true | all-gather | bytes 995328 | tf_op jit(solution)/shard_map/all_gather | solution.py:404
  30.3 0.8 slice.18
  31.2 0.1 broadcast_in_dim.6
  31.3 14.2 %all_to_all.10.mine_ref = bf16[4,8,72,256]{3,2,1,0:T(8,128)(2,1)S(1)} all-to-all(bf16[4,8,72,256]{3,2,1,0:T(8,128)(2,1)S(1)} %broadcast_in_dim.6), channel_id=1, replica_groups=mesh['y'=8,'x'=4,'core'=2,'z'=8] {'x'}, dimensions={0} | all-to-all | bytes 2359296 | tf_op jit(solution)/shard_map/all_to_all | solution.py:380
  45.5 10.1 %collective-permute-start = (bf16[4,8,72,256]{3,2,1,0:T(8,128)(2,1)S(1)}, bf16[4,8,72,256]{3,2,1,0:T(8,128)(2,1)S(1)}, u32[]{:S(2)}, u32[]{:S(2)}) collective-permute-start(bf16[4,8,72,256]{3,2,1,0:T(8,128)(2,1)S(1)} %all_to_all.10.mine_ref), channel_id=1, source_target_pairs={{0,8},{8,0},{1,9},{9,1},{2,10},{10,2},{3,11},{11,3},{4,12},{12,4},... | collective-permute-start | bytes 3538952 | tf_op jit(solution)/shard_map/ppermute | solution.py:386
  55.6 0.1 pad_add_fusion.place_ref
  55.7 2.4 %collective-permute-done.other_ref = bf16[4,8,72,256]{3,2,1,0:T(8,128)(2,1)S(1)} collective-permute-done((bf16[4,8,72,256]{3,2,1,0:T(8,128)(2,1)S(1)}, bf16[4,8,72,256]{3,2,1,0:T(8,128)(2,1)S(1)}, u32[]{:S(2)}, u32[]{:S(2)}) %collective-permute-start) | collective-permute-done | bytes 1179680 | tf_op jit(solution)/shard_map/ppermute | solution.py:386
  58.0 1.4 copy-done
  59.5 1.6 %make_keys.1 = (bf16[2,192,128]{2,1,0:T(8,128)(2,1)S(1)}, s32[2,4,8,128]{3,2,1,0:T(8,128)S(1)}) custom-call(s32[2]{0:T(128)S(1)} %pad_add_fusion.place_ref, s32[1]{0:T(128)S(6)} %copy.11.count_ref, bf16[8,200,512]{2,1,0:T(8,128)(2,1)S(1)} %bitcast.14, bf16[4,8,72,256]{3,2,1,0:T(8,128)(2,1)S(1)} %all_to_all.10.mine_ref, ...), custom_call_target="tpu_custom_call" | custom-call | tf_op jit(solution)/shard_map/make_keys/pallas_call | solution.py:119
  61.1 0.6 copy-done.2
  61.7 22.2 %all_gather.28 = bf16[8,384,128]{2,1,0:T(8,128)(2,1)S(1)} all-gather(bf16[1,384,128]{2,1,0:T(8,128)(2,1)S(1)} %bitcast.15), channel_id=1, replica_groups=mesh['y'=8,'x'=4,'core'=2,'z'=8] {'y'}, dimensions={0}, use_global_device_ids=true | all-gather | bytes 884736 | tf_op jit(solution)/shard_map/all_gather | solution.py:412
  83.9 0.8 fusion
  84.8 1.5 %broadcast_in_dim.15 = bf16[4,8,192,128]{3,2,1,0:T(8,128)(2,1)} broadcast(bf16[8,192,128]{2,1,0:T(8,128)(2,1)S(1)} %get-tuple-element.24), dimensions={1,2,3} | broadcast | bytes 1966080 | tf_op jit(solution)/shard_map/broadcast_in_dim | solution.py:381
  86.3 3.6 %all-to-all-start.1 = ((bf16[4,8,192,128]{3,2,1,0:T(8,128)(2,1)}), bf16[4,8,192,128]{3,2,1,0:T(8,128)(2,1)S(1)}, u32[]{:S(2)}, u32[]{:S(2)}) async-start(bf16[4,8,192,128]{3,2,1,0:T(8,128)(2,1)} %broadcast_in_dim.15), calls=%async_computation.1 | async-start | bytes 3145728 | tf_op jit(solution)/shard_map/all_to_all | solution.py:380
  89.9 3.6 %all-gather.10.cloned.1.call-done = bf16[32,64,512]{2,1,0:T(8,128)(2,1)} async-done(((bf16[8,64,512]{2,1,0:T(8,128)(2,1)}), bf16[32,64,512]{2,1,0:T(8,128)(2,1)}) %all-gather.10.cloned.1.call-update) | async-done | bytes 2097168 | tf_op jit(solution)/shard_map/all_gather | solution.py:407
  93.5 2.7 %collective-permute-start.2 = (bf16[4,8,64,512]{3,2,1,0:T(8,128)(2,1)}, bf16[4,8,64,512]{3,2,1,0:T(8,128)(2,1)}, u32[]{:S(2)}, u32[]{:S(2)}) collective-permute-start(bf16[4,8,64,512]{3,2,1,0:T(8,128)(2,1)} %bitcast.21), channel_id=1, source_target_pairs={{0,8},{8,0},{1,9},{9,1},{2,10},{10,2},{3,11},{11,3},{4,12},{12,4},... | collective-permute-start | bytes 6291464 | tf_op jit(solution)/shard_map/ppermute | solution.py:386
  96.2 9.7 %all-to-all-done.1.mine_hbm = bf16[4,8,192,128]{3,2,1,0:T(8,128)(2,1)S(1)} async-done(((bf16[4,8,192,128]{3,2,1,0:T(8,128)(2,1)}), bf16[4,8,192,128]{3,2,1,0:T(8,128)(2,1)S(1)}, u32[]{:S(2)}, u32[]{:S(2)}) %all-to-all-start.1) | async-done | bytes 1572896 | tf_op jit(solution)/shard_map/all_to_all | solution.py:380
  105.9 7.5 %collective-permute-start.1 = (bf16[4,8,192,128]{3,2,1,0:T(8,128)(2,1)S(1)}, bf16[4,8,192,128]{3,2,1,0:T(8,128)(2,1)S(1)}, u32[]{:S(2)}, u32[]{:S(2)}) collective-permute-start(bf16[4,8,192,128]{3,2,1,0:T(8,128)(2,1)S(1)} %all-to-all-done.1.mine_hbm), channel_id=1, source_target_pairs={{0,8},{8,0},{1,9},{9,1},{2,10},{10,2},{3,11},{11,3},{4,12},{12,4},... | collective-permute-start | bytes 4718600 | tf_op jit(solution)/shard_map/ppermute | solution.py:386
  113.5 6.5 %make_queries.1 = (bf16[192,512]{1,0:T(8,128)(2,1)}, f32[192,128]{1,0:T(8,128)}) custom-call(s32[2]{0:T(128)} %copy-done.3, bf16[8,200,512]{2,1,0:T(8,128)(2,1)} %bitcast.13, bf16[4,8,64,512]{3,2,1,0:T(8,128)(2,1)} %bitcast.22, bf16[4,8,64,512]{3,2,1,0:T(8,128)(2,1)} %collective-permute-done.2.other_hbm, f32[1,128]{1,0:T(1,128)} %bitcast.25), custom_call_target="tpu_custom_call" | custom-call | tf_op jit(solution)/shard_map/make_queries/pallas_call | solution.py:171
  120.0 1.1 copy-done.6
  121.1 5.6 %pack_keys.1 = (bf16[6144,128]{1,0:T(8,128)(2,1)}, bf16[6144,128]{1,0:T(8,128)(2,1)}, s32[3,32]{1,0:T(4,128)}) custom-call(s32[2]{0:T(128)} %copy-done.3, s32[2,4,8,128]{3,2,1,0:T(8,128)} %copy-done.2, s32[1]{0:T(128)S(6)} %copy.11.count_ref, bf16[4,8,192,128]{3,2,1,0:T(8,128)(2,1)} %copy-done.5, bf16[4,8,192,128]{3,2,1,0:T(8,128)(2,1)} %copy-done.6, ...), custom_call_target="tpu_custom_call" | custom-call | tf_op jit(solution)/shard_map/pack_keys/pallas_call | solution.py:241
  126.7 2.5 %all-gather.12.cloned.1.call-done = bf16[64,1,192,128]{3,2,1,0:T(8,128)(2,1)} async-done(((bf16[8,1,192,128]{3,2,1,0:T(8,128)(2,1)}), bf16[64,1,192,128]{3,2,1,0:T(8,128)(2,1)}) %all-gather.12.cloned.1.call-update) | async-done | bytes 3145744 | tf_op jit(solution)/shard_map/all_gather | solution.py:414
  129.2 9.0 %attend.1 = bf16[512,512]{1,0:T(8,128)(2,1)} custom-call(s32[3,32]{1,0:T(4,128)} %get-tuple-element.19.table_ref, bf16[192,512]{1,0:T(8,128)(2,1)} %get-tuple-element.18._.q_ref, bf16[2,192,128]{2,1,0:T(8,128)(2,1)} %copy-done.1, s32[1,192]{1,0:T(1,128)} %bitcast.24, f32[192,128]{1,0:T(8,128)} %get-tuple-element.20.gate_ref, ...), custom_call_target="tpu_custom_call" | custom-call | tf_op jit(solution)/shard_map/attend/pallas_call | solution.py:361
  (21 shorter events, 0.2 us)
Async XLA Ops:
  6.5 51.5 %all-gather.8.cloned.1.call-start = ((), (), s32[]{:S(2)}) async-start(), calls=%async_computation.2 | async-start | bytes 1843200 | tf_op jit(solution)/shard_map/all_gather | solution.py:402
  9.3 84.2 %all-gather.10.cloned.1.call-start = ((), (), s32[]{:S(2)}) async-start(), calls=%async_computation.3 | async-start | bytes 2621440 | tf_op jit(solution)/shard_map/all_gather | solution.py:407
  31.1 98.1 %all-gather.12.cloned.1.call-start = ((), (), s32[]{:S(2)}) async-start(), calls=%async_computation.4 | async-start | bytes 3538944 | tf_op jit(solution)/shard_map/all_gather | solution.py:414
  31.2 26.8 %copy-start.4 = (f32[128]{0:T(128)S(1)}, f32[128]{0:T(128)}, u32[]{:S(2)}) copy-start(f32[128]{0:T(128)} %param.17) | copy-start | bytes 1540
  45.5 12.6 %collective-permute-start = (bf16[4,8,72,256]{3,2,1,0:T(8,128)(2,1)S(1)}, bf16[4,8,72,256]{3,2,1,0:T(8,128)(2,1)S(1)}, u32[]{:S(2)}, u32[]{:S(2)}) collective-permute-start(bf16[4,8,72,256]{3,2,1,0:T(8,128)(2,1)S(1)} %all_to_all.10.mine_ref), channel_id=1, source_target_pairs={{0,8},{8,0},{1,9},{9,1},{2,10},{10,2},{3,11},{11,3},{4,12},{12,4},... | collective-permute-start | bytes 3538952 | tf_op jit(solution)/shard_map/ppermute | solution.py:386
  55.7 5.5 %copy-start.3 = (s32[2]{0:T(128)}, s32[2]{0:T(128)S(1)}, u32[]{:S(2)}) copy-start(s32[2]{0:T(128)S(1)} %pad_add_fusion.place_ref) | copy-start | bytes 28
  58.0 1.4 copy-start
  61.1 0.6 copy-start.2
  61.7 24.6 %copy-start.1 = (bf16[2,192,128]{2,1,0:T(8,128)(2,1)}, bf16[2,192,128]{2,1,0:T(8,128)(2,1)S(1)}, u32[]{:S(2)}) copy-start(bf16[2,192,128]{2,1,0:T(8,128)(2,1)S(1)} %get-tuple-element.17.own_ref) | copy-start | bytes 294916
  86.3 19.6 %all-to-all-start.1 = ((bf16[4,8,192,128]{3,2,1,0:T(8,128)(2,1)}), bf16[4,8,192,128]{3,2,1,0:T(8,128)(2,1)S(1)}, u32[]{:S(2)}, u32[]{:S(2)}) async-start(bf16[4,8,192,128]{3,2,1,0:T(8,128)(2,1)} %broadcast_in_dim.15), calls=%async_computation.1 | async-start | bytes 3145728 | tf_op jit(solution)/shard_map/all_to_all | solution.py:380
  93.5 19.9 %collective-permute-start.2 = (bf16[4,8,64,512]{3,2,1,0:T(8,128)(2,1)}, bf16[4,8,64,512]{3,2,1,0:T(8,128)(2,1)}, u32[]{:S(2)}, u32[]{:S(2)}) collective-permute-start(bf16[4,8,64,512]{3,2,1,0:T(8,128)(2,1)} %bitcast.21), channel_id=1, source_target_pairs={{0,8},{8,0},{1,9},{9,1},{2,10},{10,2},{3,11},{11,3},{4,12},{12,4},... | collective-permute-start | bytes 6291464 | tf_op jit(solution)/shard_map/ppermute | solution.py:386
  105.9 14.1 %copy-start.5 = (bf16[4,8,192,128]{3,2,1,0:T(8,128)(2,1)}, bf16[4,8,192,128]{3,2,1,0:T(8,128)(2,1)S(1)}, u32[]{:S(2)}) copy-start(bf16[4,8,192,128]{3,2,1,0:T(8,128)(2,1)S(1)} %all-to-all-done.1.mine_hbm) | copy-start | bytes 4718596
  105.9 14.1 %collective-permute-start.1 = (bf16[4,8,192,128]{3,2,1,0:T(8,128)(2,1)S(1)}, bf16[4,8,192,128]{3,2,1,0:T(8,128)(2,1)S(1)}, u32[]{:S(2)}, u32[]{:S(2)}) collective-permute-start(bf16[4,8,192,128]{3,2,1,0:T(8,128)(2,1)S(1)} %all-to-all-done.1.mine_hbm), channel_id=1, source_target_pairs={{0,8},{8,0},{1,9},{9,1},{2,10},{10,2},{3,11},{11,3},{4,12},{12,4},... | collective-permute-start | bytes 4718600 | tf_op jit(solution)/shard_map/ppermute | solution.py:386
  120.0 1.2 copy-start.6
Sparse Core Ops, SparseCore 0:
  9.4 43.7 all-gather.7
  55.3 38.1 all-gather.9
  95.6 33.5 all-gather.11

commit v6 on v5

--- a/solution.py
+++ b/solution.py
@@ -281,10 +281,10 @@
             copy.start()
         return carry
 
+    tiles = (end + TILE - 1) // TILE
     copies[0].start()
-    lax.fori_loop(0, (end + TILE - 1) // TILE, begin, 0)
-    for copy in copies[1:]:
-        copy.start()
+    lax.fori_loop(0, jnp.minimum(tiles, 1), begin, 0)
+    copies[1].start()
 
     across = lax.broadcasted_iota(jnp.int32, (slots, slots), 1)
     along = lax.broadcasted_iota(jnp.int32, (slots, slots), 0)
@@ -296,6 +296,10 @@
         query = q_ref[:, h * head : (h + 1) * head]
         weights = jnp.exp2(dot(query, own_ref[0], 1, 1) * factor)
         total[h] = dot(jnp.where(allowed, weights, 0.0).astype(jnp.bfloat16), summed)
+
+    lax.fori_loop(1, tiles, begin, 0)
+    for copy in copies[2:]:
+        copy.start()
 
     def weigh(start, size):
         rows = pl.ds(pl.multiple_of(start, size), size)

time: 146 us -> 146 us (level)
  no operation moved by 1% of the time
where the time goes in v6:
time: 146 us; the launch traced here: 145 us
  blocking collectives  57.3 us (39%)
  Pallas kernels  25.3 us (17%)
  starting transfers between devices  24 us (16%)
  waiting for transfers between devices  18.2 us (12%)
  between operations  13.9 us (10%)
  local copies, waits for them, and re-layouts  6.48 us (4%)
    all_gather x1, blocking collectives, local(): lax.all_gather(own.reshape(2 * slots, head), 'y', axis=0, tiled=False)  22.2 us
    all_gather x1, blocking collectives, local(): weights_y = lax.all_gather(weights, 'y', axis=0, tiled=False)  20.9 us
    ppermute x3, starting transfers between devices, swap_cores(): return lax.ppermute(block, 'core', [(0, 1), (1, 0)])  20.3 us
    all_to_all x1, blocking collectives, to_all(): lax.all_to_all(jnp.broadcast_to(block[None], (peers,) + block.shape), axe...  14.2 us
    all_to_all x1, waiting for transfers between devices, to_all(): lax.all_to_all(jnp.broadcast_to(block[None], (peers,) + block.shape), axe...  9.69 us
    pallas_call x1, Pallas kernels, attend(): pl.pallas_call(attend_kernel, out_shape=jax.ShapeDtypeStruct((block, widt...  9.44 us
    pallas_call x1, Pallas kernels, make_queries(): pl.pallas_call(queries_kernel, out_shape=(jax.ShapeDtypeStruct((slots, wi...  6.5 us
    pallas_call x1, Pallas kernels, pack_keys(): pl.pallas_call(pack_kernel, out_shape=(jax.ShapeDtypeStruct((rows + TILE,...  5.6 us
  transfers between devices with their start and end apart: 7, of which 4 were waited for; matrix products, arithmetic and copies ran while one was open for 2% of the time, Pallas kernels for 9%

profile of v6, /device:TPU:57, one launch (start us, length us, event | category | flops | bytes accessed | tf_op | source)
XLA Modules:
  0.0 145.2 jit_solution(8297858269958731940)
XLA Ops:
  7.2 2.1 %stage.1 = (bf16[200,512]{1,0:T(8,128)(2,1)}, bf16[72,768]{1,0:T(8,128)(2,1)}) custom-call(s32[1]{0:T(128)S(6)} %copy.11.count_ref, bf16[512,512]{1,0:T(8,128)(2,1)} %tokens_ref.1, s32[1,192]{1,0:T(1,128)} %bitcast.23, bf16[512]{0:T(512)(128)(2,1)} %gain_ref.1, bf16[512]{0:T(512)(128)(2,1)} %router_ref.1, bf16[64,512]{1,0:T(8,128)(2,1)} %query_ref.1, ...), custom_call_target="tpu_custom_call" | custom-call | tf_op jit(solution)/shard_map/stage/pallas_call | solution.py:56
  9.3 20.9 %all-gather.1 = bf16[576,768]{1,0:T(8,128)(2,1)S(1)} all-gather(bf16[72,768]{1,0:T(8,128)(2,1)} %get-tuple-element.15), channel_id=3, replica_groups=mesh['y'=8,'x'=4,'core'=2,'z'=8] {'y'}, dimensions={0}, use_global_device_ids=true | all-gather | bytes 995328 | tf_op jit(solution)/shard_map/all_gather | solution.py:408
  30.3 0.8 slice.18
  31.2 0.1 broadcast_in_dim.6
  31.3 14.2 %all_to_all.10.mine_ref = bf16[4,8,72,256]{3,2,1,0:T(8,128)(2,1)S(1)} all-to-all(bf16[4,8,72,256]{3,2,1,0:T(8,128)(2,1)S(1)} %broadcast_in_dim.6), channel_id=1, replica_groups=mesh['y'=8,'x'=4,'core'=2,'z'=8] {'x'}, dimensions={0} | all-to-all | bytes 2359296 | tf_op jit(solution)/shard_map/all_to_all | solution.py:384
  45.5 10.1 %collective-permute-start = (bf16[4,8,72,256]{3,2,1,0:T(8,128)(2,1)S(1)}, bf16[4,8,72,256]{3,2,1,0:T(8,128)(2,1)S(1)}, u32[]{:S(2)}, u32[]{:S(2)}) collective-permute-start(bf16[4,8,72,256]{3,2,1,0:T(8,128)(2,1)S(1)} %all_to_all.10.mine_ref), channel_id=1, source_target_pairs={{0,8},{8,0},{1,9},{9,1},{2,10},{10,2},{3,11},{11,3},{4,12},{12,4},... | collective-permute-start | bytes 3538952 | tf_op jit(solution)/shard_map/ppermute | solution.py:390
  55.6 0.1 pad_add_fusion.place_ref
  55.7 2.4 %collective-permute-done.other_ref = bf16[4,8,72,256]{3,2,1,0:T(8,128)(2,1)S(1)} collective-permute-done((bf16[4,8,72,256]{3,2,1,0:T(8,128)(2,1)S(1)}, bf16[4,8,72,256]{3,2,1,0:T(8,128)(2,1)S(1)}, u32[]{:S(2)}, u32[]{:S(2)}) %collective-permute-start) | collective-permute-done | bytes 1179680 | tf_op jit(solution)/shard_map/ppermute | solution.py:390
  58.0 1.4 copy-done
  59.5 1.6 %make_keys.1 = (bf16[2,192,128]{2,1,0:T(8,128)(2,1)S(1)}, s32[2,4,8,128]{3,2,1,0:T(8,128)S(1)}) custom-call(s32[2]{0:T(128)S(1)} %pad_add_fusion.place_ref, s32[1]{0:T(128)S(6)} %copy.11.count_ref, bf16[8,200,512]{2,1,0:T(8,128)(2,1)S(1)} %bitcast.14, bf16[4,8,72,256]{3,2,1,0:T(8,128)(2,1)S(1)} %all_to_all.10.mine_ref, ...), custom_call_target="tpu_custom_call" | custom-call | tf_op jit(solution)/shard_map/make_keys/pallas_call | solution.py:119
  61.1 0.6 copy-done.2
  61.7 22.2 %all_gather.28 = bf16[8,384,128]{2,1,0:T(8,128)(2,1)S(1)} all-gather(bf16[1,384,128]{2,1,0:T(8,128)(2,1)S(1)} %bitcast.15), channel_id=1, replica_groups=mesh['y'=8,'x'=4,'core'=2,'z'=8] {'y'}, dimensions={0}, use_global_device_ids=true | all-gather | bytes 884736 | tf_op jit(solution)/shard_map/all_gather | solution.py:416
  83.9 0.8 fusion
  84.8 1.5 %broadcast_in_dim.15 = bf16[4,8,192,128]{3,2,1,0:T(8,128)(2,1)} broadcast(bf16[8,192,128]{2,1,0:T(8,128)(2,1)S(1)} %get-tuple-element.24), dimensions={1,2,3} | broadcast | bytes 1966080 | tf_op jit(solution)/shard_map/broadcast_in_dim | solution.py:385
  86.3 3.6 %all-to-all-start.1 = ((bf16[4,8,192,128]{3,2,1,0:T(8,128)(2,1)}), bf16[4,8,192,128]{3,2,1,0:T(8,128)(2,1)S(1)}, u32[]{:S(2)}, u32[]{:S(2)}) async-start(bf16[4,8,192,128]{3,2,1,0:T(8,128)(2,1)} %broadcast_in_dim.15), calls=%async_computation.1 | async-start | bytes 3145728 | tf_op jit(solution)/shard_map/all_to_all | solution.py:384
  89.9 3.6 %all-gather.10.cloned.1.call-done = bf16[32,64,512]{2,1,0:T(8,128)(2,1)} async-done(((bf16[8,64,512]{2,1,0:T(8,128)(2,1)}), bf16[32,64,512]{2,1,0:T(8,128)(2,1)}) %all-gather.10.cloned.1.call-update) | async-done | bytes 2097168 | tf_op jit(solution)/shard_map/all_gather | solution.py:411
  93.5 2.7 %collective-permute-start.2 = (bf16[4,8,64,512]{3,2,1,0:T(8,128)(2,1)}, bf16[4,8,64,512]{3,2,1,0:T(8,128)(2,1)}, u32[]{:S(2)}, u32[]{:S(2)}) collective-permute-start(bf16[4,8,64,512]{3,2,1,0:T(8,128)(2,1)} %bitcast.21), channel_id=1, source_target_pairs={{0,8},{8,0},{1,9},{9,1},{2,10},{10,2},{3,11},{11,3},{4,12},{12,4},... | collective-permute-start | bytes 6291464 | tf_op jit(solution)/shard_map/ppermute | solution.py:390
  96.2 9.7 %all-to-all-done.1.mine_hbm = bf16[4,8,192,128]{3,2,1,0:T(8,128)(2,1)S(1)} async-done(((bf16[4,8,192,128]{3,2,1,0:T(8,128)(2,1)}), bf16[4,8,192,128]{3,2,1,0:T(8,128)(2,1)S(1)}, u32[]{:S(2)}, u32[]{:S(2)}) %all-to-all-start.1) | async-done | bytes 1572896 | tf_op jit(solution)/shard_map/all_to_all | solution.py:384
  105.9 7.5 %collective-permute-start.1 = (bf16[4,8,192,128]{3,2,1,0:T(8,128)(2,1)S(1)}, bf16[4,8,192,128]{3,2,1,0:T(8,128)(2,1)S(1)}, u32[]{:S(2)}, u32[]{:S(2)}) collective-permute-start(bf16[4,8,192,128]{3,2,1,0:T(8,128)(2,1)S(1)} %all-to-all-done.1.mine_hbm), channel_id=1, source_target_pairs={{0,8},{8,0},{1,9},{9,1},{2,10},{10,2},{3,11},{11,3},{4,12},{12,4},... | collective-permute-start | bytes 4718600 | tf_op jit(solution)/shard_map/ppermute | solution.py:390
  113.5 6.5 %make_queries.1 = (bf16[192,512]{1,0:T(8,128)(2,1)}, f32[192,128]{1,0:T(8,128)}) custom-call(s32[2]{0:T(128)} %copy-done.3, bf16[8,200,512]{2,1,0:T(8,128)(2,1)} %bitcast.13, bf16[4,8,64,512]{3,2,1,0:T(8,128)(2,1)} %bitcast.22, bf16[4,8,64,512]{3,2,1,0:T(8,128)(2,1)} %collective-permute-done.2.other_hbm, f32[1,128]{1,0:T(1,128)} %bitcast.25), custom_call_target="tpu_custom_call" | custom-call | tf_op jit(solution)/shard_map/make_queries/pallas_call | solution.py:171
  120.0 1.1 copy-done.6
  121.1 5.6 %pack_keys.1 = (bf16[6144,128]{1,0:T(8,128)(2,1)}, bf16[6144,128]{1,0:T(8,128)(2,1)}, s32[3,32]{1,0:T(4,128)}) custom-call(s32[2]{0:T(128)} %copy-done.3, s32[2,4,8,128]{3,2,1,0:T(8,128)} %copy-done.2, s32[1]{0:T(128)S(6)} %copy.11.count_ref, bf16[4,8,192,128]{3,2,1,0:T(8,128)(2,1)} %copy-done.5, bf16[4,8,192,128]{3,2,1,0:T(8,128)(2,1)} %copy-done.6, ...), custom_call_target="tpu_custom_call" | custom-call | tf_op jit(solution)/shard_map/pack_keys/pallas_call | solution.py:241
  126.7 2.5 %all-gather.12.cloned.1.call-done = bf16[64,1,192,128]{3,2,1,0:T(8,128)(2,1)} async-done(((bf16[8,1,192,128]{3,2,1,0:T(8,128)(2,1)}), bf16[64,1,192,128]{3,2,1,0:T(8,128)(2,1)}) %all-gather.12.cloned.1.call-update) | async-done | bytes 3145744 | tf_op jit(solution)/shard_map/all_gather | solution.py:418
  129.2 9.4 %attend.1 = bf16[512,512]{1,0:T(8,128)(2,1)} custom-call(s32[3,32]{1,0:T(4,128)} %get-tuple-element.19.table_ref, bf16[192,512]{1,0:T(8,128)(2,1)} %get-tuple-element.18._.q_ref, bf16[2,192,128]{2,1,0:T(8,128)(2,1)} %copy-done.1, s32[1,192]{1,0:T(1,128)} %bitcast.24, f32[192,128]{1,0:T(8,128)} %get-tuple-element.20.gate_ref, ...), custom_call_target="tpu_custom_call" | custom-call | tf_op jit(solution)/shard_map/attend/pallas_call | solution.py:365
  (21 shorter events, 0.2 us)
Async XLA Ops:
  6.5 51.5 %all-gather.8.cloned.1.call-start = ((), (), s32[]{:S(2)}) async-start(), calls=%async_computation.2 | async-start | bytes 1843200 | tf_op jit(solution)/shard_map/all_gather | solution.py:406
  9.3 84.2 %all-gather.10.cloned.1.call-start = ((), (), s32[]{:S(2)}) async-start(), calls=%async_computation.3 | async-start | bytes 2621440 | tf_op jit(solution)/shard_map/all_gather | solution.py:411
  31.1 98.1 %all-gather.12.cloned.1.call-start = ((), (), s32[]{:S(2)}) async-start(), calls=%async_computation.4 | async-start | bytes 3538944 | tf_op jit(solution)/shard_map/all_gather | solution.py:418
  31.2 26.8 %copy-start.4 = (f32[128]{0:T(128)S(1)}, f32[128]{0:T(128)}, u32[]{:S(2)}) copy-start(f32[128]{0:T(128)} %param.17) | copy-start | bytes 1540
  45.5 12.6 %collective-permute-start = (bf16[4,8,72,256]{3,2,1,0:T(8,128)(2,1)S(1)}, bf16[4,8,72,256]{3,2,1,0:T(8,128)(2,1)S(1)}, u32[]{:S(2)}, u32[]{:S(2)}) collective-permute-start(bf16[4,8,72,256]{3,2,1,0:T(8,128)(2,1)S(1)} %all_to_all.10.mine_ref), channel_id=1, source_target_pairs={{0,8},{8,0},{1,9},{9,1},{2,10},{10,2},{3,11},{11,3},{4,12},{12,4},... | collective-permute-start | bytes 3538952 | tf_op jit(solution)/shard_map/ppermute | solution.py:390
  55.7 5.5 %copy-start.3 = (s32[2]{0:T(128)}, s32[2]{0:T(128)S(1)}, u32[]{:S(2)}) copy-start(s32[2]{0:T(128)S(1)} %pad_add_fusion.place_ref) | copy-start | bytes 28
  58.0 1.4 copy-start
  61.1 0.6 copy-start.2
  61.7 24.6 %copy-start.1 = (bf16[2,192,128]{2,1,0:T(8,128)(2,1)}, bf16[2,192,128]{2,1,0:T(8,128)(2,1)S(1)}, u32[]{:S(2)}) copy-start(bf16[2,192,128]{2,1,0:T(8,128)(2,1)S(1)} %get-tuple-element.17.own_ref) | copy-start | bytes 294916
  86.3 19.6 %all-to-all-start.1 = ((bf16[4,8,192,128]{3,2,1,0:T(8,128)(2,1)}), bf16[4,8,192,128]{3,2,1,0:T(8,128)(2,1)S(1)}, u32[]{:S(2)}, u32[]{:S(2)}) async-start(bf16[4,8,192,128]{3,2,1,0:T(8,128)(2,1)} %broadcast_in_dim.15), calls=%async_computation.1 | async-start | bytes 3145728 | tf_op jit(solution)/shard_map/all_to_all | solution.py:384
  93.5 19.9 %collective-permute-start.2 = (bf16[4,8,64,512]{3,2,1,0:T(8,128)(2,1)}, bf16[4,8,64,512]{3,2,1,0:T(8,128)(2,1)}, u32[]{:S(2)}, u32[]{:S(2)}) collective-permute-start(bf16[4,8,64,512]{3,2,1,0:T(8,128)(2,1)} %bitcast.21), channel_id=1, source_target_pairs={{0,8},{8,0},{1,9},{9,1},{2,10},{10,2},{3,11},{11,3},{4,12},{12,4},... | collective-permute-start | bytes 6291464 | tf_op jit(solution)/shard_map/ppermute | solution.py:390
  105.9 14.1 %copy-start.5 = (bf16[4,8,192,128]{3,2,1,0:T(8,128)(2,1)}, bf16[4,8,192,128]{3,2,1,0:T(8,128)(2,1)S(1)}, u32[]{:S(2)}) copy-start(bf16[4,8,192,128]{3,2,1,0:T(8,128)(2,1)S(1)} %all-to-all-done.1.mine_hbm) | copy-start | bytes 4718596
  105.9 14.1 %collective-permute-start.1 = (bf16[4,8,192,128]{3,2,1,0:T(8,128)(2,1)S(1)}, bf16[4,8,192,128]{3,2,1,0:T(8,128)(2,1)S(1)}, u32[]{:S(2)}, u32[]{:S(2)}) collective-permute-start(bf16[4,8,192,128]{3,2,1,0:T(8,128)(2,1)S(1)} %all-to-all-done.1.mine_hbm), channel_id=1, source_target_pairs={{0,8},{8,0},{1,9},{9,1},{2,10},{10,2},{3,11},{11,3},{4,12},{12,4},... | collective-permute-start | bytes 4718600 | tf_op jit(solution)/shard_map/ppermute | solution.py:390
  120.0 1.2 copy-start.6
Sparse Core Ops, SparseCore 0:
  9.4 43.7 all-gather.7
  55.3 38.1 all-gather.9
  95.6 33.5 all-gather.11

commit v7 on v6

--- a/solution.py
+++ b/solution.py
@@ -27,9 +27,7 @@
     )
 
 
-def stage_kernel(
-    count_ref, tokens_ref, pos_ref, gain_ref, router_ref, query_ref, key_ref, value_ref, rows_ref, weights_ref
-):
+def stage_kernel(tokens_ref, pos_ref, gain_ref, router_ref, rows_ref):
     slots = pos_ref.shape[1]
     block, width = tokens_ref.shape
     hit = lax.broadcasted_iota(jnp.int32, (block, slots), 0) == pos_ref[...]
@@ -39,31 +37,19 @@
     extra = jnp.where(at == 0, gain_ref[...].astype(jnp.float32).reshape(1, width), 0.0)
     extra = jnp.where(at == 1, router_ref[...].astype(jnp.float32).reshape(1, width), extra)
     rows_ref[slots:, :] = extra.astype(jnp.bfloat16)
-    deep, query = query_ref.shape
-    key = key_ref.shape[1]
-    weights_ref[:deep, :query] = query_ref[...]
-    weights_ref[:deep, query : query + key] = key_ref[...]
-    weights_ref[:deep, query + key :] = value_ref[...]
-    count = jnp.full((weights_ref.shape[0] - deep, weights_ref.shape[1]), count_ref[0], jnp.int32)
-    weights_ref[deep:, :] = count.astype(jnp.float32).astype(jnp.bfloat16)
-
-
-def stage(count, tokens, route_pos, x_gain, w_router, w_query, key_weight, value_weight):
+
+
+def stage(tokens, route_pos, x_gain, w_router):
     slots = route_pos.shape[0]
     width = tokens.shape[1]
-    deep = w_query.shape[0]
-    across = w_query.shape[1] + key_weight.shape[1] + value_weight.shape[1]
     return pl.pallas_call(
         stage_kernel,
-        out_shape=(
-            jax.ShapeDtypeStruct((slots + 8, width), jnp.bfloat16),
-            jax.ShapeDtypeStruct((deep + 8, across), jnp.bfloat16),
-        ),
-        in_specs=[whole(pltpu.SMEM)] + [whole()] * 7,
-        out_specs=(whole(), whole()),
+        out_shape=jax.ShapeDtypeStruct((slots + 8, width), jnp.bfloat16),
+        in_specs=[whole()] * 4,
+        out_specs=whole(),
         compiler_params=params(),
         name="stage",
-    )(count, tokens, route_pos.reshape(1, slots), x_gain, w_router, w_query, key_weight, value_weight)
+    )(tokens, route_pos.reshape(1, slots), x_gain, w_router)
 
 
 def head_norm(projected, gain):
@@ -400,9 +386,10 @@
     deep, width = w_query.shape
     head = q_gain.shape[0]
 
-    picked, weights = stage(
-        route_count, tokens, route_pos, x_gain, w_router, w_query, key_weight, value_weight
-    )
+    picked = stage(tokens, route_pos, x_gain, w_router)
+    weights = jnp.concatenate([w_query, key_weight, value_weight], axis=1)
+    counted = jnp.full((8, weights.shape[1]), route_count[0].astype(jnp.bfloat16))
+    weights = jnp.concatenate([weights, counted], axis=0)
     rows = lax.all_gather(picked, "z", axis=0, tiled=False)
 
     weights_y = lax.all_gather(weights, "y", axis=0, tiled=False)

time: 146 us -> 145 us (level)
  transfers between devices with their start and end apart: 7 -> 7, of which waited for: 4 -> 4; matrix products, arithmetic and copies ran while one was open for 2% -> 3% of each run, Pallas kernels for 9% -> 9%
where the time goes in v7:
time: 145 us
  blocking collectives  57.3 us (40%)
  Pallas kernels  24.7 us (17%)
  starting transfers between devices  24 us (17%)
  waiting for transfers between devices  17.4 us (12%)
  between operations  13.9 us (10%)
  local copies, waits for them, and re-layouts  6.47 us (4%)
    all_gather x1, blocking collectives, local(): lax.all_gather(own.reshape(2 * slots, head), 'y', axis=0, tiled=False)  22.5 us
    all_gather x1, blocking collectives, local(): weights_y = lax.all_gather(weights, 'y', axis=0, tiled=False)  21 us
    ppermute x3, starting transfers between devices, swap_cores(): return lax.ppermute(block, 'core', [(0, 1), (1, 0)])  20.3 us
    all_to_all x1, blocking collectives, to_all(): lax.all_to_all(jnp.broadcast_to(block[None], (peers,) + block.shape), axe...  13.9 us
    all_to_all x1, waiting for transfers between devices, to_all(): lax.all_to_all(jnp.broadcast_to(block[None], (peers,) + block.shape), axe...  10.5 us
    pallas_call x1, Pallas kernels, attend(): pl.pallas_call(attend_kernel, out_shape=jax.ShapeDtypeStruct((block, widt...  8.96 us
    pallas_call x1, Pallas kernels, make_queries(): pl.pallas_call(queries_kernel, out_shape=(jax.ShapeDtypeStruct((slots, wi...  6.55 us
    pallas_call x1, Pallas kernels, pack_keys(): pl.pallas_call(pack_kernel, out_shape=(jax.ShapeDtypeStruct((rows + TILE,...  5.55 us
  transfers between devices with their start and end apart: 7, of which 4 were waited for; matrix products, arithmetic and copies ran while one was open for 3% of the time, Pallas kernels for 9%

profile of v7, /device:TPU:57, one launch (start us, length us, event | category | flops | bytes accessed | tf_op | source)
XLA Modules:
  0.0 144.8 jit_solution(16387284552501104005)
XLA Ops:
  6.5 2.0 %stage.1 = bf16[200,512]{1,0:T(8,128)(2,1)} custom-call(bf16[512,512]{1,0:T(8,128)(2,1)} %tokens_ref.1, s32[1,192]{1,0:T(1,128)} %bitcast.24, bf16[512]{0:T(512)(128)(2,1)} %gain_ref.1, bf16[512]{0:T(512)(128)(2,1)} %router_ref.1), custom_call_target="tpu_custom_call" | custom-call | tf_op jit(solution)/shard_map/stage/pallas_call | solution.py:45
  9.3 0.9 fusion.4
  10.2 21.0 %all-gather.1 = bf16[576,768]{1,0:T(8,128)(2,1)S(1)} all-gather(bf16[72,768]{1,0:T(8,128)(2,1)S(1)} %fusion.4), channel_id=3, replica_groups=mesh['y'=8,'x'=4,'core'=2,'z'=8] {'y'}, dimensions={0}, use_global_device_ids=true | all-gather | bytes 995328 | tf_op jit(solution)/shard_map/all_gather | solution.py:395
  31.2 0.8 slice.18
  32.1 0.1 broadcast_in_dim.6
  32.2 13.9 %all_to_all.10.mine_ref = bf16[4,8,72,256]{3,2,1,0:T(8,128)(2,1)S(1)} all-to-all(bf16[4,8,72,256]{3,2,1,0:T(8,128)(2,1)S(1)} %broadcast_in_dim.6), channel_id=1, replica_groups=mesh['y'=8,'x'=4,'core'=2,'z'=8] {'x'}, dimensions={0} | all-to-all | bytes 2359296 | tf_op jit(solution)/shard_map/all_to_all | solution.py:370
  46.1 10.0 %collective-permute-start = (bf16[4,8,72,256]{3,2,1,0:T(8,128)(2,1)S(1)}, bf16[4,8,72,256]{3,2,1,0:T(8,128)(2,1)S(1)}, u32[]{:S(2)}, u32[]{:S(2)}) collective-permute-start(bf16[4,8,72,256]{3,2,1,0:T(8,128)(2,1)S(1)} %all_to_all.10.mine_ref), channel_id=1, source_target_pairs={{0,8},{8,0},{1,9},{9,1},{2,10},{10,2},{3,11},{11,3},{4,12},{12,4},... | collective-permute-start | bytes 3538952 | tf_op jit(solution)/shard_map/ppermute | solution.py:376
  56.2 2.4 %collective-permute-done.other_ref = bf16[4,8,72,256]{3,2,1,0:T(8,128)(2,1)S(1)} collective-permute-done((bf16[4,8,72,256]{3,2,1,0:T(8,128)(2,1)S(1)}, bf16[4,8,72,256]{3,2,1,0:T(8,128)(2,1)S(1)}, u32[]{:S(2)}, u32[]{:S(2)}) %collective-permute-start) | collective-permute-done | bytes 1179680 | tf_op jit(solution)/shard_map/ppermute | solution.py:376
  58.6 1.4 copy-done
  60.0 1.6 %make_keys.1 = (bf16[2,192,128]{2,1,0:T(8,128)(2,1)S(1)}, s32[2,4,8,128]{3,2,1,0:T(8,128)S(1)}) custom-call(s32[2]{0:T(128)S(1)} %pad_add_fusion.place_ref, s32[1]{0:T(128)S(6)} %copy.11.count_ref, bf16[8,200,512]{2,1,0:T(8,128)(2,1)S(1)} %bitcast.15, bf16[4,8,72,256]{3,2,1,0:T(8,128)(2,1)S(1)} %all_to_all.10.mine_ref, ...), custom_call_target="tpu_custom_call" | custom-call | tf_op jit(solution)/shard_map/make_keys/pallas_call | solution.py:105
  61.7 0.6 copy-done.2
  62.3 22.5 %all_gather.28 = bf16[8,384,128]{2,1,0:T(8,128)(2,1)S(1)} all-gather(bf16[1,384,128]{2,1,0:T(8,128)(2,1)S(1)} %bitcast.16), channel_id=1, replica_groups=mesh['y'=8,'x'=4,'core'=2,'z'=8] {'y'}, dimensions={0}, use_global_device_ids=true | all-gather | bytes 884736 | tf_op jit(solution)/shard_map/all_gather | solution.py:403
  84.8 0.8 fusion.5
  85.6 1.5 %broadcast_in_dim.16 = bf16[4,8,192,128]{3,2,1,0:T(8,128)(2,1)} broadcast(bf16[8,192,128]{2,1,0:T(8,128)(2,1)S(1)} %get-tuple-element.20), dimensions={1,2,3} | broadcast | bytes 1966080 | tf_op jit(solution)/shard_map/broadcast_in_dim | solution.py:371
  87.2 3.6 %all-to-all-start.1 = ((bf16[4,8,192,128]{3,2,1,0:T(8,128)(2,1)}), bf16[4,8,192,128]{3,2,1,0:T(8,128)(2,1)S(1)}, u32[]{:S(2)}, u32[]{:S(2)}) async-start(bf16[4,8,192,128]{3,2,1,0:T(8,128)(2,1)} %broadcast_in_dim.16), calls=%async_computation.1 | async-start | bytes 3145728 | tf_op jit(solution)/shard_map/all_to_all | solution.py:370
  90.7 2.8 %all-gather.10.cloned.1.call-done = bf16[32,64,512]{2,1,0:T(8,128)(2,1)} async-done(((bf16[8,64,512]{2,1,0:T(8,128)(2,1)}), bf16[32,64,512]{2,1,0:T(8,128)(2,1)}) %all-gather.10.cloned.1.call-update) | async-done | bytes 2097168 | tf_op jit(solution)/shard_map/all_gather | solution.py:398
  93.5 3.2 %collective-permute-start.2 = (bf16[4,8,64,512]{3,2,1,0:T(8,128)(2,1)}, bf16[4,8,64,512]{3,2,1,0:T(8,128)(2,1)}, u32[]{:S(2)}, u32[]{:S(2)}) collective-permute-start(bf16[4,8,64,512]{3,2,1,0:T(8,128)(2,1)} %bitcast.22), channel_id=1, source_target_pairs={{0,8},{8,0},{1,9},{9,1},{2,10},{10,2},{3,11},{11,3},{4,12},{12,4},... | collective-permute-start | bytes 6291464 | tf_op jit(solution)/shard_map/ppermute | solution.py:376
  96.7 10.5 %all-to-all-done.1.mine_hbm = bf16[4,8,192,128]{3,2,1,0:T(8,128)(2,1)S(1)} async-done(((bf16[4,8,192,128]{3,2,1,0:T(8,128)(2,1)}), bf16[4,8,192,128]{3,2,1,0:T(8,128)(2,1)S(1)}, u32[]{:S(2)}, u32[]{:S(2)}) %all-to-all-start.1) | async-done | bytes 1572896 | tf_op jit(solution)/shard_map/all_to_all | solution.py:370
  107.1 7.1 %collective-permute-start.1 = (bf16[4,8,192,128]{3,2,1,0:T(8,128)(2,1)S(1)}, bf16[4,8,192,128]{3,2,1,0:T(8,128)(2,1)S(1)}, u32[]{:S(2)}, u32[]{:S(2)}) collective-permute-start(bf16[4,8,192,128]{3,2,1,0:T(8,128)(2,1)S(1)} %all-to-all-done.1.mine_hbm), channel_id=1, source_target_pairs={{0,8},{8,0},{1,9},{9,1},{2,10},{10,2},{3,11},{11,3},{4,12},{12,4},... | collective-permute-start | bytes 4718600 | tf_op jit(solution)/shard_map/ppermute | solution.py:376
  114.3 6.6 %make_queries.1 = (bf16[192,512]{1,0:T(8,128)(2,1)}, f32[192,128]{1,0:T(8,128)}) custom-call(s32[2]{0:T(128)} %copy-done.3, bf16[8,200,512]{2,1,0:T(8,128)(2,1)} %bitcast.14, bf16[4,8,64,512]{3,2,1,0:T(8,128)(2,1)} %bitcast.23, bf16[4,8,64,512]{3,2,1,0:T(8,128)(2,1)} %collective-permute-done.2.other_hbm, f32[1,128]{1,0:T(1,128)} %bitcast.26), custom_call_target="tpu_custom_call" | custom-call | tf_op jit(solution)/shard_map/make_queries/pallas_call | solution.py:157
  120.9 1.1 copy-done.6
  122.0 5.5 %pack_keys.1 = (bf16[6144,128]{1,0:T(8,128)(2,1)}, bf16[6144,128]{1,0:T(8,128)(2,1)}, s32[3,32]{1,0:T(4,128)}) custom-call(s32[2]{0:T(128)} %copy-done.3, s32[2,4,8,128]{3,2,1,0:T(8,128)} %copy-done.2, s32[1]{0:T(128)S(6)} %copy.11.count_ref, bf16[4,8,192,128]{3,2,1,0:T(8,128)(2,1)} %copy-done.5, bf16[4,8,192,128]{3,2,1,0:T(8,128)(2,1)} %copy-done.6, ...), custom_call_target="tpu_custom_call" | custom-call | tf_op jit(solution)/shard_map/pack_keys/pallas_call | solution.py:227
  127.5 1.7 %all-gather.12.cloned.1.call-done = bf16[64,1,192,128]{3,2,1,0:T(8,128)(2,1)} async-done(((bf16[8,1,192,128]{3,2,1,0:T(8,128)(2,1)}), bf16[64,1,192,128]{3,2,1,0:T(8,128)(2,1)}) %all-gather.12.cloned.1.call-update) | async-done | bytes 3145744 | tf_op jit(solution)/shard_map/all_gather | solution.py:405
  129.2 9.0 %attend.1 = bf16[512,512]{1,0:T(8,128)(2,1)} custom-call(s32[3,32]{1,0:T(4,128)} %get-tuple-element.15.table_ref, bf16[192,512]{1,0:T(8,128)(2,1)} %get-tuple-element.14._.q_ref, bf16[2,192,128]{2,1,0:T(8,128)(2,1)} %copy-done.1, s32[1,192]{1,0:T(1,128)} %bitcast.25, f32[192,128]{1,0:T(8,128)} %get-tuple-element.16.gate_ref, ...), custom_call_target="tpu_custom_call" | custom-call | tf_op jit(solution)/shard_map/attend/pallas_call | solution.py:351
  (22 shorter events, 0.3 us)
Async XLA Ops:
  6.5 52.0 %all-gather.8.cloned.1.call-start = ((), (), s32[]{:S(2)}) async-start(), calls=%async_computation.2 | async-start | bytes 1843200 | tf_op jit(solution)/shard_map/all_gather | solution.py:393
  8.6 84.9 %all-gather.10.cloned.1.call-start = ((), (), s32[]{:S(2)}) async-start(), calls=%async_computation.3 | async-start | bytes 2621440 | tf_op jit(solution)/shard_map/all_gather | solution.py:398
  32.0 97.2 %all-gather.12.cloned.1.call-start = ((), (), s32[]{:S(2)}) async-start(), calls=%async_computation.4 | async-start | bytes 3538944 | tf_op jit(solution)/shard_map/all_gather | solution.py:405
  32.1 26.5 %copy-start.4 = (f32[128]{0:T(128)S(1)}, f32[128]{0:T(128)}, u32[]{:S(2)}) copy-start(f32[128]{0:T(128)} %param.17) | copy-start | bytes 1540
  46.1 12.5 %collective-permute-start = (bf16[4,8,72,256]{3,2,1,0:T(8,128)(2,1)S(1)}, bf16[4,8,72,256]{3,2,1,0:T(8,128)(2,1)S(1)}, u32[]{:S(2)}, u32[]{:S(2)}) collective-permute-start(bf16[4,8,72,256]{3,2,1,0:T(8,128)(2,1)S(1)} %all_to_all.10.mine_ref), channel_id=1, source_target_pairs={{0,8},{8,0},{1,9},{9,1},{2,10},{10,2},{3,11},{11,3},{4,12},{12,4},... | collective-permute-start | bytes 3538952 | tf_op jit(solution)/shard_map/ppermute | solution.py:376
  56.2 5.5 %copy-start.3 = (s32[2]{0:T(128)}, s32[2]{0:T(128)S(1)}, u32[]{:S(2)}) copy-start(s32[2]{0:T(128)S(1)} %pad_add_fusion.place_ref) | copy-start | bytes 28
  58.6 1.4 copy-start
  61.7 0.6 copy-start.2
  62.3 24.9 %copy-start.1 = (bf16[2,192,128]{2,1,0:T(8,128)(2,1)}, bf16[2,192,128]{2,1,0:T(8,128)(2,1)S(1)}, u32[]{:S(2)}) copy-start(bf16[2,192,128]{2,1,0:T(8,128)(2,1)S(1)} %get-tuple-element.13.own_ref) | copy-start | bytes 294916
  87.2 20.0 %all-to-all-start.1 = ((bf16[4,8,192,128]{3,2,1,0:T(8,128)(2,1)}), bf16[4,8,192,128]{3,2,1,0:T(8,128)(2,1)S(1)}, u32[]{:S(2)}, u32[]{:S(2)}) async-start(bf16[4,8,192,128]{3,2,1,0:T(8,128)(2,1)} %broadcast_in_dim.16), calls=%async_computation.1 | async-start | bytes 3145728 | tf_op jit(solution)/shard_map/all_to_all | solution.py:370
  93.5 20.8 %collective-permute-start.2 = (bf16[4,8,64,512]{3,2,1,0:T(8,128)(2,1)}, bf16[4,8,64,512]{3,2,1,0:T(8,128)(2,1)}, u32[]{:S(2)}, u32[]{:S(2)}) collective-permute-start(bf16[4,8,64,512]{3,2,1,0:T(8,128)(2,1)} %bitcast.22), channel_id=1, source_target_pairs={{0,8},{8,0},{1,9},{9,1},{2,10},{10,2},{3,11},{11,3},{4,12},{12,4},... | collective-permute-start | bytes 6291464 | tf_op jit(solution)/shard_map/ppermute | solution.py:376
  107.1 13.7 %copy-start.5 = (bf16[4,8,192,128]{3,2,1,0:T(8,128)(2,1)}, bf16[4,8,192,128]{3,2,1,0:T(8,128)(2,1)S(1)}, u32[]{:S(2)}) copy-start(bf16[4,8,192,128]{3,2,1,0:T(8,128)(2,1)S(1)} %all-to-all-done.1.mine_hbm) | copy-start | bytes 4718596
  107.1 13.7 %collective-permute-start.1 = (bf16[4,8,192,128]{3,2,1,0:T(8,128)(2,1)S(1)}, bf16[4,8,192,128]{3,2,1,0:T(8,128)(2,1)S(1)}, u32[]{:S(2)}, u32[]{:S(2)}) collective-permute-start(bf16[4,8,192,128]{3,2,1,0:T(8,128)(2,1)S(1)} %all-to-all-done.1.mine_hbm), channel_id=1, source_target_pairs={{0,8},{8,0},{1,9},{9,1},{2,10},{10,2},{3,11},{11,3},{4,12},{12,4},... | collective-permute-start | bytes 4718600 | tf_op jit(solution)/shard_map/ppermute | solution.py:376
  120.9 1.1 copy-start.6
Sparse Core Ops, SparseCore 0:
  9.4 43.7 all-gather.7
  55.3 38.1 all-gather.9
  95.6 33.5 all-gather.11
